TPU v7x, 256 devices: a whole 4x4x8 slice. The times are simulated.
256 devices in a mesh: section: 16 (over x_lo, z), tp: 4 (over x_hi, core), dp: 4 (over y).
Axes of the slice: x: 4 (x_hi: 2, x_lo: 2; x = x_hi * 2 + x_lo), y: 4, z: 8, core: 2. Of those that a mesh axis runs over, the one named last changes fastest.
Arguments:
- memory: bfloat16 [512, 4, 4096], P(None, 'dp', ('section', 'tp')), may hold values from -6 to 6
- queries: bfloat16 [16, 4, 512, 2048], P('section', 'dp', None, 'tp'), may hold values from -6 to 6
- out_grad: bfloat16 [16, 4, 512, 2048], P('section', 'dp', None, 'tp'), may hold values from -6 to 6
- memory_weight: bfloat16 [16, 4096, 2, 2048], P('section', None, None, 'tp'), may hold values from -0.09375 to 0.09375
- lengths: int32 [4], P('dp'), may hold values from 256 to 512
Outputs:
- memory_grad: bfloat16 [512, 4, 4096], P(None, 'dp', ('section', 'tp'))
- query_grad: bfloat16 [16, 4, 512, 2048], P('section', 'dp', None, 'tp')
- weight_grad: bfloat16 [16, 4096, 2, 2048], P('section', 'dp', None, 'tp')
Inputs may be any that keep to these rules, and one draw needn't show every extreme that they name: `lengths`: memory positions at or beyond a sequence's length are padding.
All inputs are finite; a program needn't handle non-finite values.
Results may differ from a plain program's by a relative error of at most 0.025.
Values may be sent and summed in bfloat16 or wider, within the bound.
No kernel may reach another device: no remote copies, remote signals or barrier semaphores. Data moves between devices by JAX's collectives and lax.ppermute only.
A program may use at most 128 MiB of HBM per device.

v0:
```python
import math

import jax
import jax.numpy as jnp
from jax import lax
from jax.sharding import PartitionSpec as P

HD = 64


def pair_grads(query_pair, key_pair, value_pair, grad_pair, key_mask, factor):
    scores = (
        jnp.einsum("thc,shc->hts", query_pair, key_pair, preferred_element_type=jnp.float32)
        * factor
    )
    weights = jnp.exp(scores) * key_mask[None, None, :]
    attention = weights / jnp.sum(weights, axis=2, keepdims=True)
    attention_low = attention.astype(jnp.bfloat16)
    outputs = jnp.einsum(
        "hts,shc->thc", attention_low, value_pair, preferred_element_type=jnp.float32
    )
    prob_grad = jnp.einsum(
        "thc,shc->hts", grad_pair, value_pair, preferred_element_type=jnp.float32
    )
    row_dot = jnp.sum(grad_pair.astype(jnp.float32) * outputs, axis=2)
    score_grad = (attention * (prob_grad - jnp.transpose(row_dot)[:, :, None])).astype(jnp.bfloat16)
    query_out = (
        jnp.einsum("hts,shc->thc", score_grad, key_pair, preferred_element_type=jnp.float32)
        * factor
    ).astype(jnp.bfloat16)
    key_out = (
        jnp.einsum("hts,thc->shc", score_grad, query_pair, preferred_element_type=jnp.float32)
        * factor
    ).astype(jnp.bfloat16)
    value_out = jnp.einsum(
        "hts,thc->shc", attention_low, grad_pair, preferred_element_type=jnp.float32
    ).astype(jnp.bfloat16)
    return (query_out, key_out, value_out)


def attend(query_rows, key_rows, value_rows, grad_rows, key_mask):
    pairs = query_rows.shape[1] // (2 * HD)
    factor = 1.0 / math.sqrt(HD)

    def split(block):
        return block.reshape(block.shape[0], pairs, 2, HD).transpose(1, 0, 2, 3)

    def merge_back(block):
        return block.transpose(1, 0, 2, 3).reshape(block.shape[1], pairs * 2 * HD)

    results = lax.map(
        lambda items: pair_grads(items[0], items[1], items[2], items[3], key_mask, factor),
        (split(query_rows), split(key_rows), split(value_rows), split(grad_rows)),
    )
    return (merge_back(results[0]), merge_back(results[1]), merge_back(results[2]))


def body(memory, queries, out_grad, memory_weight, lengths):
    pieces = lax.all_gather(memory, "tp", axis=2, tiled=True)
    gathered = lax.all_gather(pieces, "section", axis=2, tiled=True)
    weight_layer = memory_weight[0]
    projected = jnp.einsum(
        "snd,dkc->ksnc", gathered, weight_layer, preferred_element_type=jnp.float32
    ).astype(jnp.bfloat16)
    positions = jnp.arange(gathered.shape[0], dtype=jnp.int32)
    key_masks = (positions[None, :] < lengths[:, None]).astype(jnp.float32)
    query_out, key_out, value_out = attend(
        queries[0, 0], projected[0, :, 0], projected[1, :, 0], out_grad[0, 0], key_masks[0]
    )
    query_list = [query_out]
    key_list = [key_out]
    value_list = [value_out]
    query_grad = jnp.stack(query_list)[None]
    grads = jnp.stack([jnp.stack(key_list, 1), jnp.stack(value_list, 1)])
    portion = weight_layer
    row_block = lax.psum_scatter(
        jnp.einsum("ksnc,dkc->dsn", grads, portion, preferred_element_type=jnp.float32).astype(
            jnp.bfloat16
        ),
        "section",
        scatter_dimension=0,
        tiled=True,
    )
    feature_block = lax.psum_scatter(row_block, "tp", scatter_dimension=0, tiled=True).astype(
        jnp.float32
    )
    memory_grad = jnp.transpose(feature_block, (1, 2, 0))
    portion = gathered
    weight_grad = lax.psum_scatter(
        jnp.einsum("snd,ksnc->dkc", portion, grads, preferred_element_type=jnp.float32).astype(
            jnp.bfloat16
        ),
        "dp",
        scatter_dimension=0,
        tiled=True,
    )[None]
    return (memory_grad.astype(jnp.bfloat16), query_grad, weight_grad)


def solution(mesh):
    return jax.shard_map(
        body,
        mesh=mesh,
        in_specs=(
            P(None, "dp", ("section", "tp")),
            P("section", "dp", None, "tp"),
            P("section", "dp", None, "tp"),
            P("section", None, None, "tp"),
            P("dp"),
        ),
        out_specs=(
            P(None, "dp", ("section", "tp")),
            P("section", "dp", None, "tp"),
            P("section", "dp", None, "tp"),
        ),
        check_vma=False,
    )
```

profile of v0, /device:TPU:33, one launch (start us, length us, event | category | flops | bytes accessed | tf_op | source)
XLA Modules:
  0.0 353.3 jit_solution(10041624648096045545)
XLA Ops:
  7.2 8.1 %all_gather.6 = bf16[512,1,256]{0,2,1:T(8,128)(2,1)S(1)} all-gather(bf16[512,1,64]{0,2,1:T(8,128)(2,1)} %param.7), channel_id=1, replica_groups=mesh['section'=16,'tp'=4,'dp'=4] {'tp'}, dimensions={2}, use_global_device_ids=true | all-gather | bytes 327680 | tf_op jit(solution)/shard_map/all_gather | solution.py:59
  15.4 0.8 copy.45
  16.3 1.3 copy.47
  17.8 79.1 %all-gather.2.cloned.1.call-done = bf16[512,1,4096]{2,0,1:T(8,128)(2,1)} async-done(((bf16[512,1,256]{2,0,1:T(8,128)(2,1)}), bf16[512,1,4096]{2,0,1:T(8,128)(2,1)}) %all-gather.2.cloned.1.call-update) | async-done | bytes 4194320 | tf_op jit(solution)/shard_map/all_gather | solution.py:60
  96.9 9.1 %fusion.57 = bf16[2,512,1,512]{1,3,0,2:T(8,128)(2,1)S(1)} fusion(bf16[512,1,4096]{2,0,1:T(8,128)(2,1)} %all-gather.2.cloned.1.call-done, bf16[4096,2,512]{2,1,0:T(2,128)(2,1)} %bitcast.162), kind=kOutput, calls=%fused_computation.55 | convolution fusion | flops 4295491584 | bytes 13631488 | tf_op jit(solution)/shard_map/snd,dkc->ksnc/dot_general | solution.py:62
  106.0 0.9 fusion.64
  106.8 16.1 %while.15 = (s32[]{:T(128)}, bf16[4,512,2,64]{1,3,2,0:T(8,128)(2,1)S(1)}, bf16[4,512,2,64]{1,3,2,0:T(8,128)(2,1)S(1)}, bf16[4,512,2,64]{1,3,2,0:T(8,128)(2,1)S(1...) while((s32[]{:T(128)}, ...), condition=%wide.region_3.4_spmd.clone, body=%wide.region_0.3_spmd.clone.sunk | while | flops 412089344 | bytes 15245453 | solution.py:51
  109.3 0.8 multiply_convert_fusion.2
  110.9 0.7 compare_convert_fusion.2
  113.4 0.8 multiply_convert_fusion.2
  114.9 0.7 compare_convert_fusion.2
  117.4 0.8 multiply_convert_fusion.2
  121.5 0.8 multiply_convert_fusion.2
  123.4 9.5 %fusion.47 = bf16[4096,512,1]{0,1,2:T(8,128)(2,1)} fusion(bf16[4096,2,512]{2,1,0:T(2,128)(2,1)} %bitcast.163, bf16[1,512,1,512]{3,1,0,2:T(8,128)(2,1)S(1)} %copy.50, bf16[1,512,1,512]{3,1,0,2:T(8,128)(2,1)S(1)} %copy.49), kind=kOutput, calls=%fused_computation.51 | convolution fusion | flops 4297588736 | bytes 13631488 | tf_op jit(solution)/shard_map/ksnc,dkc->dsn/dot_general | solution.py:77
  133.0 78.3 %reduce-scatter.6.cloned.1.call-done = bf16[256,512,1]{0,1,2:T(8,128)(2,1)} async-done(((bf16[4096,512,1]{0,1,2:T(8,128)(2,1)}), bf16[256,512,1]{0,1,2:T(8,128)(2,1)}) %reduce-scatter.6.cloned.1.call-update) | async-done | bytes 262160 | tf_op jit(solution)/shard_map/reduce_scatter | solution.py:76
  211.2 1.3 copy.62
  212.6 0.7 copy.78
  213.5 9.0 %convert_bitcast_fusion = bf16[4096,2,512]{0,2,1:T(8,128)(2,1)} fusion(bf16[512,1,4096]{2,0,1:T(8,128)(2,1)} %all-gather.2.cloned.1.call-done, bf16[1,512,1,512]{3,1,0,2:T(8,128)(2,1)S(1)} %copy.50, bf16[1,512,1,512]{3,1,0,2:T(8,128)(2,1)S(1)} %copy.49), kind=kOutput, calls=%fused_computation.46 | convolution fusion | flops 4299685888 | bytes 13631488 | tf_op jit(solution)/shard_map/snd,ksnc->dkc/dot_general | solution.py:90
  222.5 1.0 copy.54
  223.5 31.8 %reduce-scatter.10.cloned.1.call-done = bf16[64,512]{1,0:T(8,128)(2,1)} async-done(((bf16[256,512]{1,0:T(8,128)(2,1)}), bf16[64,512]{1,0:T(8,128)(2,1)}) %reduce-scatter.10.cloned.1.call-update) | async-done | bytes 65552
  255.3 0.9 reshape_bitcast_fusion
  256.4 0.7 copy.53
  257.1 83.6 %reduce-scatter.8.cloned.1.call-done = bf16[1024,2,512]{0,2,1:T(8,128)(2,1)} async-done(((bf16[4096,2,512]{0,2,1:T(8,128)(2,1)}), bf16[1024,2,512]{0,2,1:T(8,128)(2,1)}) %reduce-scatter.8.cloned.1.call-update) | async-done | bytes 2097168 | tf_op jit(solution)/shard_map/reduce_scatter | solution.py:89
  340.7 6.2 %copy.55 = bf16[1,1024,2,512]{3,2,1,0:T(2,128)(2,1)} copy(bf16[1,1024,2,512]{1,3,2,0:T(8,128)(2,1)} %bitcast.150) | data formatting | bytes 4194304
  (47 shorter events, 12.7 us)
Async XLA Ops:
  7.2 10.4 %copy-start = (bf16[1,1,512,512]{3,2,1,0:T(8,128)(2,1)S(1)}, bf16[1,1,512,512]{3,2,1,0:T(8,128)(2,1)}, u32[]{:S(2)}) copy-start(bf16[1,1,512,512]{3,2,1,0:T(8,128)(2,1)} %param.9) | copy-start | bytes 1572868
  7.2 89.7 %all-gather.2.cloned.1.call-start = ((), (), s32[]{:S(2)}) async-start(), calls=%async_computation.3 | async-start | bytes 4456448 | tf_op jit(solution)/shard_map/all_gather | solution.py:60
  16.2 195.0 %reduce-scatter.6.cloned.1.call-start = ((), (), s32[]{:S(2)}) async-start(), calls=%async_computation.4 | async-start | bytes 4456448 | tf_op jit(solution)/shard_map/reduce_scatter | solution.py:76
  106.8 1.3 copy-start.1
  110.9 1.3 copy-start.1
  114.9 1.3 copy-start.1
  118.9 1.3 copy-start.1
  132.9 122.4 %reduce-scatter.10.cloned.1.call-start = ((), (), s32[]{:S(2)}) async-start(), calls=%async_computation.6 | async-start | bytes 327680
  213.3 127.3 %reduce-scatter.8.cloned.1.call-start = ((), (), s32[]{:S(2)}) async-start(), calls=%async_computation.5 | async-start | bytes 10485760 | tf_op jit(solution)/shard_map/reduce_scatter | solution.py:89
Sparse Core Ops, SparseCore 0:
  16.4 80.4 all-gather.1
  133.0 78.1 reduce-scatter.5
  214.5 40.7 reduce-scatter.9
  257.9 82.6 reduce-scatter.7
where the time goes:
time: 355 us; the launch traced here: 353 us
  waiting for transfers between devices  273 us (77%)
  matrix products  40.6 us (11%)
  local copies, waits for them, and re-layouts  14.6 us (4%)
  between operations  13.9 us (4%)
  blocking collectives  8.15 us (2%)
    reduce_scatter x1, waiting for transfers between devices, body(): lax.psum_scatter(jnp.einsum('snd,ksnc->dkc', portion, grads, preferred_el...  83.6 us
    all_gather x1, waiting for transfers between devices, body(): gathered = lax.all_gather(pieces, 'section', axis=2, tiled=True)  79.1 us
    reduce_scatter x1, waiting for transfers between devices, body(): lax.psum_scatter(jnp.einsum('ksnc,dkc->dsn', grads, portion, preferred_el...  78.3 us
    unnamed x5, waiting for transfers between devices  31.8 us
    unnamed x11, local copies, waits for them, and re-layouts  12.5 us
    dot_general x1, matrix products, body(): jnp.einsum('ksnc,dkc->dsn', grads, portion, preferred_element_type=jnp.fl...  9.47 us
    dot_general x1, matrix products, body(): jnp.einsum('snd,dkc->ksnc', gathered, weight_layer, preferred_element_typ...  9.11 us
    dot_general x1, matrix products, body(): jnp.einsum('snd,ksnc->dkc', portion, grads, preferred_element_type=jnp.fl...  8.96 us
  transfers between devices with their start and end apart: 4, of which 4 were waited for; matrix products, arithmetic and copies ran while one was open for 4% of the time, Pallas kernels for 0%

commit v1 on v0

v1 whole, which is shorter than its diff:
```python
import functools

import jax
import jax.numpy as jnp
from jax import lax
from jax.experimental import pallas as pl
from jax.experimental.pallas import tpu as pltpu
from jax.sharding import PartitionSpec as P

PLANE = ("section", "tp")
HD = 64
HEADS = 8
F32 = jnp.float32
BF16 = jnp.bfloat16
VMEM = 28 << 20


def index_of(x, z, core):
    x, z = x % 4, z % 8
    return ((x % 2) * 8 + z) * 4 + (x // 2) * 2 + core


def place(i):
    section, tp = divmod(i, 4)
    return (tp // 2) * 2 + section // 8, section % 8, tp % 2


FAR = [
    [index_of(2 * a + px, 2 * b + pz, core) for a in range(2) for b in range(4)]
    for px in range(2)
    for pz in range(2)
    for core in range(2)
]


def beside(value, core):
    return ((value - core) ^ 1) + core


def moves(dx, dz, dcore):
    pairs = []
    for i in range(64):
        x, z, core = place(i)
        pairs.append((i, index_of(beside(x, core) if dx else x, beside(z, core) if dz else z, core ^ dcore)))
    return pairs


NEAR = {(dx, dz): moves(dx, dz, 0) for dx, dz in ((0, 1), (1, 0), (1, 1))}
SWAP = moves(0, 0, 1)


def spread(block, groups):
    count = len(groups[0])
    copies = jnp.broadcast_to(block[None], (count,) + block.shape)
    return lax.all_to_all(copies, PLANE, 0, 0, axis_index_groups=groups)


def collect(blocks, groups):
    parts = lax.all_to_all(blocks, PLANE, 0, 0, axis_index_groups=groups)
    return jnp.sum(parts.astype(F32), axis=0).astype(BF16)


def along_dp(block, step):
    return lax.ppermute(block, "dp", [(d, (d + step) % 4) for d in range(4)])


def swap(block):
    return lax.ppermute(block, PLANE, SWAP)


def near(block, dx, dz):
    return lax.ppermute(block, PLANE, NEAR[dx, dz])


def dot(a, b, dims):
    return lax.dot_general(a, b, (dims, ((), ())), preferred_element_type=F32)


NN = ((1,), (0,))
NT = ((1,), (1,))
TN = ((0,), (0,))


def split_kernel(at_ref, weight_ref, out_ref):
    weight = weight_ref[...].reshape(4, 2, 64, 2, 512)
    weight = jnp.swapaxes(weight, 0, 1).reshape(512, 2, 512)
    out_ref[...] = jnp.swapaxes(weight, 0, 1).reshape(1, 1, 2, 512, 512)


def split_weights(at, weight):
    view = weight.reshape(2, 4, 2, 2, 2, 64, 2, 512)
    return pl.pallas_call(
        split_kernel,
        grid_spec=pltpu.PrefetchScalarGridSpec(
            num_scalar_prefetch=1,
            grid=(4, 2),
            in_specs=[
                pl.BlockSpec(
                    (1, 4, 1, 2, 1, 64, 2, 512),
                    lambda r, h, at: (at[0] ^ (r // 2), 0, at[1] ^ (r % 2), 0, at[2] ^ h, 0, 0, 0),
                )
            ],
            out_specs=pl.BlockSpec((1, 1, 2, 512, 512), lambda r, h, at: (r, h, 0, 0, 0)),
        ),
        out_shape=jax.ShapeDtypeStruct((4, 2, 2, 512, 512), BF16),
        compiler_params=pltpu.CompilerParams(vmem_limit_bytes=VMEM),
        cost_estimate=pl.CostEstimate(flops=0, bytes_accessed=32 << 20, transcendentals=0),
        name="split_weights",
    )(at, view)


def project_kernel(first, count, *refs):
    sums_ref = None if first else refs[0]
    rows_refs = refs[0 if first else 1 :][: 2 * count]
    weight_ref, out_ref, turned = refs[-3:]

    @pl.when(pl.program_id(0) == 0)
    def _():
        for i, rows in enumerate(rows_refs):
            turned[:, i * 512 : (i + 1) * 512] = rows[...].T

    weight = weight_ref[...].reshape(count * 1024, 256)
    total = dot(turned[...], weight, NN)
    if not first:
        total += sums_ref[0]
    out_ref[0] = total.astype(out_ref.dtype)


def project(sums, rows, split, piece, last):
    first, count = sums is None, len(rows) // 2
    columns = pl.BlockSpec((1, 512, 256), lambda i: (i // 2, 0, i % 2))
    return pl.pallas_call(
        functools.partial(project_kernel, first, count),
        grid=(4,),
        in_specs=([] if first else [columns])
        + [pl.BlockSpec((512, 512), lambda i: (0, 0))] * (2 * count)
        + [pl.BlockSpec((count, 2, 1, 512, 256), lambda i: (piece // count, 0, i // 2, 0, i % 2))],
        out_specs=columns,
        scratch_shapes=[pltpu.VMEM((512, 1024 * count), BF16)],
        out_shape=jax.ShapeDtypeStruct((2, 512, 512), BF16 if last else F32),
        compiler_params=pltpu.CompilerParams(vmem_limit_bytes=VMEM),
        cost_estimate=pl.CostEstimate(
            flops=2 * 512 * 1024 * 1024 * count, bytes_accessed=(3 * count + 4) << 20, transcendentals=0
        ),
        name="project",
    )(*([] if first else [sums]), *rows, split)


def attend_kernel(length_ref, query_ref, grad_ref, pair_ref, query_out, grads_out, turned_out):
    position = lax.broadcasted_iota(jnp.int32, (512, 1), 0)
    mask = jnp.where(position < length_ref[0], 1.0, 0.0)
    queries, keys, values = [], [], []
    for head in range(2):
        cols = slice(head * HD, (head + 1) * HD)
        query = query_ref[:, cols] * BF16(0.125)
        grad = grad_ref[:, cols]
        key = pair_ref[0, :, cols]
        value = pair_ref[1, :, cols]
        weights = jnp.exp(dot(key, query, NT)) * mask
        attention = weights * (1.0 / jnp.sum(weights, axis=0, keepdims=True))
        low = attention.astype(BF16)
        prob = dot(value, grad, NT)
        row_dot = jnp.sum(low.astype(F32) * prob, axis=0, keepdims=True)
        score = (attention * (prob - row_dot)).astype(BF16)
        queries.append((dot(score, key, TN) * 0.125).astype(BF16))
        keys.append(dot(score, query, NN).astype(BF16))
        values.append(dot(low, grad, NN).astype(BF16))
    query_out[...] = jnp.concatenate(queries, axis=1)
    key_grad = jnp.concatenate(keys, axis=1)
    value_grad = jnp.concatenate(values, axis=1)
    grads_out[0] = key_grad
    grads_out[1] = value_grad
    turned_out[0] = key_grad.T
    turned_out[1] = value_grad.T


def attend(lengths, queries, out_grad, pair):
    block = pl.BlockSpec((512, 128), lambda i, c: (0, i))
    both = pl.BlockSpec((2, 512, 128), lambda i, c: (0, 0, i))
    return pl.pallas_call(
        attend_kernel,
        grid_spec=pltpu.PrefetchScalarGridSpec(
            num_scalar_prefetch=1,
            grid=(4,),
            in_specs=[block, block, both],
            out_specs=[block, both, pl.BlockSpec((2, 128, 512), lambda i, c: (0, i, 0))],
        ),
        out_shape=[
            jax.ShapeDtypeStruct((512, 512), BF16),
            jax.ShapeDtypeStruct((2, 512, 512), BF16),
            jax.ShapeDtypeStruct((2, 512, 512), BF16),
        ],
        compiler_params=pltpu.CompilerParams(vmem_limit_bytes=VMEM),
        cost_estimate=pl.CostEstimate(flops=8 * 6 * 2 * 512 * 512 * 64 * 4, bytes_accessed=5 << 20, transcendentals=8 << 18),
        name="attend",
    )(lengths, queries, out_grad, pair)


def memory_kernel(weight_ref, turned_ref, *refs):
    total = dot(weight_ref[0, 0, 0], turned_ref[0], NN) + dot(weight_ref[0, 0, 1], turned_ref[1], NN)
    if len(refs) == 2:
        total = total + refs[0][0].astype(F32)
    refs[-1][0] = total.astype(BF16)


def memory_pieces(split, turned, upper, half, sent=None):
    rows = pl.BlockSpec((1, 512, 512), lambda i: (i, 0, 0))
    return pl.pallas_call(
        memory_kernel,
        grid=(2,),
        in_specs=[
            pl.BlockSpec((1, 1, 2, 512, 512), lambda i: (upper - i, half, 0, 0, 0)),
            pl.BlockSpec((2, 512, 512), lambda i: (0, 0, 0)),
        ]
        + ([] if sent is None else [rows]),
        out_specs=rows,
        out_shape=jax.ShapeDtypeStruct((2, 512, 512), BF16),
        compiler_params=pltpu.CompilerParams(vmem_limit_bytes=VMEM),
        cost_estimate=pl.CostEstimate(flops=512 * 2048 * 1024, bytes_accessed=6 << 20, transcendentals=0),
        name="memory_pieces",
    )(split, turned, *([] if sent is None else [sent]))


def weight_kernel(at_ref, mine, other, left, right, across, swapped, g0, g1, g2, gk, gv, out_ref):
    own = pl.program_id(0) < 2
    rows = [jnp.where(own, mine[0], other[0])]
    for i, block in enumerate((left, right, across)):
        rows.append(jnp.where(own, block[0], swapped[i, 0]))
    keys = (g0[0], g1[0], g2[0], gk[...])
    values = (g0[1], g1[1], g2[1], gv[...])
    for_key = sum(dot(a, b, NN) for a, b in zip(rows, keys))
    for_value = sum(dot(a, b, NN) for a, b in zip(rows, values))
    both = jnp.stack([for_key.astype(BF16), for_value.astype(BF16)], axis=0)
    both = jnp.swapaxes(both, 0, 1).reshape(2, 2, 64, 2, 512)
    out_ref[...] = jnp.swapaxes(both, 0, 1).reshape(2, 1, 2, 1, 64, 2, 512)


def weight_rows(at, mine, other, left, right, across, swapped, g0, g1, g2, gk, gv):
    def whole(shape):
        return pl.BlockSpec(shape, lambda i, at: (0,) * len(shape))

    half = pl.BlockSpec((1, 256, 512), lambda i, at: (i % 2, 0, 0))
    out = pl.pallas_call(
        weight_kernel,
        grid_spec=pltpu.PrefetchScalarGridSpec(
            num_scalar_prefetch=1,
            grid=(4,),
            in_specs=[half] * 5
            + [
                pl.BlockSpec((3, 1, 256, 512), lambda i, at: (0, i % 2, 0, 0)),
                whole((2, 512, 512)),
                whole((2, 512, 512)),
                whole((2, 512, 512)),
                whole((512, 512)),
                whole((512, 512)),
            ],
            out_specs=pl.BlockSpec(
                (2, 1, 2, 1, 64, 2, 512), lambda i, at: (0, at[1] ^ (i % 2), 0, at[2] ^ (i // 2), 0, 0, 0)
            ),
        ),
        out_shape=jax.ShapeDtypeStruct((2, 2, 2, 2, 64, 2, 512), BF16),
        compiler_params=pltpu.CompilerParams(vmem_limit_bytes=VMEM),
        cost_estimate=pl.CostEstimate(flops=2 * 2048 * 1024 * 1024, bytes_accessed=12 << 20, transcendentals=0),
        name="weight_rows",
    )(at, mine, other, left, right, across, swapped, g0, g1, g2, gk, gv)
    return out.reshape(1, 1024, 2, 512)


def body(memory, queries, out_grad, memory_weight, lengths):
    section, tp = lax.axis_index("section"), lax.axis_index("tp")
    dp = lax.axis_index("dp").astype(jnp.int32)
    at = jnp.stack([section // 8, section % 2, tp % 2]).astype(jnp.int32)

    split = split_weights(at, memory_weight[0])
    own = spread(memory[:, 0, :].T, FAR).reshape(512, 512)
    own, split = lax.optimization_barrier((own, split))
    mine = [own, near(own, 0, 1), near(own, 1, 0), near(own, 1, 1)]
    other = [swap(piece) for piece in mine]
    sums = project(None, [mine[0], other[0]], split, 0, False)
    sums = project(sums, [mine[1], other[1]], split, 1, False)
    pair = project(sums, [mine[2], other[2], mine[3], other[3]], split, 2, True)

    def block_of(pieces, d):
        moved = (d // 2) ^ at[0]
        rows = []
        for dz in range(2):
            piece = jnp.where(moved == 0, pieces[dz], pieces[2 + dz]).reshape(2, 2, 128, 512)
            rows.append(lax.dynamic_slice(piece, (0, d % 2, 0, 0), (2, 1, 128, 512)).reshape(256, 512))
        return jnp.stack(rows)

    arrived = [along_dp(block_of(mine, (dp + step) % 4), step) for step in (1, 3, 2)]

    query_grad, grads, turned = attend(lengths, queries[0, 0], out_grad[0, 0], pair)
    grads, turned, arrived = lax.optimization_barrier((grads, turned, arrived))

    from_left = along_dp(grads, 1)
    from_right = along_dp(grads, 3)
    across_key = along_dp(from_left[0], 1)
    across_value = along_dp(from_right[1], 3)

    sent_far = swap(memory_pieces(split, turned, 3, 1))
    sent_near = swap(memory_pieces(split, turned, 1, 1))
    far = memory_pieces(split, turned, 3, 0, sent_far)
    from_diagonal, from_x = near(far[0], 1, 1), near(far[1], 1, 0)
    close = memory_pieces(split, turned, 1, 0, sent_near)
    from_z = near(close[0], 0, 1)
    terms = (close[1], from_z, from_x, from_diagonal)
    quarter = sum(term.astype(F32) for term in terms).astype(BF16)
    memory_grad = collect(quarter.reshape(8, 64, 512), FAR).T[:, None, :]

    swapped = swap(jnp.stack(arrived))
    weight_grad = weight_rows(
        at,
        block_of(mine, dp),
        block_of(other, dp),
        *arrived,
        swapped,
        grads,
        from_left,
        from_right,
        across_key,
        across_value,
    )
    return memory_grad, query_grad[None, None], weight_grad


def solution(mesh):
    return jax.shard_map(
        body,
        mesh=mesh,
        in_specs=(
            P(None, "dp", ("section", "tp")),
            P("section", "dp", None, "tp"),
            P("section", "dp", None, "tp"),
            P("section", None, None, "tp"),
            P("dp"),
        ),
        out_specs=(
            P(None, "dp", ("section", "tp")),
            P("section", "dp", None, "tp"),
            P("section", "dp", None, "tp"),
        ),
        check_vma=False,
    )
```

time: 355 us -> 147 us (0.41)
  waiting for transfers between devices: 273 us -> 39.1 us
  Pallas kernels: 0 us -> 44.8 us
  matrix products: 40.6 us -> 0 us
  starting transfers between devices: 0.35 us -> 33.8 us
  between operations: 13.9 us -> 1.68 us
  blocking collectives: 8.15 us -> 0 us
  other arithmetic: 2.84 us -> 10.1 us
    reduce_scatter x2 -> x0, waiting for transfers between devices: 162 us -> none  [the longest x1 83.6 us: body(): lax.psum_scatter(jnp.einsum('snd,ksnc->dkc', portion, grads, preferred_el...]
    all_gather x1 -> x0, waiting for transfers between devices: 79.1 us -> none  [body(): gathered = lax.all_gather(pieces, 'section', axis=2, tiled=True)]
    pallas_call x0 -> x10, Pallas kernels: none -> 44.8 us  [the longest x3 11.4 us: project(): pl.pallas_call(functools.partial(project_kernel, first, count), grid=(4,)...]
    dot_general x27 -> x0, matrix products: 40.6 us -> none  [the longest x1 9.47 us: body(): jnp.einsum('ksnc,dkc->dsn', grads, portion, preferred_element_type=jnp.fl...]
    unnamed x5 -> x0, waiting for transfers between devices: 31.8 us -> none
    ppermute x0 -> x20, waiting for transfers between devices: none -> 26.8 us  [the longest x7 15.2 us: along_dp(): return lax.ppermute(block, 'dp', [(d, (d + step) % 4) for d in range(4)])]
    ppermute x0 -> x20, starting transfers between devices: none -> 19.8 us  [the longest x7 8.2 us: along_dp(): return lax.ppermute(block, 'dp', [(d, (d + step) % 4) for d in range(4)])]
    all_to_all x0 -> x2, starting transfers between devices: none -> 14 us  [the longest x1 9.75 us: spread(): return lax.all_to_all(copies, PLANE, 0, 0, axis_index_groups=groups)]
  transfers between devices with their start and end apart: 4 -> 22, of which waited for: 4 -> 9; matrix products, arithmetic and copies ran while one was open for 4% -> 9% of each run, Pallas kernels for 0% -> 29%
where the time goes in v1:
time: 147 us; the launch traced here: 146 us
  Pallas kernels  44.8 us (30%)
  waiting for transfers between devices  39.1 us (27%)
  starting transfers between devices  33.8 us (23%)
  local copies, waits for them, and re-layouts  16 us (11%)
  other arithmetic  10.1 us (7%)
  between operations  1.68 us (1%)
    ppermute x7, waiting for transfers between devices, along_dp(): return lax.ppermute(block, 'dp', [(d, (d + step) % 4) for d in range(4)])  15.2 us
    ppermute x6, waiting for transfers between devices, near(): return lax.ppermute(block, PLANE, NEAR[dx, dz])  11.6 us
    pallas_call x3, Pallas kernels, project(): pl.pallas_call(functools.partial(project_kernel, first, count), grid=(4,)...  11.4 us
    pallas_call x1, Pallas kernels, attend(): pl.pallas_call(attend_kernel, grid_spec=pltpu.PrefetchScalarGridSpec(num_...  10.7 us
    unnamed x44, local copies, waits for them, and re-layouts  10.1 us
    all_to_all x1, starting transfers between devices, spread(): return lax.all_to_all(copies, PLANE, 0, 0, axis_index_groups=groups)  9.75 us
    pallas_call x4, Pallas kernels, memory_pieces(): pl.pallas_call(memory_kernel, grid=(2,), in_specs=[pl.BlockSpec((1, 1, 2,...  9.47 us
    pallas_call x1, Pallas kernels, weight_rows(): pl.pallas_call(weight_kernel, grid_spec=pltpu.PrefetchScalarGridSpec(num_...  9.29 us
  transfers between devices with their start and end apart: 22, of which 9 were waited for; matrix products, arithmetic and copies ran while one was open for 9% of the time, Pallas kernels for 29%

profile of v1, /device:TPU:33, one launch (start us, length us, event | category | flops | bytes accessed | tf_op | source)
XLA Modules:
  0.0 145.6 jit_solution(8238660337421573074)
XLA Ops:
  2.3 9.7 %all-to-all-start = ((bf16[8,64,512]{2,1,0:T(8,128)(2,1)}), bf16[8,64,512]{2,1,0:T(8,128)(2,1)S(1)}, u32[]{:S(2)}, u32[]{:S(2)}) async-start(bf16[8,64,512]{2,1,0:T(8,128)(2,1)} %broadcast_in_dim.12), calls=%async_computation | async-start | bytes 1048576 | tf_op jit(solution)/shard_map/all_to_all | solution.py:55
  12.1 3.4 %copy-done.3 = bf16[1,4096,2,512]{3,2,1,0:T(2,128)(2,1)S(1)} copy-done((bf16[1,4096,2,512]{3,2,1,0:T(2,128)(2,1)S(1)}, bf16[1,4096,2,512]{3,2,1,0:T(2,128)(2,1)}, u32[]{:S(2)}) %copy-start.3) | copy-done | bytes 8388632
  15.5 3.9 %split_weights.1.refs_2_.refs_3_.refs_5_.weight_ref = bf16[4,2,2,512,512]{4,3,2,1,0:T(8,128)(2,1)S(1)} custom-call(s32[3]{0:T(128)S(1)} %pad_add_fusion.at_ref, bf16[2,4,2,2,2,64,2,512]{7,6,5,4,3,2,1,0:T(2,128)(2,1)S(1)} %bitcast.74), custom_call_target="tpu_custom_call" | custom-call | bytes 33554432 | tf_op jit(solution)/shard_map/split_weights/pallas_call | solution.py:92
  19.5 3.3 %copy-done = bf16[4,2,2,512,512]{4,3,2,1,0:T(8,128)(2,1)} copy-done((bf16[4,2,2,512,512]{4,3,2,1,0:T(8,128)(2,1)}, bf16[4,2,2,512,512]{4,3,2,1,0:T(8,128)(2,1)S(1)}, u32[]{:S(2)}) %copy-start) | copy-done | bytes 8388632
  22.7 7.0 %all-to-all-done = bf16[8,64,512]{2,1,0:T(8,128)(2,1)S(1)} async-done(((bf16[8,64,512]{2,1,0:T(8,128)(2,1)}), bf16[8,64,512]{2,1,0:T(8,128)(2,1)S(1)}, u32[]{:S(2)}, u32[]{:S(2)}) %all-to-all-start) | async-done | bytes 524320 | tf_op jit(solution)/shard_map/all_to_all | solution.py:55
  30.9 2.6 %collective-permute-start.1 = (bf16[512,512]{1,0:T(8,128)(2,1)S(1)}, bf16[512,512]{1,0:T(8,128)(2,1)}, u32[]{:S(2)}, u32[]{:S(2)}) collective-permute-start(bf16[512,512]{1,0:T(8,128)(2,1)S(1)} %bitcast.77), channel_id=1, source_target_pairs={{0,16},{4,116},{8,24},{12,124},{16,0},{20,36},{24,8},{28,44},{32,4... | collective-permute-start | bytes 1572872 | tf_op jit(solution)/shard_map/ppermute | solution.py:72
  34.2 2.5 %collective-permute-start = (bf16[512,512]{1,0:T(8,128)(2,1)S(1)}, bf16[512,512]{1,0:T(8,128)(2,1)S(1)}, u32[]{:S(2)}, u32[]{:S(2)}) collective-permute-start(bf16[512,512]{1,0:T(8,128)(2,1)S(1)} %bitcast.78), channel_id=1, source_target_pairs={{0,4},{4,0},{8,12},{12,8},{16,20},{20,16},{24,28},{28,24},{32,36},... | collective-permute-start | bytes 1572872 | tf_op jit(solution)/shard_map/ppermute | solution.py:68
  36.7 7.9 %collective-permute-done.3.refs_1_ = bf16[512,512]{1,0:T(8,128)(2,1)S(1)} collective-permute-done((bf16[512,512]{1,0:T(8,128)(2,1)S(1)}, bf16[512,512]{1,0:T(8,128)(2,1)S(1)}, u32[]{:S(2)}, u32[]{:S(2)}) %collective-permute-start.3) | collective-permute-done | bytes 524320 | tf_op jit(solution)/shard_map/ppermute | solution.py:72
  46.2 2.9 %broadcast_select_fusion.2 = (bf16[512,512]{1,0:T(8,128)(2,1)}, bf16[512,512]{1,0:T(8,128)(2,1)S(1)}, bf16[512,512]{1,0:T(8,128)(2,1)S(1)}, bf16[512,512]{1,0:T(8,128)(2,1)S(1)}) fusion(bf16[512,512]{1,0:T(8,128)(2,1)} %collective-permute-done.1.refs_1_, bf16[512,512]{1,0:T(8,128)(2,1)} %collective-permute-done.5.refs_3_, pred[]{:T(512)S(6)} %eq.37, ...), kind=kLoop, calls=%fused_computation.18 | loop fusion | flops 1048576 | bytes 3145732 | tf_op jit(solution)/shard_map/jit(_where)/select_n | solution.py:287
  49.2 3.0 %collective-permute-start.9 = (bf16[2,256,512]{2,1,0:T(8,128)(2,1)S(1)}, bf16[2,256,512]{2,1,0:T(8,128)(2,1)S(1)}, u32[]{:S(2)}, u32[]{:S(2)}) collective-permute-start(bf16[2,256,512]{2,1,0:T(8,128)(2,1)S(1)} %pad_maximum_fusion.3), channel_id=1, source_target_pairs={{0,2},{1,3},{2,0},{3,1},{4,6},{5,7},{6,4},{7,5},{8,10},{9,11},{10,... | collective-permute-start | bytes 1572872 | tf_op jit(solution)/shard_map/ppermute | solution.py:64
  52.2 2.9 %collective-permute-start.2 = (bf16[512,512]{1,0:T(8,128)(2,1)}, bf16[512,512]{1,0:T(8,128)(2,1)S(1)}, u32[]{:S(2)}, u32[]{:S(2)}) collective-permute-start(bf16[512,512]{1,0:T(8,128)(2,1)} %collective-permute-done.1.refs_1_), channel_id=1, source_target_pairs={{0,4},{4,0},{8,12},{12,8},{16,20},{20,16},{24,28},{28,24},{32,36},... | collective-permute-start | bytes 1572872 | tf_op jit(solution)/shard_map/ppermute | solution.py:68
  56.7 2.5 %project.3.refs_0_ = f32[2,512,512]{2,1,0:T(8,128)S(1)} custom-call(bf16[512,512]{1,0:T(8,128)(2,1)S(1)} %bitcast.80, bf16[512,512]{1,0:T(8,128)(2,1)S(1)} %collective-permute-done.refs_1_, bf16[4,2,2,512,512]{4,3,2,1,0:T(8,128)(2,1)S(1)} %copy-done.1), custom_call_target="tpu_custom_call" | custom-call | flops 1073741824 | bytes 7340032 | tf_op jit(solution)/shard_map/project/pallas_call | solution.py:132
  60.3 3.7 %project.4.refs_0_ = f32[2,512,512]{2,1,0:T(8,128)S(1)} custom-call(f32[2,512,512]{2,1,0:T(8,128)S(1)} %project.3.refs_0_, bf16[512,512]{1,0:T(8,128)(2,1)} %collective-permute-done.1.refs_1_, bf16[512,512]{1,0:T(8,128)(2,1)S(1)} %collective-permute-done.2.refs_2_, bf16[4,2,2,512,512]{4,3,2,1,0:T(8,128)(2,1)S(1)} %copy-done.1), custom_call_target="tpu_custom_call" | custom-call | flops 1073741824 | bytes 7340032 | tf_op jit(solution)/shard_map/project/pallas_call | solution.py:132
  64.0 5.2 %project.5.pair_ref = bf16[2,512,512]{2,1,0:T(8,128)(2,1)S(1)} custom-call(f32[2,512,512]{2,1,0:T(8,128)S(1)} %project.4.refs_0_, bf16[512,512]{1,0:T(8,128)(2,1)S(1)} %collective-permute-done.3.refs_1_, bf16[512,512]{1,0:T(8,128)(2,1)S(1)} %collective-permute-done.4.refs_2_, bf16[512,512]{1,0:T(8,128)(2,1)} %collective-permute-done.5.refs_3_, ...), custom_call_target="tpu_custom_call" | custom-call | flops 2147483648 | bytes 10485760 | tf_op jit(solution)/shard_map/project/pallas_call | solution.py:132
  69.3 10.7 %attend.1 = (bf16[512,512]{1,0:T(8,128)(2,1)}, bf16[2,512,512]{2,1,0:T(8,128)(2,1)S(1)}, bf16[2,512,512]{2,1,0:T(8,128)(2,1)S(1)}) custom-call(s32[1]{0:T(128)S(6)} %copy.28.length_ref, bf16[512,512]{1,0:T(8,128)(2,1)S(1)} %bitcast.84, bf16[512,512]{1,0:T(8,128)(2,1)S(1)} %bitcast.85, bf16[2,512,512]{2,1,0:T(8,128)(2,1)S(1)} %project.5.pair_ref), custom_call_target="tpu_custom_call" | custom-call | flops 6442450944 | bytes 5242880 | tf_op jit(solution)/shard_map/attend/pallas_call | solution.py:180
  91.3 3.4 %copy-done.2 = bf16[4,2,2,512,512]{4,3,2,1,0:T(8,128)(2,1)S(1)} copy-done((bf16[4,2,2,512,512]{4,3,2,1,0:T(8,128)(2,1)S(1)}, bf16[4,2,2,512,512]{4,3,2,1,0:T(8,128)(2,1)}, u32[]{:S(2)}) %copy-start.2) | copy-done | bytes 8388632
  94.6 2.5 %memory_pieces.5 = bf16[2,512,512]{2,1,0:T(8,128)(2,1)S(1)} custom-call(bf16[4,2,2,512,512]{4,3,2,1,0:T(8,128)(2,1)S(1)} %copy-done.2, bf16[2,512,512]{2,1,0:T(8,128)(2,1)S(1)} %get-tuple-element.17.turned_ref, bf16[2,512,512]{2,1,0:T(8,128)(2,1)} %collective-permute-done.10.refs_0_), custom_call_target="tpu_custom_call" | custom-call | flops 1073741824 | bytes 6291456 | tf_op jit(solution)/shard_map/memory_pieces/pallas_call | solution.py:208
  97.3 2.5 %memory_pieces.7 = bf16[2,512,512]{2,1,0:T(8,128)(2,1)S(1)} custom-call(bf16[4,2,2,512,512]{4,3,2,1,0:T(8,128)(2,1)S(1)} %copy-done.2, bf16[2,512,512]{2,1,0:T(8,128)(2,1)S(1)} %get-tuple-element.17.turned_ref, bf16[2,512,512]{2,1,0:T(8,128)(2,1)} %collective-permute-done.12.refs_0_), custom_call_target="tpu_custom_call" | custom-call | flops 1073741824 | bytes 6291456 | tf_op jit(solution)/shard_map/memory_pieces/pallas_call | solution.py:208
  100.1 9.8 %collective-permute-done.17.g2 = bf16[2,512,512]{2,1,0:T(8,128)(2,1)S(1)} collective-permute-done((bf16[2,512,512]{2,1,0:T(8,128)(2,1)}, bf16[2,512,512]{2,1,0:T(8,128)(2,1)S(1)}, u32[]{:S(2)}, u32[]{:S(2)}) %collective-permute-start.17) | collective-permute-done | bytes 1048608 | tf_op jit(solution)/shard_map/ppermute | solution.py:64
  111.6 3.0 %collective-permute-done.16.g1 = bf16[2,512,512]{2,1,0:T(8,128)(2,1)S(1)} collective-permute-done((bf16[2,512,512]{2,1,0:T(8,128)(2,1)}, bf16[2,512,512]{2,1,0:T(8,128)(2,1)S(1)}, u32[]{:S(2)}, u32[]{:S(2)}) %collective-permute-start.16) | collective-permute-done | bytes 1048608 | tf_op jit(solution)/shard_map/ppermute | solution.py:64
  116.9 3.0 %collective-permute-done.14 = bf16[512,512]{1,0:T(8,128)(2,1)S(1)} collective-permute-done((bf16[512,512]{1,0:T(8,128)(2,1)S(1)}, bf16[512,512]{1,0:T(8,128)(2,1)S(1)}, u32[]{:S(2)}, u32[]{:S(2)}) %collective-permute-start.14) | collective-permute-done | bytes 524320 | tf_op jit(solution)/shard_map/ppermute | solution.py:72
  121.1 4.3 %all-to-all-start.1 = ((bf16[8,64,512]{2,1,0:T(8,128)(2,1)}), bf16[8,64,512]{2,1,0:T(8,128)(2,1)}, u32[]{:S(2)}, u32[]{:S(2)}) async-start(bf16[8,64,512]{2,1,0:T(8,128)(2,1)} %bitcast.86), calls=%async_computation.1 | async-start | bytes 1048576 | tf_op jit(solution)/shard_map/all_to_all | solution.py:59
  129.2 9.3 %weight_rows.1 = bf16[2,2,2,2,64,2,512]{6,5,4,3,2,1,0:T(2,128)(2,1)} custom-call(s32[3]{0:T(128)S(1)} %pad_add_fusion.at_ref, bf16[2,256,512]{2,1,0:T(8,128)(2,1)S(1)} %copy-done.4, bf16[2,256,512]{2,1,0:T(8,128)(2,1)S(1)} %pad_maximum_fusion.5.other, bf16[2,256,512]{2,1,0:T(8,128)(2,1)S(1)} %copy-done.13, bf16[2,256,512]{2,1,0:T(8,128)(2,1)S(1)} %copy-done.10, ...), custom_call_target="tpu_custom_call" | custom-call | flops 4294967296 | bytes 12582912 | tf_op jit(solution)/shard_map/weight_rows/pallas_call | solution.py:243
  138.5 5.3 %all-to-all-done.1 = bf16[8,64,512]{2,1,0:T(8,128)(2,1)} async-done(((bf16[8,64,512]{2,1,0:T(8,128)(2,1)}), bf16[8,64,512]{2,1,0:T(8,128)(2,1)}, u32[]{:S(2)}, u32[]{:S(2)}) %all-to-all-start.1) | async-done | bytes 524320 | tf_op jit(solution)/shard_map/all_to_all | solution.py:59
  (97 shorter events, 29.6 us)
Async XLA Ops:
  2.3 27.4 %all-to-all-start = ((bf16[8,64,512]{2,1,0:T(8,128)(2,1)}), bf16[8,64,512]{2,1,0:T(8,128)(2,1)S(1)}, u32[]{:S(2)}, u32[]{:S(2)}) async-start(bf16[8,64,512]{2,1,0:T(8,128)(2,1)} %broadcast_in_dim.12), calls=%async_computation | async-start | bytes 1048576 | tf_op jit(solution)/shard_map/all_to_all | solution.py:55
  29.7 14.9 %collective-permute-start.3 = (bf16[512,512]{1,0:T(8,128)(2,1)S(1)}, bf16[512,512]{1,0:T(8,128)(2,1)S(1)}, u32[]{:S(2)}, u32[]{:S(2)}) collective-permute-start(bf16[512,512]{1,0:T(8,128)(2,1)S(1)} %bitcast.75), channel_id=1, source_target_pairs={{0,128},{4,140},{8,136},{12,132},{16,144},{20,156},{24,152},{28,14... | collective-permute-start | bytes 1572872 | tf_op jit(solution)/shard_map/ppermute | solution.py:72
  30.0 15.6 %collective-permute-start.5 = (bf16[512,512]{1,0:T(8,128)(2,1)S(1)}, bf16[512,512]{1,0:T(8,128)(2,1)}, u32[]{:S(2)}, u32[]{:S(2)}) collective-permute-start(bf16[512,512]{1,0:T(8,128)(2,1)S(1)} %bitcast.76), channel_id=1, source_target_pairs={{0,144},{4,252},{8,152},{12,244},{16,128},{20,172},{24,136},{28,16... | collective-permute-start | bytes 1572872 | tf_op jit(solution)/shard_map/ppermute | solution.py:72
  30.9 15.3 %collective-permute-start.1 = (bf16[512,512]{1,0:T(8,128)(2,1)S(1)}, bf16[512,512]{1,0:T(8,128)(2,1)}, u32[]{:S(2)}, u32[]{:S(2)}) collective-permute-start(bf16[512,512]{1,0:T(8,128)(2,1)S(1)} %bitcast.77), channel_id=1, source_target_pairs={{0,16},{4,116},{8,24},{12,124},{16,0},{20,36},{24,8},{28,44},{32,4... | collective-permute-start | bytes 1572872 | tf_op jit(solution)/shard_map/ppermute | solution.py:72
  34.2 21.6 %collective-permute-start = (bf16[512,512]{1,0:T(8,128)(2,1)S(1)}, bf16[512,512]{1,0:T(8,128)(2,1)S(1)}, u32[]{:S(2)}, u32[]{:S(2)}) collective-permute-start(bf16[512,512]{1,0:T(8,128)(2,1)S(1)} %bitcast.78), channel_id=1, source_target_pairs={{0,4},{4,0},{8,12},{12,8},{16,20},{20,16},{24,28},{28,24},{32,36},... | collective-permute-start | bytes 1572872 | tf_op jit(solution)/shard_map/ppermute | solution.py:68
  44.6 12.1 %copy-start.1 = (bf16[4,2,2,512,512]{4,3,2,1,0:T(8,128)(2,1)S(1)}, bf16[4,2,2,512,512]{4,3,2,1,0:T(8,128)(2,1)}, u32[]{:S(2)}) copy-start(bf16[4,2,2,512,512]{4,3,2,1,0:T(8,128)(2,1)} %copy-done) | copy-start | bytes 25165828
  49.2 30.8 %collective-permute-start.9 = (bf16[2,256,512]{2,1,0:T(8,128)(2,1)S(1)}, bf16[2,256,512]{2,1,0:T(8,128)(2,1)S(1)}, u32[]{:S(2)}, u32[]{:S(2)}) collective-permute-start(bf16[2,256,512]{2,1,0:T(8,128)(2,1)S(1)} %pad_maximum_fusion.3), channel_id=1, source_target_pairs={{0,2},{1,3},{2,0},{3,1},{4,6},{5,7},{6,4},{7,5},{8,10},{9,11},{10,... | collective-permute-start | bytes 1572872 | tf_op jit(solution)/shard_map/ppermute | solution.py:64
  52.2 7.2 %collective-permute-start.2 = (bf16[512,512]{1,0:T(8,128)(2,1)}, bf16[512,512]{1,0:T(8,128)(2,1)S(1)}, u32[]{:S(2)}, u32[]{:S(2)}) collective-permute-start(bf16[512,512]{1,0:T(8,128)(2,1)} %collective-permute-done.1.refs_1_), channel_id=1, source_target_pairs={{0,4},{4,0},{8,12},{12,8},{16,20},{20,16},{24,28},{28,24},{32,36},... | collective-permute-start | bytes 1572872 | tf_op jit(solution)/shard_map/ppermute | solution.py:68
  55.2 8.8 %collective-permute-start.6 = (bf16[512,512]{1,0:T(8,128)(2,1)}, bf16[512,512]{1,0:T(8,128)(2,1)S(1)}, u32[]{:S(2)}, u32[]{:S(2)}) collective-permute-start(bf16[512,512]{1,0:T(8,128)(2,1)} %collective-permute-done.5.refs_3_), channel_id=1, source_target_pairs={{0,4},{4,0},{8,12},{12,8},{16,20},{20,16},{24,28},{28,24},{32,36},... | collective-permute-start | bytes 1572872 | tf_op jit(solution)/shard_map/ppermute | solution.py:68
  55.3 8.7 %collective-permute-start.4 = (bf16[512,512]{1,0:T(8,128)(2,1)S(1)}, bf16[512,512]{1,0:T(8,128)(2,1)S(1)}, u32[]{:S(2)}, u32[]{:S(2)}) collective-permute-start(bf16[512,512]{1,0:T(8,128)(2,1)S(1)} %collective-permute-done.3.refs_1_), channel_id=1, source_target_pairs={{0,4},{4,0},{8,12},{12,8},{16,20},{20,16},{24,28},{28,24},{32,36},... | collective-permute-start | bytes 1572872 | tf_op jit(solution)/shard_map/ppermute | solution.py:68
  55.8 24.1 %collective-permute-start.8 = (bf16[2,256,512]{2,1,0:T(8,128)(2,1)S(1)}, bf16[2,256,512]{2,1,0:T(8,128)(2,1)S(1)}, u32[]{:S(2)}, u32[]{:S(2)}) collective-permute-start(bf16[2,256,512]{2,1,0:T(8,128)(2,1)S(1)} %pad_maximum_fusion.2), channel_id=1, source_target_pairs={{0,3},{1,0},{2,1},{3,2},{4,7},{5,4},{6,5},{7,6},{8,11},{9,8},{10,9... | collective-permute-start | bytes 1572872 | tf_op jit(solution)/shard_map/ppermute | solution.py:64
  59.4 20.6 %collective-permute-start.7 = (bf16[2,256,512]{2,1,0:T(8,128)(2,1)S(1)}, bf16[2,256,512]{2,1,0:T(8,128)(2,1)S(1)}, u32[]{:S(2)}, u32[]{:S(2)}) collective-permute-start(bf16[2,256,512]{2,1,0:T(8,128)(2,1)S(1)} %pad_maximum_fusion.1), channel_id=1, source_target_pairs={{0,1},{1,2},{2,3},{3,0},{4,5},{5,6},{6,7},{7,4},{8,9},{9,10},{10,1... | collective-permute-start | bytes 1572872 | tf_op jit(solution)/shard_map/ppermute | solution.py:64
  82.3 9.0 %collective-permute-start.10 = (bf16[2,512,512]{2,1,0:T(8,128)(2,1)}, bf16[2,512,512]{2,1,0:T(8,128)(2,1)}, u32[]{:S(2)}, u32[]{:S(2)}) collective-permute-start(bf16[2,512,512]{2,1,0:T(8,128)(2,1)} %memory_pieces.4), channel_id=1, source_target_pairs={{0,4},{4,0},{8,12},{12,8},{16,20},{20,16},{24,28},{28,24},{32,36},... | collective-permute-start | bytes 3145736 | tf_op jit(solution)/shard_map/ppermute | solution.py:68
  85.2 12.0 %collective-permute-start.12 = (bf16[2,512,512]{2,1,0:T(8,128)(2,1)}, bf16[2,512,512]{2,1,0:T(8,128)(2,1)}, u32[]{:S(2)}, u32[]{:S(2)}) collective-permute-start(bf16[2,512,512]{2,1,0:T(8,128)(2,1)} %memory_pieces.6), channel_id=1, source_target_pairs={{0,4},{4,0},{8,12},{12,8},{16,20},{20,16},{24,28},{28,24},{32,36},... | collective-permute-start | bytes 3145736 | tf_op jit(solution)/shard_map/ppermute | solution.py:68
  85.3 24.6 %collective-permute-start.17 = (bf16[2,512,512]{2,1,0:T(8,128)(2,1)}, bf16[2,512,512]{2,1,0:T(8,128)(2,1)S(1)}, u32[]{:S(2)}, u32[]{:S(2)}) collective-permute-start(bf16[2,512,512]{2,1,0:T(8,128)(2,1)} %copy-done.18), channel_id=1, source_target_pairs={{0,3},{1,0},{2,1},{3,2},{4,7},{5,4},{6,5},{7,6},{8,11},{9,8},{10,9... | collective-permute-start | bytes 3145736 | tf_op jit(solution)/shard_map/ppermute | solution.py:64
  89.2 25.4 %collective-permute-start.16 = (bf16[2,512,512]{2,1,0:T(8,128)(2,1)}, bf16[2,512,512]{2,1,0:T(8,128)(2,1)S(1)}, u32[]{:S(2)}, u32[]{:S(2)}) collective-permute-start(bf16[2,512,512]{2,1,0:T(8,128)(2,1)} %copy-done.18), channel_id=1, source_target_pairs={{0,1},{1,2},{2,3},{3,0},{4,5},{5,6},{6,7},{7,4},{8,9},{9,10},{10,1... | collective-permute-start | bytes 3145736 | tf_op jit(solution)/shard_map/ppermute | solution.py:64
  90.5 38.6 %collective-permute-start.15 = (bf16[3,2,256,512]{3,2,1,0:T(8,128)(2,1)}, bf16[3,2,256,512]{3,2,1,0:T(8,128)(2,1)}, u32[]{:S(2)}, u32[]{:S(2)}) collective-permute-start(bf16[3,2,256,512]{3,2,1,0:T(8,128)(2,1)} %pad_maximum_fusion), channel_id=1, source_target_pairs={{0,4},{4,0},{8,12},{12,8},{16,20},{20,16},{24,28},{28,24},{32,36},... | collective-permute-start | bytes 4718600 | tf_op jit(solution)/shard_map/ppermute | solution.py:68
  97.2 18.6 %collective-permute-start.11 = (bf16[512,512]{1,0:T(8,128)(2,1)S(1)}, bf16[512,512]{1,0:T(8,128)(2,1)S(1)}, u32[]{:S(2)}, u32[]{:S(2)}) collective-permute-start(bf16[512,512]{1,0:T(8,128)(2,1)S(1)} %slice_bitcast_fusion.4), channel_id=1, source_target_pairs={{0,16},{4,116},{8,24},{12,124},{16,0},{20,36},{24,8},{28,44},{32,4... | collective-permute-start | bytes 1572872 | tf_op jit(solution)/shard_map/ppermute | solution.py:72
  99.9 17.1 %collective-permute-start.13 = (bf16[512,512]{1,0:T(8,128)(2,1)S(1)}, bf16[512,512]{1,0:T(8,128)(2,1)S(1)}, u32[]{:S(2)}, u32[]{:S(2)}) collective-permute-start(bf16[512,512]{1,0:T(8,128)(2,1)S(1)} %get-tuple-element.31), channel_id=1, source_target_pairs={{0,128},{4,140},{8,136},{12,132},{16,144},{20,156},{24,152},{28,14... | collective-permute-start | bytes 1572872 | tf_op jit(solution)/shard_map/ppermute | solution.py:72
  109.9 10.1 %collective-permute-start.14 = (bf16[512,512]{1,0:T(8,128)(2,1)S(1)}, bf16[512,512]{1,0:T(8,128)(2,1)S(1)}, u32[]{:S(2)}, u32[]{:S(2)}) collective-permute-start(bf16[512,512]{1,0:T(8,128)(2,1)S(1)} %get-tuple-element.32), channel_id=1, source_target_pairs={{0,144},{4,252},{8,152},{12,244},{16,128},{20,172},{24,136},{28,16... | collective-permute-start | bytes 1572872 | tf_op jit(solution)/shard_map/ppermute | solution.py:72
  114.6 12.2 %collective-permute-start.19 = (bf16[512,512]{1,0:T(8,128)(2,1)}, bf16[512,512]{1,0:T(8,128)(2,1)}, u32[]{:S(2)}, u32[]{:S(2)}) collective-permute-start(bf16[512,512]{1,0:T(8,128)(2,1)} %slice_bitcast_fusion), channel_id=1, source_target_pairs={{0,3},{1,0},{2,1},{3,2},{4,7},{5,4},{6,5},{7,6},{8,11},{9,8},{10,9... | collective-permute-start | bytes 1572872 | tf_op jit(solution)/shard_map/ppermute | solution.py:64
  115.8 13.4 %collective-permute-start.18 = (bf16[512,512]{1,0:T(8,128)(2,1)}, bf16[512,512]{1,0:T(8,128)(2,1)}, u32[]{:S(2)}, u32[]{:S(2)}) collective-permute-start(bf16[512,512]{1,0:T(8,128)(2,1)} %slice_bitcast_fusion.1), channel_id=1, source_target_pairs={{0,1},{1,2},{2,3},{3,0},{4,5},{5,6},{6,7},{7,4},{8,9},{9,10},{10,1... | collective-permute-start | bytes 1572872 | tf_op jit(solution)/shard_map/ppermute | solution.py:64
  120.0 9.2 %copy-start.19 = (bf16[2,512,512]{2,1,0:T(8,128)(2,1)S(1)}, bf16[2,512,512]{2,1,0:T(8,128)(2,1)}, u32[]{:S(2)}) copy-start(bf16[2,512,512]{2,1,0:T(8,128)(2,1)} %copy-done.18) | copy-start | bytes 3145732
  121.1 22.7 %all-to-all-start.1 = ((bf16[8,64,512]{2,1,0:T(8,128)(2,1)}), bf16[8,64,512]{2,1,0:T(8,128)(2,1)}, u32[]{:S(2)}, u32[]{:S(2)}) async-start(bf16[8,64,512]{2,1,0:T(8,128)(2,1)} %bitcast.86), calls=%async_computation.1 | async-start | bytes 1048576 | tf_op jit(solution)/shard_map/all_to_all | solution.py:59
  (20 other events, 80.9 us)

commit v2 on v1

--- a/solution.py
+++ b/solution.py
@@ -11,6 +11,7 @@
 HD = 64
 HEADS = 8
 F32 = jnp.float32
+COST = pl.CostEstimate(flops=0, bytes_accessed=1 << 16, transcendentals=0)
 BF16 = jnp.bfloat16
 VMEM = 28 << 20
 
@@ -104,7 +105,7 @@
         ),
         out_shape=jax.ShapeDtypeStruct((4, 2, 2, 512, 512), BF16),
         compiler_params=pltpu.CompilerParams(vmem_limit_bytes=VMEM),
-        cost_estimate=pl.CostEstimate(flops=0, bytes_accessed=32 << 20, transcendentals=0),
+        cost_estimate=COST,
         name="split_weights",
     )(at, view)
 
@@ -139,9 +140,7 @@
         scratch_shapes=[pltpu.VMEM((512, 1024 * count), BF16)],
         out_shape=jax.ShapeDtypeStruct((2, 512, 512), BF16 if last else F32),
         compiler_params=pltpu.CompilerParams(vmem_limit_bytes=VMEM),
-        cost_estimate=pl.CostEstimate(
-            flops=2 * 512 * 1024 * 1024 * count, bytes_accessed=(3 * count + 4) << 20, transcendentals=0
-        ),
+        cost_estimate=COST,
         name="project",
     )(*([] if first else [sums]), *rows, split)
 
@@ -191,78 +190,106 @@
             jax.ShapeDtypeStruct((2, 512, 512), BF16),
         ],
         compiler_params=pltpu.CompilerParams(vmem_limit_bytes=VMEM),
-        cost_estimate=pl.CostEstimate(flops=8 * 6 * 2 * 512 * 512 * 64 * 4, bytes_accessed=5 << 20, transcendentals=8 << 18),
+        cost_estimate=COST,
         name="attend",
     )(lengths, queries, out_grad, pair)
 
 
-def memory_kernel(weight_ref, turned_ref, *refs):
+def other_kernel(weight_ref, turned_ref, out_ref):
     total = dot(weight_ref[0, 0, 0], turned_ref[0], NN) + dot(weight_ref[0, 0, 1], turned_ref[1], NN)
-    if len(refs) == 2:
-        total = total + refs[0][0].astype(F32)
-    refs[-1][0] = total.astype(BF16)
-
-
-def memory_pieces(split, turned, upper, half, sent=None):
+    out_ref[0] = total.astype(BF16)
+
+
+def own_kernel(weight_ref, turned_ref, sent_ref, *outs):
+    total = dot(weight_ref[0, 0, 0], turned_ref[0], NN) + dot(weight_ref[0, 0, 1], turned_ref[1], NN)
+    total = (total + sent_ref[0].astype(F32)).astype(BF16)
+    for i, out_ref in enumerate(outs):
+
+        @pl.when(pl.program_id(0) == i)
+        def _():
+            out_ref[...] = total
+
+
+def memory_pieces(split, turned, upper, sent=None):
     rows = pl.BlockSpec((1, 512, 512), lambda i: (i, 0, 0))
-    return pl.pallas_call(
-        memory_kernel,
+    half = 1 if sent is None else 0
+    one = jax.ShapeDtypeStruct((512, 512), BF16)
+    return pl.pallas_call(
+        other_kernel if sent is None else own_kernel,
         grid=(2,),
         in_specs=[
             pl.BlockSpec((1, 1, 2, 512, 512), lambda i: (upper - i, half, 0, 0, 0)),
             pl.BlockSpec((2, 512, 512), lambda i: (0, 0, 0)),
         ]
         + ([] if sent is None else [rows]),
-        out_specs=rows,
-        out_shape=jax.ShapeDtypeStruct((2, 512, 512), BF16),
-        compiler_params=pltpu.CompilerParams(vmem_limit_bytes=VMEM),
-        cost_estimate=pl.CostEstimate(flops=512 * 2048 * 1024, bytes_accessed=6 << 20, transcendentals=0),
+        out_specs=rows if sent is None else [pl.BlockSpec((512, 512), lambda i: (0, 0))] * 2,
+        out_shape=jax.ShapeDtypeStruct((2, 512, 512), BF16) if sent is None else [one, one],
+        compiler_params=pltpu.CompilerParams(vmem_limit_bytes=VMEM),
+        cost_estimate=COST,
         name="memory_pieces",
     )(split, turned, *([] if sent is None else [sent]))
 
 
-def weight_kernel(at_ref, mine, other, left, right, across, swapped, g0, g1, g2, gk, gv, out_ref):
+def sum_kernel(at_ref, mine, other, left, right, swapped, g0, g1, g2, out_ref):
     own = pl.program_id(0) < 2
-    rows = [jnp.where(own, mine[0], other[0])]
-    for i, block in enumerate((left, right, across)):
-        rows.append(jnp.where(own, block[0], swapped[i, 0]))
-    keys = (g0[0], g1[0], g2[0], gk[...])
-    values = (g0[1], g1[1], g2[1], gv[...])
-    for_key = sum(dot(a, b, NN) for a, b in zip(rows, keys))
-    for_value = sum(dot(a, b, NN) for a, b in zip(rows, values))
+    pairs = ((mine[0], other[0]), (left[0], swapped[0, 0]), (right[0], swapped[1, 0]))
+    rows = [jnp.where(own, here, there) for here, there in pairs]
+    for kind in range(2):
+        out_ref[0, kind] = sum(dot(a, b[kind], NN) for a, b in zip(rows, (g0, g1, g2)))
+
+
+def last_kernel(at_ref, across, swapped, key, value, sums, out_ref):
+    rows = jnp.where(pl.program_id(0) < 2, across[0], swapped[0, 0])
+    for_key = sums[0, 0] + dot(rows, key[...], NN)
+    for_value = sums[0, 1] + dot(rows, value[...], NN)
     both = jnp.stack([for_key.astype(BF16), for_value.astype(BF16)], axis=0)
     both = jnp.swapaxes(both, 0, 1).reshape(2, 2, 64, 2, 512)
     out_ref[...] = jnp.swapaxes(both, 0, 1).reshape(2, 1, 2, 1, 64, 2, 512)
 
 
-def weight_rows(at, mine, other, left, right, across, swapped, g0, g1, g2, gk, gv):
-    def whole(shape):
-        return pl.BlockSpec(shape, lambda i, at: (0,) * len(shape))
-
-    half = pl.BlockSpec((1, 256, 512), lambda i, at: (i % 2, 0, 0))
-    out = pl.pallas_call(
-        weight_kernel,
+HALF = pl.BlockSpec((1, 256, 512), lambda i, at: (i % 2, 0, 0))
+SUMS = pl.BlockSpec((1, 2, 256, 512), lambda i, at: (i, 0, 0, 0))
+
+
+def whole(shape):
+    return pl.BlockSpec(shape, lambda i, at: (0,) * len(shape))
+
+
+def weight_sums(at, mine, other, left, right, swapped, grads):
+    return pl.pallas_call(
+        sum_kernel,
         grid_spec=pltpu.PrefetchScalarGridSpec(
             num_scalar_prefetch=1,
             grid=(4,),
-            in_specs=[half] * 5
-            + [
-                pl.BlockSpec((3, 1, 256, 512), lambda i, at: (0, i % 2, 0, 0)),
-                whole((2, 512, 512)),
-                whole((2, 512, 512)),
-                whole((2, 512, 512)),
-                whole((512, 512)),
-                whole((512, 512)),
-            ],
+            in_specs=[HALF] * 4
+            + [pl.BlockSpec((2, 1, 256, 512), lambda i, at: (0, i % 2, 0, 0))]
+            + [whole((2, 512, 512))] * 3,
+            out_specs=SUMS,
+        ),
+        out_shape=jax.ShapeDtypeStruct((4, 2, 256, 512), F32),
+        compiler_params=pltpu.CompilerParams(vmem_limit_bytes=VMEM),
+        cost_estimate=COST,
+        name="weight_sums",
+    )(at, mine, other, left, right, swapped, *grads)
+
+
+def weight_rows(at, across, swapped, key, value, sums):
+    out = pl.pallas_call(
+        last_kernel,
+        grid_spec=pltpu.PrefetchScalarGridSpec(
+            num_scalar_prefetch=1,
+            grid=(4,),
+            in_specs=[HALF, pl.BlockSpec((1, 1, 256, 512), lambda i, at: (2, i % 2, 0, 0))]
+            + [whole((512, 512)), whole((512, 512)), SUMS],
             out_specs=pl.BlockSpec(
                 (2, 1, 2, 1, 64, 2, 512), lambda i, at: (0, at[1] ^ (i % 2), 0, at[2] ^ (i // 2), 0, 0, 0)
             ),
         ),
         out_shape=jax.ShapeDtypeStruct((2, 2, 2, 2, 64, 2, 512), BF16),
         compiler_params=pltpu.CompilerParams(vmem_limit_bytes=VMEM),
-        cost_estimate=pl.CostEstimate(flops=2 * 2048 * 1024 * 1024, bytes_accessed=12 << 20, transcendentals=0),
+        cost_estimate=COST,
         name="weight_rows",
-    )(at, mine, other, left, right, across, swapped, g0, g1, g2, gk, gv)
+    )(at, across, swapped, key, value, sums)
     return out.reshape(1, 1024, 2, 512)
 
 
@@ -274,9 +301,12 @@
     split = split_weights(at, memory_weight[0])
     own = spread(memory[:, 0, :].T, FAR).reshape(512, 512)
     own, split = lax.optimization_barrier((own, split))
-    mine = [own, near(own, 0, 1), near(own, 1, 0), near(own, 1, 1)]
-    other = [swap(piece) for piece in mine]
-    sums = project(None, [mine[0], other[0]], split, 0, False)
+    own_other = swap(own)
+    from_z, from_x, from_diagonal = near(own, 0, 1), near(own, 1, 0), near(own, 1, 1)
+    sums = project(None, [own, own_other], split, 0, False)
+    sums, from_z, from_x, from_diagonal = lax.optimization_barrier((sums, from_z, from_x, from_diagonal))
+    mine = [own, from_z, from_x, from_diagonal]
+    other = [own_other] + [swap(piece) for piece in mine[1:]]
     sums = project(sums, [mine[1], other[1]], split, 1, False)
     pair = project(sums, [mine[2], other[2], mine[3], other[3]], split, 2, True)
 
@@ -291,36 +321,30 @@
     arrived = [along_dp(block_of(mine, (dp + step) % 4), step) for step in (1, 3, 2)]
 
     query_grad, grads, turned = attend(lengths, queries[0, 0], out_grad[0, 0], pair)
-    grads, turned, arrived = lax.optimization_barrier((grads, turned, arrived))
+    left, right, across = arrived
+    grads, turned, left, right = lax.optimization_barrier((grads, turned, left, right))
 
     from_left = along_dp(grads, 1)
     from_right = along_dp(grads, 3)
+    for_other, across = lax.optimization_barrier((memory_pieces(split, turned, 3), across))
+    sent_far = swap(for_other)
+    sent_near = swap(memory_pieces(split, turned, 1))
+    diagonal, far_x = memory_pieces(split, turned, 3, sent_far)
+    from_diagonal, from_x = near(diagonal, 1, 1), near(far_x, 1, 0)
+    close_z, close = memory_pieces(split, turned, 1, sent_near)
+    from_z = near(close_z, 0, 1)
+    terms = (close, from_z, from_x, from_diagonal)
+    quarter = sum(term.astype(F32) for term in terms).astype(BF16)
+    _, from_left, from_right = lax.optimization_barrier((quarter, from_left, from_right))
     across_key = along_dp(from_left[0], 1)
     across_value = along_dp(from_right[1], 3)
-
-    sent_far = swap(memory_pieces(split, turned, 3, 1))
-    sent_near = swap(memory_pieces(split, turned, 1, 1))
-    far = memory_pieces(split, turned, 3, 0, sent_far)
-    from_diagonal, from_x = near(far[0], 1, 1), near(far[1], 1, 0)
-    close = memory_pieces(split, turned, 1, 0, sent_near)
-    from_z = near(close[0], 0, 1)
-    terms = (close[1], from_z, from_x, from_diagonal)
-    quarter = sum(term.astype(F32) for term in terms).astype(BF16)
     memory_grad = collect(quarter.reshape(8, 64, 512), FAR).T[:, None, :]
 
-    swapped = swap(jnp.stack(arrived))
-    weight_grad = weight_rows(
-        at,
-        block_of(mine, dp),
-        block_of(other, dp),
-        *arrived,
-        swapped,
-        grads,
-        from_left,
-        from_right,
-        across_key,
-        across_value,
-    )
+    swapped = swap(jnp.stack([left, right, across]))
+    rows, rows_other = block_of(mine, dp), block_of(other, dp)
+    sums = weight_sums(at, rows, rows_other, left, right, swapped, (grads, from_left, from_right))
+    sums, across_key, across_value = lax.optimization_barrier((sums, across_key, across_value))
+    weight_grad = weight_rows(at, across, swapped, across_key, across_value, sums)
     return memory_grad, query_grad[None, None], weight_grad
 
 

time: 147 us -> 138 us (0.939)
  the two profiles are of different devices: /device:TPU:33 before, /device:TPU:6 now
where the time goes in v2:
time: 138 us
  starting transfers between devices  44.7 us (32%)
  Pallas kernels  42 us (30%)
  waiting for transfers between devices  25.1 us (18%)
  local copies, waits for them, and re-layouts  16.9 us (12%)
  other arithmetic  7.26 us (5%)
  between operations  1.8 us (1%)
    ppermute x6, waiting for transfers between devices, near(): return lax.ppermute(block, PLANE, NEAR[dx, dz])  14.4 us
    ppermute x7, starting transfers between devices, along_dp(): return lax.ppermute(block, 'dp', [(d, (d + step) % 4) for d in range(4)])  14.3 us
    unnamed x46, local copies, waits for them, and re-layouts  12 us
    all_to_all x1, starting transfers between devices, spread(): return lax.all_to_all(copies, PLANE, 0, 0, axis_index_groups=groups)  11.4 us
    pallas_call x1, Pallas kernels, attend(): pl.pallas_call(attend_kernel, grid_spec=pltpu.PrefetchScalarGridSpec(num_...  10.9 us
    pallas_call x3, Pallas kernels, project(): pl.pallas_call(functools.partial(project_kernel, first, count), grid=(4,)...  9.43 us
    ppermute x6, starting transfers between devices, near(): return lax.ppermute(block, PLANE, NEAR[dx, dz])  8.2 us
    ppermute x7, waiting for transfers between devices, along_dp(): return lax.ppermute(block, 'dp', [(d, (d + step) % 4) for d in range(4)])  7.16 us
  transfers between devices with their start and end apart: 22, of which 7 were waited for; matrix products, arithmetic and copies ran while one was open for 6% of the time, Pallas kernels for 30%

profile of v2, /device:TPU:6, one launch (start us, length us, event | category | flops | bytes accessed | tf_op | source)
XLA Modules:
  0.0 137.8 jit_solution(17423606443478106552)
XLA Ops:
  2.3 11.4 %all-to-all-start = ((bf16[8,64,512]{2,1,0:T(8,128)(2,1)}), bf16[8,64,512]{2,1,0:T(8,128)(2,1)S(1)}, u32[]{:S(2)}, u32[]{:S(2)}) async-start(bf16[8,64,512]{2,1,0:T(8,128)(2,1)} %broadcast_in_dim.12), calls=%async_computation | async-start | bytes 1048576 | tf_op jit(solution)/shard_map/all_to_all | solution.py:56
  13.8 3.4 %copy-done.2 = bf16[1,4096,2,512]{3,2,1,0:T(2,128)(2,1)S(1)} copy-done((bf16[1,4096,2,512]{3,2,1,0:T(2,128)(2,1)S(1)}, bf16[1,4096,2,512]{3,2,1,0:T(2,128)(2,1)}, u32[]{:S(2)}) %copy-start.2) | copy-done | bytes 8388632
  17.2 3.9 %split_weights.1.refs_2_.refs_3_.refs_5_.weight_ref = bf16[4,2,2,512,512]{4,3,2,1,0:T(8,128)(2,1)S(1)} custom-call(s32[3]{0:T(128)S(1)} %pad_add_fusion.at_ref, bf16[2,4,2,2,2,64,2,512]{7,6,5,4,3,2,1,0:T(2,128)(2,1)S(1)} %bitcast.65), custom_call_target="tpu_custom_call" | custom-call | bytes 65536 | tf_op jit(solution)/shard_map/split_weights/pallas_call | solution.py:93
  21.1 3.3 %copy-done = bf16[4,2,2,512,512]{4,3,2,1,0:T(8,128)(2,1)} copy-done((bf16[4,2,2,512,512]{4,3,2,1,0:T(8,128)(2,1)}, bf16[4,2,2,512,512]{4,3,2,1,0:T(8,128)(2,1)S(1)}, u32[]{:S(2)}) %copy-start) | copy-done | bytes 8388632
  24.4 3.6 %all-to-all-done = bf16[8,64,512]{2,1,0:T(8,128)(2,1)S(1)} async-done(((bf16[8,64,512]{2,1,0:T(8,128)(2,1)}), bf16[8,64,512]{2,1,0:T(8,128)(2,1)S(1)}, u32[]{:S(2)}, u32[]{:S(2)}) %all-to-all-start) | async-done | bytes 524320 | tf_op jit(solution)/shard_map/all_to_all | solution.py:56
  28.0 3.5 %collective-permute-start.3 = (bf16[512,512]{1,0:T(8,128)(2,1)S(1)}, bf16[512,512]{1,0:T(8,128)(2,1)S(1)}, u32[]{:S(2)}, u32[]{:S(2)}) collective-permute-start(bf16[512,512]{1,0:T(8,128)(2,1)S(1)} %bitcast.67), channel_id=1, source_target_pairs={{0,144},{4,252},{8,152},{12,244},{16,128},{20,172},{24,136},{28,16... | collective-permute-start | bytes 1572872 | tf_op jit(solution)/shard_map/ppermute | solution.py:73
  32.7 3.4 %copy-done.1 = bf16[4,2,2,512,512]{4,3,2,1,0:T(8,128)(2,1)S(1)} copy-done((bf16[4,2,2,512,512]{4,3,2,1,0:T(8,128)(2,1)S(1)}, bf16[4,2,2,512,512]{4,3,2,1,0:T(8,128)(2,1)}, u32[]{:S(2)}) %copy-start.1) | copy-done | bytes 8388632
  36.1 2.5 %project.3.refs_0_ = f32[2,512,512]{2,1,0:T(8,128)S(1)} custom-call(bf16[512,512]{1,0:T(8,128)(2,1)S(1)} %bitcast.70, bf16[512,512]{1,0:T(8,128)(2,1)S(1)} %collective-permute-done.refs_1_, bf16[4,2,2,512,512]{4,3,2,1,0:T(8,128)(2,1)S(1)} %copy-done.1), custom_call_target="tpu_custom_call" | custom-call | bytes 65536 | tf_op jit(solution)/shard_map/project/pallas_call | solution.py:133
  38.8 5.5 %collective-permute-done.2.refs_1_ = bf16[512,512]{1,0:T(8,128)(2,1)S(1)} collective-permute-done((bf16[512,512]{1,0:T(8,128)(2,1)S(1)}, bf16[512,512]{1,0:T(8,128)(2,1)S(1)}, u32[]{:S(2)}, u32[]{:S(2)}) %collective-permute-start.2) | collective-permute-done | bytes 524320 | tf_op jit(solution)/shard_map/ppermute | solution.py:73
  51.5 2.3 %collective-permute-start.11 = (bf16[2,256,512]{2,1,0:T(8,128)(2,1)S(1)}, bf16[2,256,512]{2,1,0:T(8,128)(2,1)S(1)}, u32[]{:S(2)}, u32[]{:S(2)}) collective-permute-start(bf16[2,256,512]{2,1,0:T(8,128)(2,1)S(1)} %pad_maximum_fusion.3), channel_id=1, source_target_pairs={{0,2},{1,3},{2,0},{3,1},{4,6},{5,7},{6,4},{7,5},{8,10},{9,11},{10,... | collective-permute-start | bytes 1572872 | tf_op jit(solution)/shard_map/ppermute | solution.py:65
  54.5 2.7 %project.4.refs_0_ = f32[2,512,512]{2,1,0:T(8,128)S(1)} custom-call(f32[2,512,512]{2,1,0:T(8,128)S(1)} %project.3.refs_0_, bf16[512,512]{1,0:T(8,128)(2,1)S(1)} %collective-permute-done.1.refs_1_, bf16[512,512]{1,0:T(8,128)(2,1)S(1)} %collective-permute-done.4.refs_2_, bf16[4,2,2,512,512]{4,3,2,1,0:T(8,128)(2,1)S(1)} %copy-done.1), custom_call_target="tpu_custom_call" | custom-call | bytes 65536 | tf_op jit(solution)/shard_map/project/pallas_call | solution.py:133
  57.3 4.2 %project.5.pair_ref = bf16[2,512,512]{2,1,0:T(8,128)(2,1)S(1)} custom-call(f32[2,512,512]{2,1,0:T(8,128)S(1)} %project.4.refs_0_, bf16[512,512]{1,0:T(8,128)(2,1)S(1)} %collective-permute-done.2.refs_1_, bf16[512,512]{1,0:T(8,128)(2,1)S(1)} %collective-permute-done.5.refs_2_, bf16[512,512]{1,0:T(8,128)(2,1)S(1)} %collective-permute-done.3.refs_3_, ...), custom_call_target="tpu_custom_call" | custom-call | bytes 65536 | tf_op jit(solution)/shard_map/project/pallas_call | solution.py:133
  61.5 10.9 %attend.1 = (bf16[512,512]{1,0:T(8,128)(2,1)}, bf16[2,512,512]{2,1,0:T(8,128)(2,1)}, bf16[2,512,512]{2,1,0:T(8,128)(2,1)S(1)}) custom-call(s32[1]{0:T(128)S(6)} %copy.28.length_ref, bf16[512,512]{1,0:T(8,128)(2,1)S(1)} %bitcast.75, bf16[512,512]{1,0:T(8,128)(2,1)S(1)} %bitcast.76, bf16[2,512,512]{2,1,0:T(8,128)(2,1)S(1)} %project.5.pair_ref), custom_call_target="tpu_custom_call" | custom-call | bytes 65536 | tf_op jit(solution)/shard_map/attend/pallas_call | solution.py:179
  76.1 5.0 %collective-permute-start.17 = (bf16[2,512,512]{2,1,0:T(8,128)(2,1)}, bf16[2,512,512]{2,1,0:T(8,128)(2,1)S(1)}, u32[]{:S(2)}, u32[]{:S(2)}) collective-permute-start(bf16[2,512,512]{2,1,0:T(8,128)(2,1)} %get-tuple-element.45.g0), channel_id=1, source_target_pairs={{0,3},{1,0},{2,1},{3,2},{4,7},{5,4},{6,5},{7,6},{8,11},{9,8},{10,9... | collective-permute-start | bytes 3145736 | tf_op jit(solution)/shard_map/ppermute | solution.py:65
  83.4 1.9 %collective-permute-start.10 = (bf16[512,512]{1,0:T(8,128)(2,1)S(1)}, bf16[512,512]{1,0:T(8,128)(2,1)}, u32[]{:S(2)}, u32[]{:S(2)}) collective-permute-start(bf16[512,512]{1,0:T(8,128)(2,1)S(1)} %get-tuple-element.37), channel_id=1, source_target_pairs={{0,16},{4,116},{8,24},{12,124},{16,0},{20,36},{24,8},{28,44},{32,4... | collective-permute-start | bytes 1572872 | tf_op jit(solution)/shard_map/ppermute | solution.py:73
  85.3 2.5 %memory_pieces.7 = (bf16[512,512]{1,0:T(8,128)(2,1)}, bf16[512,512]{1,0:T(8,128)(2,1)}) custom-call(bf16[4,2,2,512,512]{4,3,2,1,0:T(8,128)(2,1)S(1)} %bitcast.64, bf16[2,512,512]{2,1,0:T(8,128)(2,1)S(1)} %get-tuple-element.35.turned_ref, bf16[2,512,512]{2,1,0:T(8,128)(2,1)S(1)} %collective-permute-done.12.sent_ref), custom_call_target="tpu_custom_call" | custom-call | bytes 65536 | tf_op jit(solution)/shard_map/memory_pieces/pallas_call | solution.py:217
  94.2 8.7 %collective-permute-done.13 = bf16[512,512]{1,0:T(8,128)(2,1)} collective-permute-done((bf16[512,512]{1,0:T(8,128)(2,1)}, bf16[512,512]{1,0:T(8,128)(2,1)}, u32[]{:S(2)}, u32[]{:S(2)}) %collective-permute-start.13) | collective-permute-done | bytes 524320 | tf_op jit(solution)/shard_map/ppermute | solution.py:73
  102.9 2.4 %add_convert_fusion = bf16[512,512]{1,0:T(8,128)(2,1)} fusion(bf16[512,512]{1,0:T(8,128)(2,1)} %collective-permute-done.14, bf16[512,512]{1,0:T(8,128)(2,1)} %collective-permute-done.13, bf16[512,512]{1,0:T(8,128)(2,1)} %collective-permute-done.10, bf16[512,512]{1,0:T(8,128)(2,1)S(1)} %copy-done.20), kind=kLoop, calls=%fused_computation.1 | loop fusion | flops 2097152 | bytes 2621440 | tf_op jit(solution)/shard_map/convert_element_type | solution.py:337
  105.3 6.6 %all-to-all-start.1 = ((bf16[8,64,512]{2,1,0:T(8,128)(2,1)}), bf16[8,64,512]{2,1,0:T(8,128)(2,1)}, u32[]{:S(2)}, u32[]{:S(2)}) async-start(bf16[8,64,512]{2,1,0:T(8,128)(2,1)} %bitcast.78), calls=%async_computation.1 | async-start | bytes 1048576 | tf_op jit(solution)/shard_map/all_to_all | solution.py:60
  112.1 3.5 %collective-permute-start.19 = (bf16[512,512]{1,0:T(8,128)(2,1)S(1)}, bf16[512,512]{1,0:T(8,128)(2,1)S(1)}, u32[]{:S(2)}, u32[]{:S(2)}) collective-permute-start(bf16[512,512]{1,0:T(8,128)(2,1)S(1)} %slice_bitcast_fusion), channel_id=1, source_target_pairs={{0,3},{1,0},{2,1},{3,2},{4,7},{5,4},{6,5},{7,6},{8,11},{9,8},{10,9... | collective-permute-start | bytes 1572872 | tf_op jit(solution)/shard_map/ppermute | solution.py:65
  118.1 6.2 %weight_sums.1.sums = f32[4,2,256,512]{3,2,1,0:T(8,128)S(1)} custom-call(s32[3]{0:T(128)S(1)} %pad_add_fusion.at_ref, bf16[2,256,512]{2,1,0:T(8,128)(2,1)S(1)} %pad_maximum_fusion.4.mine, bf16[2,256,512]{2,1,0:T(8,128)(2,1)S(1)} %pad_maximum_fusion.5.other, bf16[2,256,512]{2,1,0:T(8,128)(2,1)S(1)} %copy-done.6, bf16[2,256,512]{2,1,0:T(8,128)(2,1)S(1)} %copy-done.10, ...), custom_call_target="tpu_custom_call" | custom-call | bytes 65536 | tf_op jit(solution)/shard_map/weight_sums/pallas_call | solution.py:259
  124.3 2.5 %collective-permute-done.19.value = bf16[512,512]{1,0:T(8,128)(2,1)S(1)} collective-permute-done((bf16[512,512]{1,0:T(8,128)(2,1)S(1)}, bf16[512,512]{1,0:T(8,128)(2,1)S(1)}, u32[]{:S(2)}, u32[]{:S(2)}) %collective-permute-start.19) | collective-permute-done | bytes 524320 | tf_op jit(solution)/shard_map/ppermute | solution.py:65
  126.8 4.6 %collective-permute-done.18.key = bf16[512,512]{1,0:T(8,128)(2,1)S(1)} collective-permute-done((bf16[512,512]{1,0:T(8,128)(2,1)S(1)}, bf16[512,512]{1,0:T(8,128)(2,1)S(1)}, u32[]{:S(2)}, u32[]{:S(2)}) %collective-permute-start.18) | collective-permute-done | bytes 524320 | tf_op jit(solution)/shard_map/ppermute | solution.py:65
  131.4 4.6 %weight_rows.1 = bf16[2,2,2,2,64,2,512]{6,5,4,3,2,1,0:T(2,128)(2,1)} custom-call(s32[3]{0:T(128)S(1)} %pad_add_fusion.at_ref, bf16[2,256,512]{2,1,0:T(8,128)(2,1)S(1)} %copy-done.8, bf16[3,2,256,512]{3,2,1,0:T(8,128)(2,1)S(1)} %collective-permute-done.15.swapped, bf16[512,512]{1,0:T(8,128)(2,1)S(1)} %collective-permute-done.18.key, ...), custom_call_target="tpu_custom_call" | custom-call | bytes 65536 | tf_op jit(solution)/shard_map/weight_rows/pallas_call | solution.py:277
  (102 shorter events, 26.8 us)
Async XLA Ops:
  2.3 25.7 %all-to-all-start = ((bf16[8,64,512]{2,1,0:T(8,128)(2,1)}), bf16[8,64,512]{2,1,0:T(8,128)(2,1)S(1)}, u32[]{:S(2)}, u32[]{:S(2)}) async-start(bf16[8,64,512]{2,1,0:T(8,128)(2,1)} %broadcast_in_dim.12), calls=%async_computation | async-start | bytes 1048576 | tf_op jit(solution)/shard_map/all_to_all | solution.py:56
  28.0 4.7 %collective-permute-start = (bf16[512,512]{1,0:T(8,128)(2,1)S(1)}, bf16[512,512]{1,0:T(8,128)(2,1)S(1)}, u32[]{:S(2)}, u32[]{:S(2)}) collective-permute-start(bf16[512,512]{1,0:T(8,128)(2,1)S(1)} %bitcast.66), channel_id=1, source_target_pairs={{0,4},{4,0},{8,12},{12,8},{16,20},{20,16},{24,28},{28,24},{32,36},... | collective-permute-start | bytes 1572872 | tf_op jit(solution)/shard_map/ppermute | solution.py:69
  28.0 10.8 %collective-permute-start.3 = (bf16[512,512]{1,0:T(8,128)(2,1)S(1)}, bf16[512,512]{1,0:T(8,128)(2,1)S(1)}, u32[]{:S(2)}, u32[]{:S(2)}) collective-permute-start(bf16[512,512]{1,0:T(8,128)(2,1)S(1)} %bitcast.67), channel_id=1, source_target_pairs={{0,144},{4,252},{8,152},{12,244},{16,128},{20,172},{24,136},{28,16... | collective-permute-start | bytes 1572872 | tf_op jit(solution)/shard_map/ppermute | solution.py:73
  31.5 12.8 %collective-permute-start.2 = (bf16[512,512]{1,0:T(8,128)(2,1)S(1)}, bf16[512,512]{1,0:T(8,128)(2,1)S(1)}, u32[]{:S(2)}, u32[]{:S(2)}) collective-permute-start(bf16[512,512]{1,0:T(8,128)(2,1)S(1)} %bitcast.68), channel_id=1, source_target_pairs={{0,128},{4,140},{8,136},{12,132},{16,144},{20,156},{24,152},{28,14... | collective-permute-start | bytes 1572872 | tf_op jit(solution)/shard_map/ppermute | solution.py:73
  32.7 11.6 %collective-permute-start.1 = (bf16[512,512]{1,0:T(8,128)(2,1)S(1)}, bf16[512,512]{1,0:T(8,128)(2,1)S(1)}, u32[]{:S(2)}, u32[]{:S(2)}) collective-permute-start(bf16[512,512]{1,0:T(8,128)(2,1)S(1)} %bitcast.69), channel_id=1, source_target_pairs={{0,16},{4,116},{8,24},{12,124},{16,0},{20,36},{24,8},{28,44},{32,4... | collective-permute-start | bytes 1572872 | tf_op jit(solution)/shard_map/ppermute | solution.py:73
  44.3 7.2 %collective-permute-start.4 = (bf16[512,512]{1,0:T(8,128)(2,1)S(1)}, bf16[512,512]{1,0:T(8,128)(2,1)S(1)}, u32[]{:S(2)}, u32[]{:S(2)}) collective-permute-start(bf16[512,512]{1,0:T(8,128)(2,1)S(1)} %collective-permute-done.1.refs_1_), channel_id=1, source_target_pairs={{0,4},{4,0},{8,12},{12,8},{16,20},{20,16},{24,28},{28,24},{32,36},... | collective-permute-start | bytes 1572872 | tf_op jit(solution)/shard_map/ppermute | solution.py:69
  46.0 11.3 %collective-permute-start.5 = (bf16[512,512]{1,0:T(8,128)(2,1)S(1)}, bf16[512,512]{1,0:T(8,128)(2,1)S(1)}, u32[]{:S(2)}, u32[]{:S(2)}) collective-permute-start(bf16[512,512]{1,0:T(8,128)(2,1)S(1)} %collective-permute-done.2.refs_1_), channel_id=1, source_target_pairs={{0,4},{4,0},{8,12},{12,8},{16,20},{20,16},{24,28},{28,24},{32,36},... | collective-permute-start | bytes 1572872 | tf_op jit(solution)/shard_map/ppermute | solution.py:69
  46.0 11.3 %collective-permute-start.6 = (bf16[512,512]{1,0:T(8,128)(2,1)S(1)}, bf16[512,512]{1,0:T(8,128)(2,1)S(1)}, u32[]{:S(2)}, u32[]{:S(2)}) collective-permute-start(bf16[512,512]{1,0:T(8,128)(2,1)S(1)} %collective-permute-done.3.refs_3_), channel_id=1, source_target_pairs={{0,4},{4,0},{8,12},{12,8},{16,20},{20,16},{24,28},{28,24},{32,36},... | collective-permute-start | bytes 1572872 | tf_op jit(solution)/shard_map/ppermute | solution.py:69
  48.0 24.5 %collective-permute-start.7 = (bf16[2,256,512]{2,1,0:T(8,128)(2,1)S(1)}, bf16[2,256,512]{2,1,0:T(8,128)(2,1)S(1)}, u32[]{:S(2)}, u32[]{:S(2)}) collective-permute-start(bf16[2,256,512]{2,1,0:T(8,128)(2,1)S(1)} %pad_maximum_fusion.1), channel_id=1, source_target_pairs={{0,1},{1,2},{2,3},{3,0},{4,5},{5,6},{6,7},{7,4},{8,9},{9,10},{10,1... | collective-permute-start | bytes 1572872 | tf_op jit(solution)/shard_map/ppermute | solution.py:65
  49.7 22.8 %collective-permute-start.8 = (bf16[2,256,512]{2,1,0:T(8,128)(2,1)S(1)}, bf16[2,256,512]{2,1,0:T(8,128)(2,1)S(1)}, u32[]{:S(2)}, u32[]{:S(2)}) collective-permute-start(bf16[2,256,512]{2,1,0:T(8,128)(2,1)S(1)} %pad_maximum_fusion.2), channel_id=1, source_target_pairs={{0,3},{1,0},{2,1},{3,2},{4,7},{5,4},{6,5},{7,6},{8,11},{9,8},{10,9... | collective-permute-start | bytes 1572872 | tf_op jit(solution)/shard_map/ppermute | solution.py:65
  51.5 24.0 %collective-permute-start.11 = (bf16[2,256,512]{2,1,0:T(8,128)(2,1)S(1)}, bf16[2,256,512]{2,1,0:T(8,128)(2,1)S(1)}, u32[]{:S(2)}, u32[]{:S(2)}) collective-permute-start(bf16[2,256,512]{2,1,0:T(8,128)(2,1)S(1)} %pad_maximum_fusion.3), channel_id=1, source_target_pairs={{0,2},{1,3},{2,0},{3,1},{4,6},{5,7},{6,4},{7,5},{8,10},{9,11},{10,... | collective-permute-start | bytes 1572872 | tf_op jit(solution)/shard_map/ppermute | solution.py:65
  72.4 18.9 %copy-start.5 = (bf16[2,256,512]{2,1,0:T(8,128)(2,1)}, bf16[2,256,512]{2,1,0:T(8,128)(2,1)S(1)}, u32[]{:S(2)}) copy-start(bf16[2,256,512]{2,1,0:T(8,128)(2,1)S(1)} %collective-permute-done.7.left) | copy-start | bytes 1572868
  72.4 18.9 %copy-start.9 = (bf16[2,256,512]{2,1,0:T(8,128)(2,1)}, bf16[2,256,512]{2,1,0:T(8,128)(2,1)S(1)}, u32[]{:S(2)}) copy-start(bf16[2,256,512]{2,1,0:T(8,128)(2,1)S(1)} %collective-permute-done.8.right) | copy-start | bytes 1572868
  73.9 7.2 %collective-permute-start.9 = (bf16[2,512,512]{2,1,0:T(8,128)(2,1)S(1)}, bf16[2,512,512]{2,1,0:T(8,128)(2,1)S(1)}, u32[]{:S(2)}, u32[]{:S(2)}) collective-permute-start(bf16[2,512,512]{2,1,0:T(8,128)(2,1)S(1)} %memory_pieces.4), channel_id=1, source_target_pairs={{0,4},{4,0},{8,12},{12,8},{16,20},{20,16},{24,28},{28,24},{32,36},... | collective-permute-start | bytes 3145736 | tf_op jit(solution)/shard_map/ppermute | solution.py:69
  75.6 9.7 %collective-permute-start.12 = (bf16[2,512,512]{2,1,0:T(8,128)(2,1)S(1)}, bf16[2,512,512]{2,1,0:T(8,128)(2,1)S(1)}, u32[]{:S(2)}, u32[]{:S(2)}) collective-permute-start(bf16[2,512,512]{2,1,0:T(8,128)(2,1)S(1)} %memory_pieces.6), channel_id=1, source_target_pairs={{0,4},{4,0},{8,12},{12,8},{16,20},{20,16},{24,28},{28,24},{32,36},... | collective-permute-start | bytes 3145736 | tf_op jit(solution)/shard_map/ppermute | solution.py:69
  76.1 35.9 %collective-permute-start.17 = (bf16[2,512,512]{2,1,0:T(8,128)(2,1)}, bf16[2,512,512]{2,1,0:T(8,128)(2,1)S(1)}, u32[]{:S(2)}, u32[]{:S(2)}) collective-permute-start(bf16[2,512,512]{2,1,0:T(8,128)(2,1)} %get-tuple-element.45.g0), channel_id=1, source_target_pairs={{0,3},{1,0},{2,1},{3,2},{4,7},{5,4},{6,5},{7,6},{8,11},{9,8},{10,9... | collective-permute-start | bytes 3145736 | tf_op jit(solution)/shard_map/ppermute | solution.py:65
  81.1 30.9 %collective-permute-start.16 = (bf16[2,512,512]{2,1,0:T(8,128)(2,1)}, bf16[2,512,512]{2,1,0:T(8,128)(2,1)}, u32[]{:S(2)}, u32[]{:S(2)}) collective-permute-start(bf16[2,512,512]{2,1,0:T(8,128)(2,1)} %get-tuple-element.45.g0), channel_id=1, source_target_pairs={{0,1},{1,2},{2,3},{3,0},{4,5},{5,6},{6,7},{7,4},{8,9},{9,10},{10,1... | collective-permute-start | bytes 3145736 | tf_op jit(solution)/shard_map/ppermute | solution.py:65
  83.4 9.3 %collective-permute-start.10 = (bf16[512,512]{1,0:T(8,128)(2,1)S(1)}, bf16[512,512]{1,0:T(8,128)(2,1)}, u32[]{:S(2)}, u32[]{:S(2)}) collective-permute-start(bf16[512,512]{1,0:T(8,128)(2,1)S(1)} %get-tuple-element.37), channel_id=1, source_target_pairs={{0,16},{4,116},{8,24},{12,124},{16,0},{20,36},{24,8},{28,44},{32,4... | collective-permute-start | bytes 1572872 | tf_op jit(solution)/shard_map/ppermute | solution.py:73
  87.8 15.1 %collective-permute-start.13 = (bf16[512,512]{1,0:T(8,128)(2,1)}, bf16[512,512]{1,0:T(8,128)(2,1)}, u32[]{:S(2)}, u32[]{:S(2)}) collective-permute-start(bf16[512,512]{1,0:T(8,128)(2,1)} %get-tuple-element.39), channel_id=1, source_target_pairs={{0,128},{4,140},{8,136},{12,132},{16,144},{20,156},{24,152},{28,14... | collective-permute-start | bytes 1572872 | tf_op jit(solution)/shard_map/ppermute | solution.py:73
  88.0 14.9 %collective-permute-start.14 = (bf16[512,512]{1,0:T(8,128)(2,1)}, bf16[512,512]{1,0:T(8,128)(2,1)}, u32[]{:S(2)}, u32[]{:S(2)}) collective-permute-start(bf16[512,512]{1,0:T(8,128)(2,1)} %get-tuple-element.40), channel_id=1, source_target_pairs={{0,144},{4,252},{8,152},{12,244},{16,128},{20,172},{24,136},{28,16... | collective-permute-start | bytes 1572872 | tf_op jit(solution)/shard_map/ppermute | solution.py:73
  92.7 24.4 %collective-permute-start.15 = (bf16[3,2,256,512]{3,2,1,0:T(8,128)(2,1)}, bf16[3,2,256,512]{3,2,1,0:T(8,128)(2,1)S(1)}, u32[]{:S(2)}, u32[]{:S(2)}) collective-permute-start(bf16[3,2,256,512]{3,2,1,0:T(8,128)(2,1)} %pad_maximum_fusion), channel_id=1, source_target_pairs={{0,4},{4,0},{8,12},{12,8},{16,20},{20,16},{24,28},{28,24},{32,36},... | collective-permute-start | bytes 4718600 | tf_op jit(solution)/shard_map/ppermute | solution.py:69
  105.3 30.7 %all-to-all-start.1 = ((bf16[8,64,512]{2,1,0:T(8,128)(2,1)}), bf16[8,64,512]{2,1,0:T(8,128)(2,1)}, u32[]{:S(2)}, u32[]{:S(2)}) async-start(bf16[8,64,512]{2,1,0:T(8,128)(2,1)} %bitcast.78), calls=%async_computation.1 | async-start | bytes 1048576 | tf_op jit(solution)/shard_map/all_to_all | solution.py:60
  112.1 14.8 %collective-permute-start.19 = (bf16[512,512]{1,0:T(8,128)(2,1)S(1)}, bf16[512,512]{1,0:T(8,128)(2,1)S(1)}, u32[]{:S(2)}, u32[]{:S(2)}) collective-permute-start(bf16[512,512]{1,0:T(8,128)(2,1)S(1)} %slice_bitcast_fusion), channel_id=1, source_target_pairs={{0,3},{1,0},{2,1},{3,2},{4,7},{5,4},{6,5},{7,6},{8,11},{9,8},{10,9... | collective-permute-start | bytes 1572872 | tf_op jit(solution)/shard_map/ppermute | solution.py:65
  116.7 14.7 %collective-permute-start.18 = (bf16[512,512]{1,0:T(8,128)(2,1)S(1)}, bf16[512,512]{1,0:T(8,128)(2,1)S(1)}, u32[]{:S(2)}, u32[]{:S(2)}) collective-permute-start(bf16[512,512]{1,0:T(8,128)(2,1)S(1)} %slice_bitcast_fusion.1), channel_id=1, source_target_pairs={{0,1},{1,2},{2,3},{3,0},{4,5},{5,6},{6,7},{7,4},{8,9},{9,10},{10,1... | collective-permute-start | bytes 1572872 | tf_op jit(solution)/shard_map/ppermute | solution.py:65
  (21 other events, 132.5 us)

commit v3 on v2

--- a/solution.py
+++ b/solution.py
@@ -57,12 +57,15 @@
 
 
 def collect(blocks, groups):
-    parts = lax.all_to_all(blocks, PLANE, 0, 0, axis_index_groups=groups)
-    return jnp.sum(parts.astype(F32), axis=0).astype(BF16)
+    return lax.all_to_all(blocks, PLANE, 0, 0, axis_index_groups=groups)
 
 
 def along_dp(block, step):
-    return lax.ppermute(block, "dp", [(d, (d + step) % 4) for d in range(4)])
+    pairs = []
+    for tp in range(4):
+        for d in range(4):
+            pairs.append((tp * 4 + d, tp * 4 + (d + (-step if tp % 2 else step)) % 4))
+    return lax.ppermute(block, ("tp", "dp"), pairs)
 
 
 def swap(block):
@@ -230,18 +233,18 @@
     )(split, turned, *([] if sent is None else [sent]))
 
 
-def sum_kernel(at_ref, mine, other, left, right, swapped, g0, g1, g2, out_ref):
+def sum_kernel(at_ref, mine, other, behind, ahead, swapped, g0, g1, g2, out_ref):
     own = pl.program_id(0) < 2
-    pairs = ((mine[0], other[0]), (left[0], swapped[0, 0]), (right[0], swapped[1, 0]))
+    pairs = ((mine[0], other[0]), (behind[0], swapped[1, 0]), (ahead[0], swapped[0, 0]))
     rows = [jnp.where(own, here, there) for here, there in pairs]
     for kind in range(2):
         out_ref[0, kind] = sum(dot(a, b[kind], NN) for a, b in zip(rows, (g0, g1, g2)))
 
 
-def last_kernel(at_ref, across, swapped, key, value, sums, out_ref):
+def last_kernel(at_ref, across, swapped, grads, sums, out_ref):
     rows = jnp.where(pl.program_id(0) < 2, across[0], swapped[0, 0])
-    for_key = sums[0, 0] + dot(rows, key[...], NN)
-    for_value = sums[0, 1] + dot(rows, value[...], NN)
+    for_key = sums[0, 0] + dot(rows, grads[0], NN)
+    for_value = sums[0, 1] + dot(rows, grads[1], NN)
     both = jnp.stack([for_key.astype(BF16), for_value.astype(BF16)], axis=0)
     both = jnp.swapaxes(both, 0, 1).reshape(2, 2, 64, 2, 512)
     out_ref[...] = jnp.swapaxes(both, 0, 1).reshape(2, 1, 2, 1, 64, 2, 512)
@@ -255,7 +258,7 @@
     return pl.BlockSpec(shape, lambda i, at: (0,) * len(shape))
 
 
-def weight_sums(at, mine, other, left, right, swapped, grads):
+def weight_sums(at, mine, other, behind, ahead, swapped, grads):
     return pl.pallas_call(
         sum_kernel,
         grid_spec=pltpu.PrefetchScalarGridSpec(
@@ -270,17 +273,17 @@
         compiler_params=pltpu.CompilerParams(vmem_limit_bytes=VMEM),
         cost_estimate=COST,
         name="weight_sums",
-    )(at, mine, other, left, right, swapped, *grads)
-
-
-def weight_rows(at, across, swapped, key, value, sums):
+    )(at, mine, other, behind, ahead, swapped, *grads)
+
+
+def weight_rows(at, across, swapped, grads, sums):
     out = pl.pallas_call(
         last_kernel,
         grid_spec=pltpu.PrefetchScalarGridSpec(
             num_scalar_prefetch=1,
             grid=(4,),
             in_specs=[HALF, pl.BlockSpec((1, 1, 256, 512), lambda i, at: (2, i % 2, 0, 0))]
-            + [whole((512, 512)), whole((512, 512)), SUMS],
+            + [whole((2, 512, 512)), SUMS],
             out_specs=pl.BlockSpec(
                 (2, 1, 2, 1, 64, 2, 512), lambda i, at: (0, at[1] ^ (i % 2), 0, at[2] ^ (i // 2), 0, 0, 0)
             ),
@@ -289,7 +292,7 @@
         compiler_params=pltpu.CompilerParams(vmem_limit_bytes=VMEM),
         cost_estimate=COST,
         name="weight_rows",
-    )(at, across, swapped, key, value, sums)
+    )(at, across, swapped, grads, sums)
     return out.reshape(1, 1024, 2, 512)
 
 
@@ -318,14 +321,15 @@
             rows.append(lax.dynamic_slice(piece, (0, d % 2, 0, 0), (2, 1, 128, 512)).reshape(256, 512))
         return jnp.stack(rows)
 
-    arrived = [along_dp(block_of(mine, (dp + step) % 4), step) for step in (1, 3, 2)]
+    way = 1 - 2 * at[2]
+    arrived = [along_dp(block_of(mine, (dp + 4 + way * step) % 4), step) for step in (1, -1, 2)]
 
     query_grad, grads, turned = attend(lengths, queries[0, 0], out_grad[0, 0], pair)
-    left, right, across = arrived
-    grads, turned, left, right = lax.optimization_barrier((grads, turned, left, right))
-
-    from_left = along_dp(grads, 1)
-    from_right = along_dp(grads, 3)
+    behind, ahead, across = arrived
+    grads, turned, behind, ahead = lax.optimization_barrier((grads, turned, behind, ahead))
+
+    from_behind = along_dp(grads, 1)
+    from_ahead = along_dp(grads, -1)
     for_other, across = lax.optimization_barrier((memory_pieces(split, turned, 3), across))
     sent_far = swap(for_other)
     sent_near = swap(memory_pieces(split, turned, 1))
@@ -335,16 +339,17 @@
     from_z = near(close_z, 0, 1)
     terms = (close, from_z, from_x, from_diagonal)
     quarter = sum(term.astype(F32) for term in terms).astype(BF16)
-    _, from_left, from_right = lax.optimization_barrier((quarter, from_left, from_right))
-    across_key = along_dp(from_left[0], 1)
-    across_value = along_dp(from_right[1], 3)
-    memory_grad = collect(quarter.reshape(8, 64, 512), FAR).T[:, None, :]
-
-    swapped = swap(jnp.stack([left, right, across]))
+    _, from_behind, from_ahead = lax.optimization_barrier((quarter, from_behind, from_ahead))
+    from_across = along_dp(from_behind, 1)
+    parts = collect(quarter.reshape(8, 64, 512), FAR)
+
+    swapped = swap(jnp.stack([behind, ahead, across]))
     rows, rows_other = block_of(mine, dp), block_of(other, dp)
-    sums = weight_sums(at, rows, rows_other, left, right, swapped, (grads, from_left, from_right))
-    sums, across_key, across_value = lax.optimization_barrier((sums, across_key, across_value))
-    weight_grad = weight_rows(at, across, swapped, across_key, across_value, sums)
+    sums = weight_sums(at, rows, rows_other, behind, ahead, swapped, (grads, from_behind, from_ahead))
+    sums, from_across = lax.optimization_barrier((sums, from_across))
+    weight_grad = weight_rows(at, across, swapped, from_across, sums)
+    parts, weight_grad = lax.optimization_barrier((parts, weight_grad))
+    memory_grad = jnp.sum(parts.astype(F32), axis=0).astype(BF16).T[:, None, :]
     return memory_grad, query_grad[None, None], weight_grad
 
 

time: 138 us -> 134 us (0.971)
  the two profiles are of different devices: /device:TPU:6 before, /device:TPU:33 now
where the time goes in v3:
time: 134 us
  Pallas kernels  42.8 us (32%)
  starting transfers between devices  40.1 us (30%)
  waiting for transfers between devices  25.6 us (19%)
  local copies, waits for them, and re-layouts  16.4 us (12%)
  other arithmetic  6.95 us (5%)
  between operations  1.76 us (1%)
    ppermute x6, waiting for transfers between devices, near(): return lax.ppermute(block, PLANE, NEAR[dx, dz])  14.2 us
    unnamed x38, local copies, waits for them, and re-layouts  12.5 us
    ppermute x6, starting transfers between devices, along_dp(): return lax.ppermute(block, ('tp', 'dp'), pairs)  11.8 us
    pallas_call x1, Pallas kernels, attend(): pl.pallas_call(attend_kernel, grid_spec=pltpu.PrefetchScalarGridSpec(num_...  10.7 us
    pallas_call x3, Pallas kernels, project(): pl.pallas_call(functools.partial(project_kernel, first, count), grid=(4,)...  10.5 us
    all_to_all x1, starting transfers between devices, spread(): return lax.all_to_all(copies, PLANE, 0, 0, axis_index_groups=groups)  9.75 us
    ppermute x6, starting transfers between devices, near(): return lax.ppermute(block, PLANE, NEAR[dx, dz])  7.89 us
    all_to_all x1, waiting for transfers between devices, spread(): return lax.all_to_all(copies, PLANE, 0, 0, axis_index_groups=groups)  6.98 us
  transfers between devices with their start and end apart: 21, of which 7 were waited for; matrix products, arithmetic and copies ran while one was open for 6% of the time, Pallas kernels for 32%

profile of v3, /device:TPU:33, one launch (start us, length us, event | category | flops | bytes accessed | tf_op | source)
XLA Modules:
  0.0 133.6 jit_solution(12452859598314058130)
XLA Ops:
  2.3 9.7 %all-to-all-start = ((bf16[8,64,512]{2,1,0:T(8,128)(2,1)}), bf16[8,64,512]{2,1,0:T(8,128)(2,1)S(1)}, u32[]{:S(2)}, u32[]{:S(2)}) async-start(bf16[8,64,512]{2,1,0:T(8,128)(2,1)} %broadcast_in_dim.12), calls=%async_computation | async-start | bytes 1048576 | tf_op jit(solution)/shard_map/all_to_all | solution.py:56
  12.1 3.4 %copy-done.2 = bf16[1,4096,2,512]{3,2,1,0:T(2,128)(2,1)S(1)} copy-done((bf16[1,4096,2,512]{3,2,1,0:T(2,128)(2,1)S(1)}, bf16[1,4096,2,512]{3,2,1,0:T(2,128)(2,1)}, u32[]{:S(2)}) %copy-start.2) | copy-done | bytes 8388632
  15.5 3.9 %split_weights.1.refs_2_.refs_3_.refs_5_.weight_ref = bf16[4,2,2,512,512]{4,3,2,1,0:T(8,128)(2,1)S(1)} custom-call(s32[3]{0:T(128)S(1)} %pad_add_fusion.at_ref, bf16[2,4,2,2,2,64,2,512]{7,6,5,4,3,2,1,0:T(2,128)(2,1)S(1)} %bitcast.61), custom_call_target="tpu_custom_call" | custom-call | bytes 65536 | tf_op jit(solution)/shard_map/split_weights/pallas_call | solution.py:96
  19.5 3.3 %copy-done = bf16[4,2,2,512,512]{4,3,2,1,0:T(8,128)(2,1)} copy-done((bf16[4,2,2,512,512]{4,3,2,1,0:T(8,128)(2,1)}, bf16[4,2,2,512,512]{4,3,2,1,0:T(8,128)(2,1)S(1)}, u32[]{:S(2)}) %copy-start) | copy-done | bytes 8388632
  22.7 7.0 %all-to-all-done = bf16[8,64,512]{2,1,0:T(8,128)(2,1)S(1)} async-done(((bf16[8,64,512]{2,1,0:T(8,128)(2,1)}), bf16[8,64,512]{2,1,0:T(8,128)(2,1)S(1)}, u32[]{:S(2)}, u32[]{:S(2)}) %all-to-all-start) | async-done | bytes 524320 | tf_op jit(solution)/shard_map/all_to_all | solution.py:56
  29.7 2.7 %collective-permute-start = (bf16[512,512]{1,0:T(8,128)(2,1)S(1)}, bf16[512,512]{1,0:T(8,128)(2,1)S(1)}, u32[]{:S(2)}, u32[]{:S(2)}) collective-permute-start(bf16[512,512]{1,0:T(8,128)(2,1)S(1)} %bitcast.62), channel_id=1, source_target_pairs={{0,4},{4,0},{8,12},{12,8},{16,20},{20,16},{24,28},{28,24},{32,36},... | collective-permute-start | bytes 1572872 | tf_op jit(solution)/shard_map/ppermute | solution.py:72
  32.5 2.0 %collective-permute-start.2 = (bf16[512,512]{1,0:T(8,128)(2,1)S(1)}, bf16[512,512]{1,0:T(8,128)(2,1)S(1)}, u32[]{:S(2)}, u32[]{:S(2)}) collective-permute-start(bf16[512,512]{1,0:T(8,128)(2,1)S(1)} %bitcast.64), channel_id=1, source_target_pairs={{0,128},{4,140},{8,136},{12,132},{16,144},{20,156},{24,152},{28,14... | collective-permute-start | bytes 1572872 | tf_op jit(solution)/shard_map/ppermute | solution.py:76
  36.3 3.4 %copy-done.1 = bf16[4,2,2,512,512]{4,3,2,1,0:T(8,128)(2,1)S(1)} copy-done((bf16[4,2,2,512,512]{4,3,2,1,0:T(8,128)(2,1)S(1)}, bf16[4,2,2,512,512]{4,3,2,1,0:T(8,128)(2,1)}, u32[]{:S(2)}) %copy-start.1) | copy-done | bytes 8388632
  39.7 2.5 %project.3.refs_0_ = f32[2,512,512]{2,1,0:T(8,128)S(1)} custom-call(bf16[512,512]{1,0:T(8,128)(2,1)S(1)} %bitcast.66, bf16[512,512]{1,0:T(8,128)(2,1)S(1)} %collective-permute-done.refs_1_, bf16[4,2,2,512,512]{4,3,2,1,0:T(8,128)(2,1)S(1)} %copy-done.1), custom_call_target="tpu_custom_call" | custom-call | bytes 65536 | tf_op jit(solution)/shard_map/project/pallas_call | solution.py:136
  42.7 4.6 %collective-permute-done.2.refs_1_ = bf16[512,512]{1,0:T(8,128)(2,1)S(1)} collective-permute-done((bf16[512,512]{1,0:T(8,128)(2,1)S(1)}, bf16[512,512]{1,0:T(8,128)(2,1)S(1)}, u32[]{:S(2)}, u32[]{:S(2)}) %collective-permute-start.2) | collective-permute-done | bytes 524320 | tf_op jit(solution)/shard_map/ppermute | solution.py:76
  47.9 2.3 %broadcast_select_fusion.2 = (bf16[512,512]{1,0:T(8,128)(2,1)}, bf16[512,512]{1,0:T(8,128)(2,1)S(1)}, bf16[512,512]{1,0:T(8,128)(2,1)S(1)}, bf16[512,512]{1,0:T(...) fusion(bf16[512,512]{1,0:T(8,128)(2,1)} %collective-permute-don, ...), kind=kLoop, calls=%fused_computation.9 | loop fusion | flops 2097152 | bytes 6291460 | tf_op jit(solution)/shard_map/jit(_where)/select_n | solution.py:320
  50.5 2.8 %collective-permute-start.7 = (bf16[2,256,512]{2,1,0:T(8,128)(2,1)S(1)}, bf16[2,256,512]{2,1,0:T(8,128)(2,1)S(1)}, u32[]{:S(2)}, u32[]{:S(2)}) collective-permute-start(bf16[2,256,512]{2,1,0:T(8,128)(2,1)S(1)} %pad_maximum_fusion.1), channel_id=1, source_target_pairs={{0,1},{1,2},{2,3},{3,0},{4,7},{5,4},{6,5},{7,6},{8,9},{9,10},{10,1... | collective-permute-start | bytes 1572872 | tf_op jit(solution)/shard_map/ppermute | solution.py:68
  53.6 1.9 %collective-permute-start.11 = (bf16[2,256,512]{2,1,0:T(8,128)(2,1)S(1)}, bf16[2,256,512]{2,1,0:T(8,128)(2,1)S(1)}, u32[]{:S(2)}, u32[]{:S(2)}) collective-permute-start(bf16[2,256,512]{2,1,0:T(8,128)(2,1)S(1)} %pad_maximum_fusion.3), channel_id=1, source_target_pairs={{0,2},{1,3},{2,0},{3,1},{4,6},{5,7},{6,4},{7,5},{8,10},{9,11},{10,... | collective-permute-start | bytes 1572872 | tf_op jit(solution)/shard_map/ppermute | solution.py:68
  56.1 3.8 %project.4.refs_0_ = f32[2,512,512]{2,1,0:T(8,128)S(1)} custom-call(f32[2,512,512]{2,1,0:T(8,128)S(1)} %project.3.refs_0_, bf16[512,512]{1,0:T(8,128)(2,1)} %collective-permute-done.1.refs_1_, bf16[512,512]{1,0:T(8,128)(2,1)S(1)} %collective-permute-done.4.refs_2_, bf16[4,2,2,512,512]{4,3,2,1,0:T(8,128)(2,1)S(1)} %copy-done.1), custom_call_target="tpu_custom_call" | custom-call | bytes 65536 | tf_op jit(solution)/shard_map/project/pallas_call | solution.py:136
  60.1 4.2 %project.5.pair_ref = bf16[2,512,512]{2,1,0:T(8,128)(2,1)S(1)} custom-call(f32[2,512,512]{2,1,0:T(8,128)S(1)} %project.4.refs_0_, bf16[512,512]{1,0:T(8,128)(2,1)S(1)} %collective-permute-done.2.refs_1_, bf16[512,512]{1,0:T(8,128)(2,1)S(1)} %collective-permute-done.5.refs_2_, bf16[512,512]{1,0:T(8,128)(2,1)S(1)} %collective-permute-done.3.refs_3_, ...), custom_call_target="tpu_custom_call" | custom-call | bytes 65536 | tf_op jit(solution)/shard_map/project/pallas_call | solution.py:136
  64.3 10.7 %attend.1 = (bf16[512,512]{1,0:T(8,128)(2,1)}, bf16[2,512,512]{2,1,0:T(8,128)(2,1)S(1)}, bf16[2,512,512]{2,1,0:T(8,128)(2,1)S(1)}) custom-call(s32[1]{0:T(128)S(6)} %copy.28.length_ref, bf16[512,512]{1,0:T(8,128)(2,1)S(1)} %bitcast.71, bf16[512,512]{1,0:T(8,128)(2,1)S(1)} %bitcast.72, bf16[2,512,512]{2,1,0:T(8,128)(2,1)S(1)} %project.5.pair_ref), custom_call_target="tpu_custom_call" | custom-call | bytes 65536 | tf_op jit(solution)/shard_map/attend/pallas_call | solution.py:182
  80.2 3.1 %collective-permute-start.16 = (bf16[2,512,512]{2,1,0:T(8,128)(2,1)S(1)}, bf16[2,512,512]{2,1,0:T(8,128)(2,1)}, u32[]{:S(2)}, u32[]{:S(2)}) collective-permute-start(bf16[2,512,512]{2,1,0:T(8,128)(2,1)S(1)} %get-tuple-element.45.g0), channel_id=1, source_target_pairs={{0,1},{1,2},{2,3},{3,0},{4,7},{5,4},{6,5},{7,6},{8,9},{9,10},{10,1... | collective-permute-start | bytes 3145736 | tf_op jit(solution)/shard_map/ppermute | solution.py:68
  87.8 2.6 %collective-permute-start.14 = (bf16[512,512]{1,0:T(8,128)(2,1)S(1)}, bf16[512,512]{1,0:T(8,128)(2,1)S(1)}, u32[]{:S(2)}, u32[]{:S(2)}) collective-permute-start(bf16[512,512]{1,0:T(8,128)(2,1)S(1)} %get-tuple-element.41), channel_id=1, source_target_pairs={{0,144},{4,252},{8,152},{12,244},{16,128},{20,172},{24,136},{28,16... | collective-permute-start | bytes 1572872 | tf_op jit(solution)/shard_map/ppermute | solution.py:76
  94.8 7.5 %collective-permute-done.13 = bf16[512,512]{1,0:T(8,128)(2,1)S(1)} collective-permute-done((bf16[512,512]{1,0:T(8,128)(2,1)S(1)}, bf16[512,512]{1,0:T(8,128)(2,1)S(1)}, u32[]{:S(2)}, u32[]{:S(2)}) %collective-permute-start.13) | collective-permute-done | bytes 524320 | tf_op jit(solution)/shard_map/ppermute | solution.py:76
  105.6 3.4 %collective-permute-start.18 = (bf16[2,512,512]{2,1,0:T(8,128)(2,1)}, bf16[2,512,512]{2,1,0:T(8,128)(2,1)}, u32[]{:S(2)}, u32[]{:S(2)}) collective-permute-start(bf16[2,512,512]{2,1,0:T(8,128)(2,1)} %collective-permute-done.16.g1), channel_id=1, source_target_pairs={{0,1},{1,2},{2,3},{3,0},{4,7},{5,4},{6,5},{7,6},{8,9},{9,10},{10,1... | collective-permute-start | bytes 3145736 | tf_op jit(solution)/shard_map/ppermute | solution.py:68
  109.0 4.1 %all-to-all-start.1 = ((bf16[8,64,512]{2,1,0:T(8,128)(2,1)}), bf16[8,64,512]{2,1,0:T(8,128)(2,1)}, u32[]{:S(2)}, u32[]{:S(2)}) async-start(bf16[8,64,512]{2,1,0:T(8,128)(2,1)} %bitcast.74), calls=%async_computation.1 | async-start | bytes 1048576 | tf_op jit(solution)/shard_map/all_to_all | solution.py:60
  117.0 5.9 %weight_sums.1.sums = f32[4,2,256,512]{3,2,1,0:T(8,128)S(1)} custom-call(s32[3]{0:T(128)S(1)} %pad_add_fusion.at_ref, bf16[2,256,512]{2,1,0:T(8,128)(2,1)S(1)} %pad_maximum_fusion.4.mine, bf16[2,256,512]{2,1,0:T(8,128)(2,1)S(1)} %pad_maximum_fusion.5.other, bf16[2,256,512]{2,1,0:T(8,128)(2,1)S(1)} %collective-permute-done.7.behind, ...), custom_call_target="tpu_custom_call" | custom-call | bytes 65536 | tf_op jit(solution)/shard_map/weight_sums/pallas_call | solution.py:262
  123.0 5.8 %weight_rows.1 = bf16[2,2,2,2,64,2,512]{6,5,4,3,2,1,0:T(2,128)(2,1)} custom-call(s32[3]{0:T(128)S(1)} %pad_add_fusion.at_ref, bf16[2,256,512]{2,1,0:T(8,128)(2,1)S(1)} %copy-done.4, bf16[3,2,256,512]{3,2,1,0:T(8,128)(2,1)S(1)} %collective-permute-done.15.swapped, bf16[2,512,512]{2,1,0:T(8,128)(2,1)} %collective-permute-done.18.grads, ...), custom_call_target="tpu_custom_call" | custom-call | bytes 65536 | tf_op jit(solution)/shard_map/weight_rows/pallas_call | solution.py:280
  128.8 3.1 %all-to-all-done.1 = bf16[8,64,512]{2,1,0:T(8,128)(2,1)} async-done(((bf16[8,64,512]{2,1,0:T(8,128)(2,1)}), bf16[8,64,512]{2,1,0:T(8,128)(2,1)}, u32[]{:S(2)}, u32[]{:S(2)}) %all-to-all-start.1) | async-done | bytes 524320 | tf_op jit(solution)/shard_map/all_to_all | solution.py:60
  (90 shorter events, 27.9 us)
Async XLA Ops:
  2.3 27.4 %all-to-all-start = ((bf16[8,64,512]{2,1,0:T(8,128)(2,1)}), bf16[8,64,512]{2,1,0:T(8,128)(2,1)S(1)}, u32[]{:S(2)}, u32[]{:S(2)}) async-start(bf16[8,64,512]{2,1,0:T(8,128)(2,1)} %broadcast_in_dim.12), calls=%async_computation | async-start | bytes 1048576 | tf_op jit(solution)/shard_map/all_to_all | solution.py:56
  29.7 6.6 %collective-permute-start = (bf16[512,512]{1,0:T(8,128)(2,1)S(1)}, bf16[512,512]{1,0:T(8,128)(2,1)S(1)}, u32[]{:S(2)}, u32[]{:S(2)}) collective-permute-start(bf16[512,512]{1,0:T(8,128)(2,1)S(1)} %bitcast.62), channel_id=1, source_target_pairs={{0,4},{4,0},{8,12},{12,8},{16,20},{20,16},{24,28},{28,24},{32,36},... | collective-permute-start | bytes 1572872 | tf_op jit(solution)/shard_map/ppermute | solution.py:72
  32.5 10.2 %collective-permute-start.3 = (bf16[512,512]{1,0:T(8,128)(2,1)S(1)}, bf16[512,512]{1,0:T(8,128)(2,1)S(1)}, u32[]{:S(2)}, u32[]{:S(2)}) collective-permute-start(bf16[512,512]{1,0:T(8,128)(2,1)S(1)} %bitcast.63), channel_id=1, source_target_pairs={{0,144},{4,252},{8,152},{12,244},{16,128},{20,172},{24,136},{28,16... | collective-permute-start | bytes 1572872 | tf_op jit(solution)/shard_map/ppermute | solution.py:76
  32.5 14.9 %collective-permute-start.2 = (bf16[512,512]{1,0:T(8,128)(2,1)S(1)}, bf16[512,512]{1,0:T(8,128)(2,1)S(1)}, u32[]{:S(2)}, u32[]{:S(2)}) collective-permute-start(bf16[512,512]{1,0:T(8,128)(2,1)S(1)} %bitcast.64), channel_id=1, source_target_pairs={{0,128},{4,140},{8,136},{12,132},{16,144},{20,156},{24,152},{28,14... | collective-permute-start | bytes 1572872 | tf_op jit(solution)/shard_map/ppermute | solution.py:76
  34.5 12.8 %collective-permute-start.1 = (bf16[512,512]{1,0:T(8,128)(2,1)S(1)}, bf16[512,512]{1,0:T(8,128)(2,1)}, u32[]{:S(2)}, u32[]{:S(2)}) collective-permute-start(bf16[512,512]{1,0:T(8,128)(2,1)S(1)} %bitcast.65), channel_id=1, source_target_pairs={{0,16},{4,116},{8,24},{12,124},{16,0},{20,36},{24,8},{28,44},{32,4... | collective-permute-start | bytes 1572872 | tf_op jit(solution)/shard_map/ppermute | solution.py:76
  47.3 6.2 %collective-permute-start.4 = (bf16[512,512]{1,0:T(8,128)(2,1)}, bf16[512,512]{1,0:T(8,128)(2,1)S(1)}, u32[]{:S(2)}, u32[]{:S(2)}) collective-permute-start(bf16[512,512]{1,0:T(8,128)(2,1)} %collective-permute-done.1.refs_1_), channel_id=1, source_target_pairs={{0,4},{4,0},{8,12},{12,8},{16,20},{20,16},{24,28},{28,24},{32,36},... | collective-permute-start | bytes 1572872 | tf_op jit(solution)/shard_map/ppermute | solution.py:72
  47.4 12.6 %collective-permute-start.5 = (bf16[512,512]{1,0:T(8,128)(2,1)S(1)}, bf16[512,512]{1,0:T(8,128)(2,1)S(1)}, u32[]{:S(2)}, u32[]{:S(2)}) collective-permute-start(bf16[512,512]{1,0:T(8,128)(2,1)S(1)} %collective-permute-done.2.refs_1_), channel_id=1, source_target_pairs={{0,4},{4,0},{8,12},{12,8},{16,20},{20,16},{24,28},{28,24},{32,36},... | collective-permute-start | bytes 1572872 | tf_op jit(solution)/shard_map/ppermute | solution.py:72
  47.8 12.2 %collective-permute-start.6 = (bf16[512,512]{1,0:T(8,128)(2,1)S(1)}, bf16[512,512]{1,0:T(8,128)(2,1)S(1)}, u32[]{:S(2)}, u32[]{:S(2)}) collective-permute-start(bf16[512,512]{1,0:T(8,128)(2,1)S(1)} %collective-permute-done.3.refs_3_), channel_id=1, source_target_pairs={{0,4},{4,0},{8,12},{12,8},{16,20},{20,16},{24,28},{28,24},{32,36},... | collective-permute-start | bytes 1572872 | tf_op jit(solution)/shard_map/ppermute | solution.py:72
  50.5 24.5 %collective-permute-start.7 = (bf16[2,256,512]{2,1,0:T(8,128)(2,1)S(1)}, bf16[2,256,512]{2,1,0:T(8,128)(2,1)S(1)}, u32[]{:S(2)}, u32[]{:S(2)}) collective-permute-start(bf16[2,256,512]{2,1,0:T(8,128)(2,1)S(1)} %pad_maximum_fusion.1), channel_id=1, source_target_pairs={{0,1},{1,2},{2,3},{3,0},{4,7},{5,4},{6,5},{7,6},{8,9},{9,10},{10,1... | collective-permute-start | bytes 1572872 | tf_op jit(solution)/shard_map/ppermute | solution.py:68
  53.3 21.6 %collective-permute-start.8 = (bf16[2,256,512]{2,1,0:T(8,128)(2,1)S(1)}, bf16[2,256,512]{2,1,0:T(8,128)(2,1)S(1)}, u32[]{:S(2)}, u32[]{:S(2)}) collective-permute-start(bf16[2,256,512]{2,1,0:T(8,128)(2,1)S(1)} %pad_maximum_fusion.2), channel_id=1, source_target_pairs={{0,3},{1,0},{2,1},{3,2},{4,5},{5,6},{6,7},{7,4},{8,11},{9,8},{10,9... | collective-permute-start | bytes 1572872 | tf_op jit(solution)/shard_map/ppermute | solution.py:68
  53.6 26.0 %collective-permute-start.11 = (bf16[2,256,512]{2,1,0:T(8,128)(2,1)S(1)}, bf16[2,256,512]{2,1,0:T(8,128)(2,1)S(1)}, u32[]{:S(2)}, u32[]{:S(2)}) collective-permute-start(bf16[2,256,512]{2,1,0:T(8,128)(2,1)S(1)} %pad_maximum_fusion.3), channel_id=1, source_target_pairs={{0,2},{1,3},{2,0},{3,1},{4,6},{5,7},{6,4},{7,5},{8,10},{9,11},{10,... | collective-permute-start | bytes 1572872 | tf_op jit(solution)/shard_map/ppermute | solution.py:68
  56.1 18.9 %slice-start = ((s8[8388608]{0:T(1024)(128)(4,1)}), s8[4194304]{0:T(1024)(128)(4,1)S(1)}, s32[]{:S(2)}) async-start(s8[8388608]{0:T(1024)(128)(4,1)} %bitcast.59), calls=%async_computation.2 | async-start | bytes 8388608
  60.0 15.0 %slice-start.1 = ((s8[8388608]{0:T(1024)(128)(4,1)}), s8[4194304]{0:T(1024)(128)(4,1)S(1)}, s32[]{:S(2)}) async-start(s8[8388608]{0:T(1024)(128)(4,1)} %bitcast.59), calls=%async_computation.3 | async-start | bytes 8388608
  76.4 6.9 %collective-permute-start.9 = (bf16[2,512,512]{2,1,0:T(8,128)(2,1)S(1)}, bf16[2,512,512]{2,1,0:T(8,128)(2,1)S(1)}, u32[]{:S(2)}, u32[]{:S(2)}) collective-permute-start(bf16[2,512,512]{2,1,0:T(8,128)(2,1)S(1)} %memory_pieces.4), channel_id=1, source_target_pairs={{0,4},{4,0},{8,12},{12,8},{16,20},{20,16},{24,28},{28,24},{32,36},... | collective-permute-start | bytes 3145736 | tf_op jit(solution)/shard_map/ppermute | solution.py:72
  79.6 10.8 %copy-start.3 = (bf16[2,256,512]{2,1,0:T(8,128)(2,1)}, bf16[2,256,512]{2,1,0:T(8,128)(2,1)S(1)}, u32[]{:S(2)}) copy-start(bf16[2,256,512]{2,1,0:T(8,128)(2,1)S(1)} %collective-permute-done.11.across) | copy-start | bytes 1572868
  79.6 5.7 %collective-permute-start.12 = (bf16[2,512,512]{2,1,0:T(8,128)(2,1)S(1)}, bf16[2,512,512]{2,1,0:T(8,128)(2,1)S(1)}, u32[]{:S(2)}, u32[]{:S(2)}) collective-permute-start(bf16[2,512,512]{2,1,0:T(8,128)(2,1)S(1)} %memory_pieces.6), channel_id=1, source_target_pairs={{0,4},{4,0},{8,12},{12,8},{16,20},{20,16},{24,28},{28,24},{32,36},... | collective-permute-start | bytes 3145736 | tf_op jit(solution)/shard_map/ppermute | solution.py:72
  79.8 23.6 %collective-permute-start.17 = (bf16[2,512,512]{2,1,0:T(8,128)(2,1)S(1)}, bf16[2,512,512]{2,1,0:T(8,128)(2,1)S(1)}, u32[]{:S(2)}, u32[]{:S(2)}) collective-permute-start(bf16[2,512,512]{2,1,0:T(8,128)(2,1)S(1)} %get-tuple-element.45.g0), channel_id=1, source_target_pairs={{0,3},{1,0},{2,1},{3,2},{4,5},{5,6},{6,7},{7,4},{8,11},{9,8},{10,9... | collective-permute-start | bytes 3145736 | tf_op jit(solution)/shard_map/ppermute | solution.py:68
  80.2 25.4 %collective-permute-start.16 = (bf16[2,512,512]{2,1,0:T(8,128)(2,1)S(1)}, bf16[2,512,512]{2,1,0:T(8,128)(2,1)}, u32[]{:S(2)}, u32[]{:S(2)}) collective-permute-start(bf16[2,512,512]{2,1,0:T(8,128)(2,1)S(1)} %get-tuple-element.45.g0), channel_id=1, source_target_pairs={{0,1},{1,2},{2,3},{3,0},{4,7},{5,4},{6,5},{7,6},{8,9},{9,10},{10,1... | collective-permute-start | bytes 3145736 | tf_op jit(solution)/shard_map/ppermute | solution.py:68
  84.9 8.5 %collective-permute-start.10 = (bf16[512,512]{1,0:T(8,128)(2,1)S(1)}, bf16[512,512]{1,0:T(8,128)(2,1)S(1)}, u32[]{:S(2)}, u32[]{:S(2)}) collective-permute-start(bf16[512,512]{1,0:T(8,128)(2,1)S(1)} %get-tuple-element.38), channel_id=1, source_target_pairs={{0,16},{4,116},{8,24},{12,124},{16,0},{20,36},{24,8},{28,44},{32,4... | collective-permute-start | bytes 1572872 | tf_op jit(solution)/shard_map/ppermute | solution.py:76
  86.9 15.3 %collective-permute-start.13 = (bf16[512,512]{1,0:T(8,128)(2,1)S(1)}, bf16[512,512]{1,0:T(8,128)(2,1)S(1)}, u32[]{:S(2)}, u32[]{:S(2)}) collective-permute-start(bf16[512,512]{1,0:T(8,128)(2,1)S(1)} %get-tuple-element.40), channel_id=1, source_target_pairs={{0,128},{4,140},{8,136},{12,132},{16,144},{20,156},{24,152},{28,14... | collective-permute-start | bytes 1572872 | tf_op jit(solution)/shard_map/ppermute | solution.py:76
  87.8 14.4 %collective-permute-start.14 = (bf16[512,512]{1,0:T(8,128)(2,1)S(1)}, bf16[512,512]{1,0:T(8,128)(2,1)S(1)}, u32[]{:S(2)}, u32[]{:S(2)}) collective-permute-start(bf16[512,512]{1,0:T(8,128)(2,1)S(1)} %get-tuple-element.41), channel_id=1, source_target_pairs={{0,144},{4,252},{8,152},{12,244},{16,128},{20,172},{24,136},{28,16... | collective-permute-start | bytes 1572872 | tf_op jit(solution)/shard_map/ppermute | solution.py:76
  93.4 22.2 %collective-permute-start.15 = (bf16[3,2,256,512]{3,2,1,0:T(8,128)(2,1)}, bf16[3,2,256,512]{3,2,1,0:T(8,128)(2,1)S(1)}, u32[]{:S(2)}, u32[]{:S(2)}) collective-permute-start(bf16[3,2,256,512]{3,2,1,0:T(8,128)(2,1)} %pad_maximum_fusion), channel_id=1, source_target_pairs={{0,4},{4,0},{8,12},{12,8},{16,20},{20,16},{24,28},{28,24},{32,36},... | collective-permute-start | bytes 4718600 | tf_op jit(solution)/shard_map/ppermute | solution.py:72
  105.6 17.4 %collective-permute-start.18 = (bf16[2,512,512]{2,1,0:T(8,128)(2,1)}, bf16[2,512,512]{2,1,0:T(8,128)(2,1)}, u32[]{:S(2)}, u32[]{:S(2)}) collective-permute-start(bf16[2,512,512]{2,1,0:T(8,128)(2,1)} %collective-permute-done.16.g1), channel_id=1, source_target_pairs={{0,1},{1,2},{2,3},{3,0},{4,7},{5,4},{6,5},{7,6},{8,9},{9,10},{10,1... | collective-permute-start | bytes 3145736 | tf_op jit(solution)/shard_map/ppermute | solution.py:68
  109.0 22.9 %all-to-all-start.1 = ((bf16[8,64,512]{2,1,0:T(8,128)(2,1)}), bf16[8,64,512]{2,1,0:T(8,128)(2,1)}, u32[]{:S(2)}, u32[]{:S(2)}) async-start(bf16[8,64,512]{2,1,0:T(8,128)(2,1)} %bitcast.74), calls=%async_computation.1 | async-start | bytes 1048576 | tf_op jit(solution)/shard_map/all_to_all | solution.py:60
  (16 other events, 56.3 us)

commit v4 on v3

--- a/solution.py
+++ b/solution.py
@@ -326,11 +326,11 @@
 
     query_grad, grads, turned = attend(lengths, queries[0, 0], out_grad[0, 0], pair)
     behind, ahead, across = arrived
-    grads, turned, behind, ahead = lax.optimization_barrier((grads, turned, behind, ahead))
 
     from_behind = along_dp(grads, 1)
     from_ahead = along_dp(grads, -1)
-    for_other, across = lax.optimization_barrier((memory_pieces(split, turned, 3), across))
+    for_other = memory_pieces(split, turned, 3)
+    for_other, behind, ahead, across = lax.optimization_barrier((for_other, behind, ahead, across))
     sent_far = swap(for_other)
     sent_near = swap(memory_pieces(split, turned, 1))
     diagonal, far_x = memory_pieces(split, turned, 3, sent_far)

time: 134 us -> 137 us (1.022)
  starting transfers between devices: 40.1 us -> 38.1 us
  other arithmetic: 6.95 us -> 8.75 us
  Pallas kernels: 42.8 us -> 44.4 us
  waiting for transfers between devices: 25.6 us -> 27.2 us
    ppermute x7, starting transfers between devices: 6.59 us -> 4.43 us  [swap(): return lax.ppermute(block, PLANE, SWAP)]
    select_n x2 -> x4, other arithmetic: 2.49 us -> 4.27 us  [block_of(): jnp.where(moved == 0, pieces[dz], pieces[2 + dz]).reshape(2, 2, 128, 512)]
    pallas_call x3, Pallas kernels: 10.5 us -> 12.1 us  [project(): pl.pallas_call(functools.partial(project_kernel, first, count), grid=(4,)...]
  transfers between devices with their start and end apart: 21 -> 21, of which waited for: 7 -> 8; matrix products, arithmetic and copies ran while one was open for 6% -> 6% of each run, Pallas kernels for 32% -> 32%
where the time goes in v4:
time: 137 us
  Pallas kernels  44.4 us (32%)
  starting transfers between devices  38.1 us (28%)
  waiting for transfers between devices  27.2 us (20%)
  local copies, waits for them, and re-layouts  16.6 us (12%)
  other arithmetic  8.75 us (6%)
  between operations  1.67 us (1%)
    ppermute x6, waiting for transfers between devices, near(): return lax.ppermute(block, PLANE, NEAR[dx, dz])  15.3 us
    unnamed x38, local copies, waits for them, and re-layouts  13.6 us
    pallas_call x3, Pallas kernels, project(): pl.pallas_call(functools.partial(project_kernel, first, count), grid=(4,)...  12.1 us
    ppermute x6, starting transfers between devices, along_dp(): return lax.ppermute(block, ('tp', 'dp'), pairs)  11.9 us
    pallas_call x1, Pallas kernels, attend(): pl.pallas_call(attend_kernel, grid_spec=pltpu.PrefetchScalarGridSpec(num_...  10.7 us
    all_to_all x1, starting transfers between devices, spread(): return lax.all_to_all(copies, PLANE, 0, 0, axis_index_groups=groups)  9.75 us
    ppermute x6, starting transfers between devices, near(): return lax.ppermute(block, PLANE, NEAR[dx, dz])  7.89 us
    all_to_all x1, waiting for transfers between devices, spread(): return lax.all_to_all(copies, PLANE, 0, 0, axis_index_groups=groups)  6.96 us
  transfers between devices with their start and end apart: 21, of which 8 were waited for; matrix products, arithmetic and copies ran while one was open for 6% of the time, Pallas kernels for 32%

profile of v4, /device:TPU:33, one launch (start us, length us, event | category | flops | bytes accessed | tf_op | source)
XLA Modules:
  0.0 136.8 jit_solution(13963623533617788033)
XLA Ops:
  2.3 9.7 %all-to-all-start = ((bf16[8,64,512]{2,1,0:T(8,128)(2,1)}), bf16[8,64,512]{2,1,0:T(8,128)(2,1)S(1)}, u32[]{:S(2)}, u32[]{:S(2)}) async-start(bf16[8,64,512]{2,1,0:T(8,128)(2,1)} %broadcast_in_dim.12), calls=%async_computation | async-start | bytes 1048576 | tf_op jit(solution)/shard_map/all_to_all | solution.py:56
  12.1 3.4 %copy-done.2 = bf16[1,4096,2,512]{3,2,1,0:T(2,128)(2,1)S(1)} copy-done((bf16[1,4096,2,512]{3,2,1,0:T(2,128)(2,1)S(1)}, bf16[1,4096,2,512]{3,2,1,0:T(2,128)(2,1)}, u32[]{:S(2)}) %copy-start.2) | copy-done | bytes 8388632
  15.5 3.9 %split_weights.1.refs_2_.refs_3_.refs_5_.weight_ref = bf16[4,2,2,512,512]{4,3,2,1,0:T(8,128)(2,1)S(1)} custom-call(s32[3]{0:T(128)S(1)} %pad_add_fusion.at_ref, bf16[2,4,2,2,2,64,2,512]{7,6,5,4,3,2,1,0:T(2,128)(2,1)S(1)} %bitcast.61), custom_call_target="tpu_custom_call" | custom-call | bytes 65536 | tf_op jit(solution)/shard_map/split_weights/pallas_call | solution.py:96
  19.5 3.3 %copy-done = bf16[4,2,2,512,512]{4,3,2,1,0:T(8,128)(2,1)} copy-done((bf16[4,2,2,512,512]{4,3,2,1,0:T(8,128)(2,1)}, bf16[4,2,2,512,512]{4,3,2,1,0:T(8,128)(2,1)S(1)}, u32[]{:S(2)}) %copy-start) | copy-done | bytes 8388632
  22.8 7.0 %all-to-all-done = bf16[8,64,512]{2,1,0:T(8,128)(2,1)S(1)} async-done(((bf16[8,64,512]{2,1,0:T(8,128)(2,1)}), bf16[8,64,512]{2,1,0:T(8,128)(2,1)S(1)}, u32[]{:S(2)}, u32[]{:S(2)}) %all-to-all-start) | async-done | bytes 524320 | tf_op jit(solution)/shard_map/all_to_all | solution.py:56
  29.7 2.7 %collective-permute-start = (bf16[512,512]{1,0:T(8,128)(2,1)S(1)}, bf16[512,512]{1,0:T(8,128)(2,1)S(1)}, u32[]{:S(2)}, u32[]{:S(2)}) collective-permute-start(bf16[512,512]{1,0:T(8,128)(2,1)S(1)} %bitcast.62), channel_id=1, source_target_pairs={{0,4},{4,0},{8,12},{12,8},{16,20},{20,16},{24,28},{28,24},{32,36},... | collective-permute-start | bytes 1572872 | tf_op jit(solution)/shard_map/ppermute | solution.py:72
  32.5 2.0 %collective-permute-start.2 = (bf16[512,512]{1,0:T(8,128)(2,1)S(1)}, bf16[512,512]{1,0:T(8,128)(2,1)}, u32[]{:S(2)}, u32[]{:S(2)}) collective-permute-start(bf16[512,512]{1,0:T(8,128)(2,1)S(1)} %bitcast.64), channel_id=1, source_target_pairs={{0,128},{4,140},{8,136},{12,132},{16,144},{20,156},{24,152},{28,14... | collective-permute-start | bytes 1572872 | tf_op jit(solution)/shard_map/ppermute | solution.py:76
  36.3 3.4 %copy-done.1 = bf16[4,2,2,512,512]{4,3,2,1,0:T(8,128)(2,1)S(1)} copy-done((bf16[4,2,2,512,512]{4,3,2,1,0:T(8,128)(2,1)S(1)}, bf16[4,2,2,512,512]{4,3,2,1,0:T(8,128)(2,1)}, u32[]{:S(2)}) %copy-start.1) | copy-done | bytes 8388632
  39.7 2.5 %project.3.refs_0_ = f32[2,512,512]{2,1,0:T(8,128)S(1)} custom-call(bf16[512,512]{1,0:T(8,128)(2,1)S(1)} %bitcast.66, bf16[512,512]{1,0:T(8,128)(2,1)S(1)} %collective-permute-done.refs_1_, bf16[4,2,2,512,512]{4,3,2,1,0:T(8,128)(2,1)S(1)} %copy-done.1), custom_call_target="tpu_custom_call" | custom-call | bytes 65536 | tf_op jit(solution)/shard_map/project/pallas_call | solution.py:136
  42.8 4.6 %collective-permute-done.2.refs_1_ = bf16[512,512]{1,0:T(8,128)(2,1)} collective-permute-done((bf16[512,512]{1,0:T(8,128)(2,1)S(1)}, bf16[512,512]{1,0:T(8,128)(2,1)}, u32[]{:S(2)}, u32[]{:S(2)}) %collective-permute-start.2) | collective-permute-done | bytes 524320 | tf_op jit(solution)/shard_map/ppermute | solution.py:76
  47.9 2.1 %broadcast_select_fusion.2 = (bf16[512,512]{1,0:T(8,128)(2,1)}, bf16[512,512]{1,0:T(8,128)(2,1)S(1)}, bf16[512,512]{1,0:T(8,128)(2,1)S(1)}, bf16[512,512]{1,0:T(8,128)(2,1)S(1)}) fusion(bf16[512,512]{1,0:T(8,128)(2,1)} %collective-permute-done.1.refs_1_, bf16[512,512]{1,0:T(8,128)(2,1)} %collective-permute-done.3.refs_3_, pred[]{:T(512)S(6)} %eq.37, ...), kind=kLoop, calls=%fused_computation.9 | loop fusion | flops 1048576 | bytes 3145732 | tf_op jit(solution)/shard_map/jit(_where)/select_n | solution.py:320
  52.2 3.0 %collective-permute-start.11 = (bf16[2,256,512]{2,1,0:T(8,128)(2,1)S(1)}, bf16[2,256,512]{2,1,0:T(8,128)(2,1)S(1)}, u32[]{:S(2)}, u32[]{:S(2)}) collective-permute-start(bf16[2,256,512]{2,1,0:T(8,128)(2,1)S(1)} %pad_maximum_fusion.3), channel_id=1, source_target_pairs={{0,2},{1,3},{2,0},{3,1},{4,6},{5,7},{6,4},{7,5},{8,10},{9,11},{10,... | collective-permute-start | bytes 1572872 | tf_op jit(solution)/shard_map/ppermute | solution.py:68
  55.9 2.5 %collective-permute-start.9 = (bf16[2,256,512]{2,1,0:T(8,128)(2,1)S(1)}, bf16[2,256,512]{2,1,0:T(8,128)(2,1)S(1)}, u32[]{:S(2)}, u32[]{:S(2)}) collective-permute-start(bf16[2,256,512]{2,1,0:T(8,128)(2,1)S(1)} %pad_maximum_fusion.1), channel_id=1, source_target_pairs={{0,1},{1,2},{2,3},{3,0},{4,7},{5,4},{6,5},{7,6},{8,9},{9,10},{10,1... | collective-permute-start | bytes 1572872 | tf_op jit(solution)/shard_map/ppermute | solution.py:68
  59.1 3.8 %project.4.refs_0_ = f32[2,512,512]{2,1,0:T(8,128)S(1)} custom-call(f32[2,512,512]{2,1,0:T(8,128)S(1)} %project.3.refs_0_, bf16[512,512]{1,0:T(8,128)(2,1)} %collective-permute-done.1.refs_1_, bf16[512,512]{1,0:T(8,128)(2,1)S(1)} %collective-permute-done.4.refs_2_, bf16[4,2,2,512,512]{4,3,2,1,0:T(8,128)(2,1)S(1)} %copy-done.1), custom_call_target="tpu_custom_call" | custom-call | bytes 65536 | tf_op jit(solution)/shard_map/project/pallas_call | solution.py:136
  63.0 5.8 %project.5.pair_ref = bf16[2,512,512]{2,1,0:T(8,128)(2,1)S(1)} custom-call(f32[2,512,512]{2,1,0:T(8,128)S(1)} %project.4.refs_0_, bf16[512,512]{1,0:T(8,128)(2,1)} %collective-permute-done.2.refs_1_, bf16[512,512]{1,0:T(8,128)(2,1)S(1)} %collective-permute-done.5.refs_2_, bf16[512,512]{1,0:T(8,128)(2,1)} %collective-permute-done.3.refs_3_, ...), custom_call_target="tpu_custom_call" | custom-call | bytes 65536 | tf_op jit(solution)/shard_map/project/pallas_call | solution.py:136
  68.8 10.7 %attend.1 = (bf16[512,512]{1,0:T(8,128)(2,1)}, bf16[2,512,512]{2,1,0:T(8,128)(2,1)S(1)}, bf16[2,512,512]{2,1,0:T(8,128)(2,1)S(1)}) custom-call(s32[1]{0:T(128)S(6)} %copy.28.length_ref, bf16[512,512]{1,0:T(8,128)(2,1)S(1)} %bitcast.71, bf16[512,512]{1,0:T(8,128)(2,1)S(1)} %bitcast.72, bf16[2,512,512]{2,1,0:T(8,128)(2,1)S(1)} %project.5.pair_ref), custom_call_target="tpu_custom_call" | custom-call | bytes 65536 | tf_op jit(solution)/shard_map/attend/pallas_call | solution.py:182
  83.2 2.6 %collective-permute-start.16 = (bf16[2,512,512]{2,1,0:T(8,128)(2,1)S(1)}, bf16[2,512,512]{2,1,0:T(8,128)(2,1)}, u32[]{:S(2)}, u32[]{:S(2)}) collective-permute-start(bf16[2,512,512]{2,1,0:T(8,128)(2,1)S(1)} %get-tuple-element.41.g0), channel_id=1, source_target_pairs={{0,1},{1,2},{2,3},{3,0},{4,7},{5,4},{6,5},{7,6},{8,9},{9,10},{10,1... | collective-permute-start | bytes 3145736 | tf_op jit(solution)/shard_map/ppermute | solution.py:68
  90.3 2.6 %collective-permute-start.14 = (bf16[512,512]{1,0:T(8,128)(2,1)S(1)}, bf16[512,512]{1,0:T(8,128)(2,1)S(1)}, u32[]{:S(2)}, u32[]{:S(2)}) collective-permute-start(bf16[512,512]{1,0:T(8,128)(2,1)S(1)} %get-tuple-element.37), channel_id=1, source_target_pairs={{0,144},{4,252},{8,152},{12,244},{16,128},{20,172},{24,136},{28,16... | collective-permute-start | bytes 1572872 | tf_op jit(solution)/shard_map/ppermute | solution.py:76
  96.3 8.5 %collective-permute-done.13 = bf16[512,512]{1,0:T(8,128)(2,1)S(1)} collective-permute-done((bf16[512,512]{1,0:T(8,128)(2,1)S(1)}, bf16[512,512]{1,0:T(8,128)(2,1)S(1)}, u32[]{:S(2)}, u32[]{:S(2)}) %collective-permute-start.13) | collective-permute-done | bytes 524320 | tf_op jit(solution)/shard_map/ppermute | solution.py:76
  108.7 3.2 %collective-permute-start.18 = (bf16[2,512,512]{2,1,0:T(8,128)(2,1)}, bf16[2,512,512]{2,1,0:T(8,128)(2,1)}, u32[]{:S(2)}, u32[]{:S(2)}) collective-permute-start(bf16[2,512,512]{2,1,0:T(8,128)(2,1)} %collective-permute-done.16.g1), channel_id=1, source_target_pairs={{0,1},{1,2},{2,3},{3,0},{4,7},{5,4},{6,5},{7,6},{8,9},{9,10},{10,1... | collective-permute-start | bytes 3145736 | tf_op jit(solution)/shard_map/ppermute | solution.py:68
  112.0 4.1 %all-to-all-start.1 = ((bf16[8,64,512]{2,1,0:T(8,128)(2,1)}), bf16[8,64,512]{2,1,0:T(8,128)(2,1)}, u32[]{:S(2)}, u32[]{:S(2)}) async-start(bf16[8,64,512]{2,1,0:T(8,128)(2,1)} %bitcast.74), calls=%async_computation.1 | async-start | bytes 1048576 | tf_op jit(solution)/shard_map/all_to_all | solution.py:60
  120.2 5.9 %weight_sums.1.sums = f32[4,2,256,512]{3,2,1,0:T(8,128)S(1)} custom-call(s32[3]{0:T(128)S(1)} %pad_add_fusion.at_ref, bf16[2,256,512]{2,1,0:T(8,128)(2,1)S(1)} %pad_maximum_fusion.4.mine, bf16[2,256,512]{2,1,0:T(8,128)(2,1)S(1)} %pad_maximum_fusion.5.other, bf16[2,256,512]{2,1,0:T(8,128)(2,1)S(1)} %copy-done.4, ...), custom_call_target="tpu_custom_call" | custom-call | bytes 65536 | tf_op jit(solution)/shard_map/weight_sums/pallas_call | solution.py:262
  126.1 5.8 %weight_rows.1 = bf16[2,2,2,2,64,2,512]{6,5,4,3,2,1,0:T(2,128)(2,1)} custom-call(s32[3]{0:T(128)S(1)} %pad_add_fusion.at_ref, bf16[2,256,512]{2,1,0:T(8,128)(2,1)S(1)} %collective-permute-done.11.across, bf16[3,2,256,512]{3,2,1,0:T(8,128)(2,1)S(1)} %collective-permute-done.15.swapped, bf16[2,512,512]{2,1,0:T(8,128)(2,1)} %collective-permute-done.18.grads, ...), custom_call_target="tpu_custom_call" | custom-call | bytes 65536 | tf_op jit(solution)/shard_map/weight_rows/pallas_call | solution.py:280
  132.0 3.0 %all-to-all-done.1 = bf16[8,64,512]{2,1,0:T(8,128)(2,1)} async-done(((bf16[8,64,512]{2,1,0:T(8,128)(2,1)}), bf16[8,64,512]{2,1,0:T(8,128)(2,1)}, u32[]{:S(2)}, u32[]{:S(2)}) %all-to-all-start.1) | async-done | bytes 524320 | tf_op jit(solution)/shard_map/all_to_all | solution.py:60
  (87 shorter events, 28.7 us)
Async XLA Ops:
  2.3 27.4 %all-to-all-start = ((bf16[8,64,512]{2,1,0:T(8,128)(2,1)}), bf16[8,64,512]{2,1,0:T(8,128)(2,1)S(1)}, u32[]{:S(2)}, u32[]{:S(2)}) async-start(bf16[8,64,512]{2,1,0:T(8,128)(2,1)} %broadcast_in_dim.12), calls=%async_computation | async-start | bytes 1048576 | tf_op jit(solution)/shard_map/all_to_all | solution.py:56
  29.7 6.6 %collective-permute-start = (bf16[512,512]{1,0:T(8,128)(2,1)S(1)}, bf16[512,512]{1,0:T(8,128)(2,1)S(1)}, u32[]{:S(2)}, u32[]{:S(2)}) collective-permute-start(bf16[512,512]{1,0:T(8,128)(2,1)S(1)} %bitcast.62), channel_id=1, source_target_pairs={{0,4},{4,0},{8,12},{12,8},{16,20},{20,16},{24,28},{28,24},{32,36},... | collective-permute-start | bytes 1572872 | tf_op jit(solution)/shard_map/ppermute | solution.py:72
  32.5 10.4 %collective-permute-start.3 = (bf16[512,512]{1,0:T(8,128)(2,1)S(1)}, bf16[512,512]{1,0:T(8,128)(2,1)}, u32[]{:S(2)}, u32[]{:S(2)}) collective-permute-start(bf16[512,512]{1,0:T(8,128)(2,1)S(1)} %bitcast.63), channel_id=1, source_target_pairs={{0,144},{4,252},{8,152},{12,244},{16,128},{20,172},{24,136},{28,16... | collective-permute-start | bytes 1572872 | tf_op jit(solution)/shard_map/ppermute | solution.py:76
  32.5 15.0 %collective-permute-start.2 = (bf16[512,512]{1,0:T(8,128)(2,1)S(1)}, bf16[512,512]{1,0:T(8,128)(2,1)}, u32[]{:S(2)}, u32[]{:S(2)}) collective-permute-start(bf16[512,512]{1,0:T(8,128)(2,1)S(1)} %bitcast.64), channel_id=1, source_target_pairs={{0,128},{4,140},{8,136},{12,132},{16,144},{20,156},{24,152},{28,14... | collective-permute-start | bytes 1572872 | tf_op jit(solution)/shard_map/ppermute | solution.py:76
  34.5 12.9 %collective-permute-start.1 = (bf16[512,512]{1,0:T(8,128)(2,1)S(1)}, bf16[512,512]{1,0:T(8,128)(2,1)}, u32[]{:S(2)}, u32[]{:S(2)}) collective-permute-start(bf16[512,512]{1,0:T(8,128)(2,1)S(1)} %bitcast.65), channel_id=1, source_target_pairs={{0,16},{4,116},{8,24},{12,124},{16,0},{20,36},{24,8},{28,44},{32,4... | collective-permute-start | bytes 1572872 | tf_op jit(solution)/shard_map/ppermute | solution.py:76
  47.4 8.4 %collective-permute-start.4 = (bf16[512,512]{1,0:T(8,128)(2,1)}, bf16[512,512]{1,0:T(8,128)(2,1)S(1)}, u32[]{:S(2)}, u32[]{:S(2)}) collective-permute-start(bf16[512,512]{1,0:T(8,128)(2,1)} %collective-permute-done.1.refs_1_), channel_id=1, source_target_pairs={{0,4},{4,0},{8,12},{12,8},{16,20},{20,16},{24,28},{28,24},{32,36},... | collective-permute-start | bytes 1572872 | tf_op jit(solution)/shard_map/ppermute | solution.py:72
  47.4 15.5 %collective-permute-start.5 = (bf16[512,512]{1,0:T(8,128)(2,1)}, bf16[512,512]{1,0:T(8,128)(2,1)S(1)}, u32[]{:S(2)}, u32[]{:S(2)}) collective-permute-start(bf16[512,512]{1,0:T(8,128)(2,1)} %collective-permute-done.2.refs_1_), channel_id=1, source_target_pairs={{0,4},{4,0},{8,12},{12,8},{16,20},{20,16},{24,28},{28,24},{32,36},... | collective-permute-start | bytes 1572872 | tf_op jit(solution)/shard_map/ppermute | solution.py:72
  47.9 15.1 %collective-permute-start.6 = (bf16[512,512]{1,0:T(8,128)(2,1)}, bf16[512,512]{1,0:T(8,128)(2,1)S(1)}, u32[]{:S(2)}, u32[]{:S(2)}) collective-permute-start(bf16[512,512]{1,0:T(8,128)(2,1)} %collective-permute-done.3.refs_3_), channel_id=1, source_target_pairs={{0,4},{4,0},{8,12},{12,8},{16,20},{20,16},{24,28},{28,24},{32,36},... | collective-permute-start | bytes 1572872 | tf_op jit(solution)/shard_map/ppermute | solution.py:72
  52.2 30.4 %collective-permute-start.11 = (bf16[2,256,512]{2,1,0:T(8,128)(2,1)S(1)}, bf16[2,256,512]{2,1,0:T(8,128)(2,1)S(1)}, u32[]{:S(2)}, u32[]{:S(2)}) collective-permute-start(bf16[2,256,512]{2,1,0:T(8,128)(2,1)S(1)} %pad_maximum_fusion.3), channel_id=1, source_target_pairs={{0,2},{1,3},{2,0},{3,1},{4,6},{5,7},{6,4},{7,5},{8,10},{9,11},{10,... | collective-permute-start | bytes 1572872 | tf_op jit(solution)/shard_map/ppermute | solution.py:68
  55.3 27.3 %collective-permute-start.10 = (bf16[2,256,512]{2,1,0:T(8,128)(2,1)S(1)}, bf16[2,256,512]{2,1,0:T(8,128)(2,1)S(1)}, u32[]{:S(2)}, u32[]{:S(2)}) collective-permute-start(bf16[2,256,512]{2,1,0:T(8,128)(2,1)S(1)} %pad_maximum_fusion.2), channel_id=1, source_target_pairs={{0,3},{1,0},{2,1},{3,2},{4,5},{5,6},{6,7},{7,4},{8,11},{9,8},{10,9... | collective-permute-start | bytes 1572872 | tf_op jit(solution)/shard_map/ppermute | solution.py:68
  55.9 26.7 %collective-permute-start.9 = (bf16[2,256,512]{2,1,0:T(8,128)(2,1)S(1)}, bf16[2,256,512]{2,1,0:T(8,128)(2,1)S(1)}, u32[]{:S(2)}, u32[]{:S(2)}) collective-permute-start(bf16[2,256,512]{2,1,0:T(8,128)(2,1)S(1)} %pad_maximum_fusion.1), channel_id=1, source_target_pairs={{0,1},{1,2},{2,3},{3,0},{4,7},{5,4},{6,5},{7,6},{8,9},{9,10},{10,1... | collective-permute-start | bytes 1572872 | tf_op jit(solution)/shard_map/ppermute | solution.py:68
  59.1 20.4 %slice-start = ((s8[8388608]{0:T(1024)(128)(4,1)}), s8[4194304]{0:T(1024)(128)(4,1)S(1)}, s32[]{:S(2)}) async-start(s8[8388608]{0:T(1024)(128)(4,1)} %bitcast.59), calls=%async_computation.2 | async-start | bytes 8388608
  63.0 16.5 %slice-start.1 = ((s8[8388608]{0:T(1024)(128)(4,1)}), s8[4194304]{0:T(1024)(128)(4,1)S(1)}, s32[]{:S(2)}) async-start(s8[8388608]{0:T(1024)(128)(4,1)} %bitcast.59), calls=%async_computation.3 | async-start | bytes 8388608
  80.9 4.8 %collective-permute-start.7 = (bf16[2,512,512]{2,1,0:T(8,128)(2,1)S(1)}, bf16[2,512,512]{2,1,0:T(8,128)(2,1)S(1)}, u32[]{:S(2)}, u32[]{:S(2)}) collective-permute-start(bf16[2,512,512]{2,1,0:T(8,128)(2,1)S(1)} %memory_pieces.4), channel_id=1, source_target_pairs={{0,4},{4,0},{8,12},{12,8},{16,20},{20,16},{24,28},{28,24},{32,36},... | collective-permute-start | bytes 3145736 | tf_op jit(solution)/shard_map/ppermute | solution.py:72
  82.6 10.3 %copy-start.3 = (bf16[2,256,512]{2,1,0:T(8,128)(2,1)}, bf16[2,256,512]{2,1,0:T(8,128)(2,1)S(1)}, u32[]{:S(2)}) copy-start(bf16[2,256,512]{2,1,0:T(8,128)(2,1)S(1)} %collective-permute-done.9.behind) | copy-start | bytes 1572868
  82.6 5.3 %collective-permute-start.12 = (bf16[2,512,512]{2,1,0:T(8,128)(2,1)S(1)}, bf16[2,512,512]{2,1,0:T(8,128)(2,1)S(1)}, u32[]{:S(2)}, u32[]{:S(2)}) collective-permute-start(bf16[2,512,512]{2,1,0:T(8,128)(2,1)S(1)} %memory_pieces.6), channel_id=1, source_target_pairs={{0,4},{4,0},{8,12},{12,8},{16,20},{20,16},{24,28},{28,24},{32,36},... | collective-permute-start | bytes 3145736 | tf_op jit(solution)/shard_map/ppermute | solution.py:72
  83.1 23.6 %collective-permute-start.17 = (bf16[2,512,512]{2,1,0:T(8,128)(2,1)S(1)}, bf16[2,512,512]{2,1,0:T(8,128)(2,1)S(1)}, u32[]{:S(2)}, u32[]{:S(2)}) collective-permute-start(bf16[2,512,512]{2,1,0:T(8,128)(2,1)S(1)} %get-tuple-element.41.g0), channel_id=1, source_target_pairs={{0,3},{1,0},{2,1},{3,2},{4,5},{5,6},{6,7},{7,4},{8,11},{9,8},{10,9... | collective-permute-start | bytes 3145736 | tf_op jit(solution)/shard_map/ppermute | solution.py:68
  83.2 25.5 %collective-permute-start.16 = (bf16[2,512,512]{2,1,0:T(8,128)(2,1)S(1)}, bf16[2,512,512]{2,1,0:T(8,128)(2,1)}, u32[]{:S(2)}, u32[]{:S(2)}) collective-permute-start(bf16[2,512,512]{2,1,0:T(8,128)(2,1)S(1)} %get-tuple-element.41.g0), channel_id=1, source_target_pairs={{0,1},{1,2},{2,3},{3,0},{4,7},{5,4},{6,5},{7,6},{8,9},{9,10},{10,1... | collective-permute-start | bytes 3145736 | tf_op jit(solution)/shard_map/ppermute | solution.py:68
  87.3 8.5 %collective-permute-start.8 = (bf16[512,512]{1,0:T(8,128)(2,1)S(1)}, bf16[512,512]{1,0:T(8,128)(2,1)S(1)}, u32[]{:S(2)}, u32[]{:S(2)}) collective-permute-start(bf16[512,512]{1,0:T(8,128)(2,1)S(1)} %get-tuple-element.34), channel_id=1, source_target_pairs={{0,16},{4,116},{8,24},{12,124},{16,0},{20,36},{24,8},{28,44},{32,4... | collective-permute-start | bytes 1572872 | tf_op jit(solution)/shard_map/ppermute | solution.py:76
  89.5 15.3 %collective-permute-start.13 = (bf16[512,512]{1,0:T(8,128)(2,1)S(1)}, bf16[512,512]{1,0:T(8,128)(2,1)S(1)}, u32[]{:S(2)}, u32[]{:S(2)}) collective-permute-start(bf16[512,512]{1,0:T(8,128)(2,1)S(1)} %get-tuple-element.36), channel_id=1, source_target_pairs={{0,128},{4,140},{8,136},{12,132},{16,144},{20,156},{24,152},{28,14... | collective-permute-start | bytes 1572872 | tf_op jit(solution)/shard_map/ppermute | solution.py:76
  90.3 14.5 %collective-permute-start.14 = (bf16[512,512]{1,0:T(8,128)(2,1)S(1)}, bf16[512,512]{1,0:T(8,128)(2,1)S(1)}, u32[]{:S(2)}, u32[]{:S(2)}) collective-permute-start(bf16[512,512]{1,0:T(8,128)(2,1)S(1)} %get-tuple-element.37), channel_id=1, source_target_pairs={{0,144},{4,252},{8,152},{12,244},{16,128},{20,172},{24,136},{28,16... | collective-permute-start | bytes 1572872 | tf_op jit(solution)/shard_map/ppermute | solution.py:76
  95.8 22.8 %collective-permute-start.15 = (bf16[3,2,256,512]{3,2,1,0:T(8,128)(2,1)}, bf16[3,2,256,512]{3,2,1,0:T(8,128)(2,1)S(1)}, u32[]{:S(2)}, u32[]{:S(2)}) collective-permute-start(bf16[3,2,256,512]{3,2,1,0:T(8,128)(2,1)} %pad_maximum_fusion), channel_id=1, source_target_pairs={{0,4},{4,0},{8,12},{12,8},{16,20},{20,16},{24,28},{28,24},{32,36},... | collective-permute-start | bytes 4718600 | tf_op jit(solution)/shard_map/ppermute | solution.py:72
  108.7 17.4 %collective-permute-start.18 = (bf16[2,512,512]{2,1,0:T(8,128)(2,1)}, bf16[2,512,512]{2,1,0:T(8,128)(2,1)}, u32[]{:S(2)}, u32[]{:S(2)}) collective-permute-start(bf16[2,512,512]{2,1,0:T(8,128)(2,1)} %collective-permute-done.16.g1), channel_id=1, source_target_pairs={{0,1},{1,2},{2,3},{3,0},{4,7},{5,4},{6,5},{7,6},{8,9},{9,10},{10,1... | collective-permute-start | bytes 3145736 | tf_op jit(solution)/shard_map/ppermute | solution.py:68
  112.0 23.1 %all-to-all-start.1 = ((bf16[8,64,512]{2,1,0:T(8,128)(2,1)}), bf16[8,64,512]{2,1,0:T(8,128)(2,1)}, u32[]{:S(2)}, u32[]{:S(2)}) async-start(bf16[8,64,512]{2,1,0:T(8,128)(2,1)} %bitcast.74), calls=%async_computation.1 | async-start | bytes 1048576 | tf_op jit(solution)/shard_map/all_to_all | solution.py:60
  (16 other events, 52.7 us)

commit v5 on v3

--- a/solution.py
+++ b/solution.py
@@ -290,7 +290,7 @@
         ),
         out_shape=jax.ShapeDtypeStruct((2, 2, 2, 2, 64, 2, 512), BF16),
         compiler_params=pltpu.CompilerParams(vmem_limit_bytes=VMEM),
-        cost_estimate=COST,
+        cost_estimate=pl.CostEstimate(flops=1 << 30, bytes_accessed=12 << 20, transcendentals=0),
         name="weight_rows",
     )(at, across, swapped, grads, sums)
     return out.reshape(1, 1024, 2, 512)

time: 134 us -> 135 us (level)
  no operation moved by 1% of the time
where the time goes in v5:
time: 135 us
  Pallas kernels  42.8 us (32%)
  starting transfers between devices  40.2 us (30%)
  waiting for transfers between devices  26.3 us (19%)
  local copies, waits for them, and re-layouts  16.6 us (12%)
  other arithmetic  6.94 us (5%)
  between operations  1.74 us (1%)
    ppermute x6, waiting for transfers between devices, near(): return lax.ppermute(block, PLANE, NEAR[dx, dz])  14.2 us
    unnamed x38, local copies, waits for them, and re-layouts  12.7 us
    ppermute x6, starting transfers between devices, along_dp(): return lax.ppermute(block, ('tp', 'dp'), pairs)  11.8 us
    pallas_call x1, Pallas kernels, attend(): pl.pallas_call(attend_kernel, grid_spec=pltpu.PrefetchScalarGridSpec(num_...  10.7 us
    pallas_call x3, Pallas kernels, project(): pl.pallas_call(functools.partial(project_kernel, first, count), grid=(4,)...  10.5 us
    all_to_all x1, starting transfers between devices, spread(): return lax.all_to_all(copies, PLANE, 0, 0, axis_index_groups=groups)  9.75 us
    ppermute x6, starting transfers between devices, near(): return lax.ppermute(block, PLANE, NEAR[dx, dz])  7.89 us
    all_to_all x1, waiting for transfers between devices, spread(): return lax.all_to_all(copies, PLANE, 0, 0, axis_index_groups=groups)  6.98 us
  transfers between devices with their start and end apart: 21, of which 7 were waited for; matrix products, arithmetic and copies ran while one was open for 6% of the time, Pallas kernels for 32%

profile of v5, /device:TPU:33, one launch (start us, length us, event | category | flops | bytes accessed | tf_op | source)
XLA Modules:
  0.0 134.6 jit_solution(11933859453474654230)
XLA Ops:
  2.3 9.7 %all-to-all-start = ((bf16[8,64,512]{2,1,0:T(8,128)(2,1)}), bf16[8,64,512]{2,1,0:T(8,128)(2,1)S(1)}, u32[]{:S(2)}, u32[]{:S(2)}) async-start(bf16[8,64,512]{2,1,0:T(8,128)(2,1)} %broadcast_in_dim.12), calls=%async_computation | async-start | bytes 1048576 | tf_op jit(solution)/shard_map/all_to_all | solution.py:56
  12.1 3.4 %copy-done.2 = bf16[1,4096,2,512]{3,2,1,0:T(2,128)(2,1)S(1)} copy-done((bf16[1,4096,2,512]{3,2,1,0:T(2,128)(2,1)S(1)}, bf16[1,4096,2,512]{3,2,1,0:T(2,128)(2,1)}, u32[]{:S(2)}) %copy-start.2) | copy-done | bytes 8388632
  15.5 3.9 %split_weights.1.refs_2_.refs_3_.refs_5_.weight_ref = bf16[4,2,2,512,512]{4,3,2,1,0:T(8,128)(2,1)S(1)} custom-call(s32[3]{0:T(128)S(1)} %pad_add_fusion.at_ref, bf16[2,4,2,2,2,64,2,512]{7,6,5,4,3,2,1,0:T(2,128)(2,1)S(1)} %bitcast.61), custom_call_target="tpu_custom_call" | custom-call | bytes 65536 | tf_op jit(solution)/shard_map/split_weights/pallas_call | solution.py:96
  19.5 3.3 %copy-done = bf16[4,2,2,512,512]{4,3,2,1,0:T(8,128)(2,1)} copy-done((bf16[4,2,2,512,512]{4,3,2,1,0:T(8,128)(2,1)}, bf16[4,2,2,512,512]{4,3,2,1,0:T(8,128)(2,1)S(1)}, u32[]{:S(2)}) %copy-start) | copy-done | bytes 8388632
  22.7 7.0 %all-to-all-done = bf16[8,64,512]{2,1,0:T(8,128)(2,1)S(1)} async-done(((bf16[8,64,512]{2,1,0:T(8,128)(2,1)}), bf16[8,64,512]{2,1,0:T(8,128)(2,1)S(1)}, u32[]{:S(2)}, u32[]{:S(2)}) %all-to-all-start) | async-done | bytes 524320 | tf_op jit(solution)/shard_map/all_to_all | solution.py:56
  29.7 2.7 %collective-permute-start = (bf16[512,512]{1,0:T(8,128)(2,1)S(1)}, bf16[512,512]{1,0:T(8,128)(2,1)S(1)}, u32[]{:S(2)}, u32[]{:S(2)}) collective-permute-start(bf16[512,512]{1,0:T(8,128)(2,1)S(1)} %bitcast.62), channel_id=1, source_target_pairs={{0,4},{4,0},{8,12},{12,8},{16,20},{20,16},{24,28},{28,24},{32,36},... | collective-permute-start | bytes 1572872 | tf_op jit(solution)/shard_map/ppermute | solution.py:72
  32.5 2.0 %collective-permute-start.2 = (bf16[512,512]{1,0:T(8,128)(2,1)S(1)}, bf16[512,512]{1,0:T(8,128)(2,1)S(1)}, u32[]{:S(2)}, u32[]{:S(2)}) collective-permute-start(bf16[512,512]{1,0:T(8,128)(2,1)S(1)} %bitcast.64), channel_id=1, source_target_pairs={{0,128},{4,140},{8,136},{12,132},{16,144},{20,156},{24,152},{28,14... | collective-permute-start | bytes 1572872 | tf_op jit(solution)/shard_map/ppermute | solution.py:76
  36.3 3.4 %copy-done.1 = bf16[4,2,2,512,512]{4,3,2,1,0:T(8,128)(2,1)S(1)} copy-done((bf16[4,2,2,512,512]{4,3,2,1,0:T(8,128)(2,1)S(1)}, bf16[4,2,2,512,512]{4,3,2,1,0:T(8,128)(2,1)}, u32[]{:S(2)}) %copy-start.1) | copy-done | bytes 8388632
  39.7 2.5 %project.3.refs_0_ = f32[2,512,512]{2,1,0:T(8,128)S(1)} custom-call(bf16[512,512]{1,0:T(8,128)(2,1)S(1)} %bitcast.66, bf16[512,512]{1,0:T(8,128)(2,1)S(1)} %collective-permute-done.refs_1_, bf16[4,2,2,512,512]{4,3,2,1,0:T(8,128)(2,1)S(1)} %copy-done.1), custom_call_target="tpu_custom_call" | custom-call | bytes 65536 | tf_op jit(solution)/shard_map/project/pallas_call | solution.py:136
  42.7 4.6 %collective-permute-done.2.refs_1_ = bf16[512,512]{1,0:T(8,128)(2,1)S(1)} collective-permute-done((bf16[512,512]{1,0:T(8,128)(2,1)S(1)}, bf16[512,512]{1,0:T(8,128)(2,1)S(1)}, u32[]{:S(2)}, u32[]{:S(2)}) %collective-permute-start.2) | collective-permute-done | bytes 524320 | tf_op jit(solution)/shard_map/ppermute | solution.py:76
  47.9 2.3 %broadcast_select_fusion.2 = (bf16[512,512]{1,0:T(8,128)(2,1)}, bf16[512,512]{1,0:T(8,128)(2,1)S(1)}, bf16[512,512]{1,0:T(8,128)(2,1)S(1)}, bf16[512,512]{1,0:T(...) fusion(bf16[512,512]{1,0:T(8,128)(2,1)} %collective-permute-don, ...), kind=kLoop, calls=%fused_computation.9 | loop fusion | flops 2097152 | bytes 6291460 | tf_op jit(solution)/shard_map/jit(_where)/select_n | solution.py:320
  50.5 2.8 %collective-permute-start.7 = (bf16[2,256,512]{2,1,0:T(8,128)(2,1)S(1)}, bf16[2,256,512]{2,1,0:T(8,128)(2,1)S(1)}, u32[]{:S(2)}, u32[]{:S(2)}) collective-permute-start(bf16[2,256,512]{2,1,0:T(8,128)(2,1)S(1)} %pad_maximum_fusion.1), channel_id=1, source_target_pairs={{0,1},{1,2},{2,3},{3,0},{4,7},{5,4},{6,5},{7,6},{8,9},{9,10},{10,1... | collective-permute-start | bytes 1572872 | tf_op jit(solution)/shard_map/ppermute | solution.py:68
  53.6 1.9 %collective-permute-start.11 = (bf16[2,256,512]{2,1,0:T(8,128)(2,1)S(1)}, bf16[2,256,512]{2,1,0:T(8,128)(2,1)S(1)}, u32[]{:S(2)}, u32[]{:S(2)}) collective-permute-start(bf16[2,256,512]{2,1,0:T(8,128)(2,1)S(1)} %pad_maximum_fusion.3), channel_id=1, source_target_pairs={{0,2},{1,3},{2,0},{3,1},{4,6},{5,7},{6,4},{7,5},{8,10},{9,11},{10,... | collective-permute-start | bytes 1572872 | tf_op jit(solution)/shard_map/ppermute | solution.py:68
  56.1 3.8 %project.4.refs_0_ = f32[2,512,512]{2,1,0:T(8,128)S(1)} custom-call(f32[2,512,512]{2,1,0:T(8,128)S(1)} %project.3.refs_0_, bf16[512,512]{1,0:T(8,128)(2,1)} %collective-permute-done.1.refs_1_, bf16[512,512]{1,0:T(8,128)(2,1)S(1)} %collective-permute-done.4.refs_2_, bf16[4,2,2,512,512]{4,3,2,1,0:T(8,128)(2,1)S(1)} %copy-done.1), custom_call_target="tpu_custom_call" | custom-call | bytes 65536 | tf_op jit(solution)/shard_map/project/pallas_call | solution.py:136
  60.0 4.2 %project.5.pair_ref = bf16[2,512,512]{2,1,0:T(8,128)(2,1)S(1)} custom-call(f32[2,512,512]{2,1,0:T(8,128)S(1)} %project.4.refs_0_, bf16[512,512]{1,0:T(8,128)(2,1)S(1)} %collective-permute-done.2.refs_1_, bf16[512,512]{1,0:T(8,128)(2,1)S(1)} %collective-permute-done.5.refs_2_, bf16[512,512]{1,0:T(8,128)(2,1)S(1)} %collective-permute-done.3.refs_3_, ...), custom_call_target="tpu_custom_call" | custom-call | bytes 65536 | tf_op jit(solution)/shard_map/project/pallas_call | solution.py:136
  64.3 10.7 %attend.1 = (bf16[512,512]{1,0:T(8,128)(2,1)}, bf16[2,512,512]{2,1,0:T(8,128)(2,1)S(1)}, bf16[2,512,512]{2,1,0:T(8,128)(2,1)S(1)}) custom-call(s32[1]{0:T(128)S(6)} %copy.28.length_ref, bf16[512,512]{1,0:T(8,128)(2,1)S(1)} %bitcast.71, bf16[512,512]{1,0:T(8,128)(2,1)S(1)} %bitcast.72, bf16[2,512,512]{2,1,0:T(8,128)(2,1)S(1)} %project.5.pair_ref), custom_call_target="tpu_custom_call" | custom-call | bytes 65536 | tf_op jit(solution)/shard_map/attend/pallas_call | solution.py:182
  80.2 3.1 %collective-permute-start.16 = (bf16[2,512,512]{2,1,0:T(8,128)(2,1)S(1)}, bf16[2,512,512]{2,1,0:T(8,128)(2,1)}, u32[]{:S(2)}, u32[]{:S(2)}) collective-permute-start(bf16[2,512,512]{2,1,0:T(8,128)(2,1)S(1)} %get-tuple-element.45.g0), channel_id=1, source_target_pairs={{0,1},{1,2},{2,3},{3,0},{4,7},{5,4},{6,5},{7,6},{8,9},{9,10},{10,1... | collective-permute-start | bytes 3145736 | tf_op jit(solution)/shard_map/ppermute | solution.py:68
  87.8 2.6 %collective-permute-start.14 = (bf16[512,512]{1,0:T(8,128)(2,1)S(1)}, bf16[512,512]{1,0:T(8,128)(2,1)S(1)}, u32[]{:S(2)}, u32[]{:S(2)}) collective-permute-start(bf16[512,512]{1,0:T(8,128)(2,1)S(1)} %get-tuple-element.41), channel_id=1, source_target_pairs={{0,144},{4,252},{8,152},{12,244},{16,128},{20,172},{24,136},{28,16... | collective-permute-start | bytes 1572872 | tf_op jit(solution)/shard_map/ppermute | solution.py:76
  94.8 7.5 %collective-permute-done.13 = bf16[512,512]{1,0:T(8,128)(2,1)S(1)} collective-permute-done((bf16[512,512]{1,0:T(8,128)(2,1)S(1)}, bf16[512,512]{1,0:T(8,128)(2,1)S(1)}, u32[]{:S(2)}, u32[]{:S(2)}) %collective-permute-start.13) | collective-permute-done | bytes 524320 | tf_op jit(solution)/shard_map/ppermute | solution.py:76
  105.6 3.4 %collective-permute-start.18 = (bf16[2,512,512]{2,1,0:T(8,128)(2,1)}, bf16[2,512,512]{2,1,0:T(8,128)(2,1)}, u32[]{:S(2)}, u32[]{:S(2)}) collective-permute-start(bf16[2,512,512]{2,1,0:T(8,128)(2,1)} %collective-permute-done.16.g1), channel_id=1, source_target_pairs={{0,1},{1,2},{2,3},{3,0},{4,7},{5,4},{6,5},{7,6},{8,9},{9,10},{10,1... | collective-permute-start | bytes 3145736 | tf_op jit(solution)/shard_map/ppermute | solution.py:68
  109.9 4.2 %all-to-all-start.1 = ((bf16[8,64,512]{2,1,0:T(8,128)(2,1)}), bf16[8,64,512]{2,1,0:T(8,128)(2,1)}, u32[]{:S(2)}, u32[]{:S(2)}) async-start(bf16[8,64,512]{2,1,0:T(8,128)(2,1)} %bitcast.74), calls=%async_computation.1 | async-start | bytes 1048576 | tf_op jit(solution)/shard_map/all_to_all | solution.py:60
  117.2 5.9 %weight_sums.1.sums = f32[4,2,256,512]{3,2,1,0:T(8,128)S(1)} custom-call(s32[3]{0:T(128)S(1)} %pad_add_fusion.at_ref, bf16[2,256,512]{2,1,0:T(8,128)(2,1)S(1)} %pad_maximum_fusion.4.mine, bf16[2,256,512]{2,1,0:T(8,128)(2,1)S(1)} %pad_maximum_fusion.5.other, bf16[2,256,512]{2,1,0:T(8,128)(2,1)S(1)} %collective-permute-done.7.behind, ...), custom_call_target="tpu_custom_call" | custom-call | bytes 65536 | tf_op jit(solution)/shard_map/weight_sums/pallas_call | solution.py:262
  123.2 5.8 %weight_rows.1 = bf16[2,2,2,2,64,2,512]{6,5,4,3,2,1,0:T(2,128)(2,1)} custom-call(s32[3]{0:T(128)S(1)} %pad_add_fusion.at_ref, bf16[2,256,512]{2,1,0:T(8,128)(2,1)S(1)} %copy-done.4, bf16[3,2,256,512]{3,2,1,0:T(8,128)(2,1)S(1)} %collective-permute-done.15.swapped, bf16[2,512,512]{2,1,0:T(8,128)(2,1)} %collective-permute-done.18.grads, ...), custom_call_target="tpu_custom_call" | custom-call | flops 1073741824 | bytes 12582912 | tf_op jit(solution)/shard_map/weight_rows/pallas_call | solution.py:280
  129.0 3.8 %all-to-all-done.1 = bf16[8,64,512]{2,1,0:T(8,128)(2,1)} async-done(((bf16[8,64,512]{2,1,0:T(8,128)(2,1)}), bf16[8,64,512]{2,1,0:T(8,128)(2,1)}, u32[]{:S(2)}, u32[]{:S(2)}) %all-to-all-start.1) | async-done | bytes 524320 | tf_op jit(solution)/shard_map/all_to_all | solution.py:60
  (90 shorter events, 28.1 us)
Async XLA Ops:
  2.3 27.4 %all-to-all-start = ((bf16[8,64,512]{2,1,0:T(8,128)(2,1)}), bf16[8,64,512]{2,1,0:T(8,128)(2,1)S(1)}, u32[]{:S(2)}, u32[]{:S(2)}) async-start(bf16[8,64,512]{2,1,0:T(8,128)(2,1)} %broadcast_in_dim.12), calls=%async_computation | async-start | bytes 1048576 | tf_op jit(solution)/shard_map/all_to_all | solution.py:56
  29.7 6.6 %collective-permute-start = (bf16[512,512]{1,0:T(8,128)(2,1)S(1)}, bf16[512,512]{1,0:T(8,128)(2,1)S(1)}, u32[]{:S(2)}, u32[]{:S(2)}) collective-permute-start(bf16[512,512]{1,0:T(8,128)(2,1)S(1)} %bitcast.62), channel_id=1, source_target_pairs={{0,4},{4,0},{8,12},{12,8},{16,20},{20,16},{24,28},{28,24},{32,36},... | collective-permute-start | bytes 1572872 | tf_op jit(solution)/shard_map/ppermute | solution.py:72
  32.5 10.2 %collective-permute-start.3 = (bf16[512,512]{1,0:T(8,128)(2,1)S(1)}, bf16[512,512]{1,0:T(8,128)(2,1)S(1)}, u32[]{:S(2)}, u32[]{:S(2)}) collective-permute-start(bf16[512,512]{1,0:T(8,128)(2,1)S(1)} %bitcast.63), channel_id=1, source_target_pairs={{0,144},{4,252},{8,152},{12,244},{16,128},{20,172},{24,136},{28,16... | collective-permute-start | bytes 1572872 | tf_op jit(solution)/shard_map/ppermute | solution.py:76
  32.5 14.9 %collective-permute-start.2 = (bf16[512,512]{1,0:T(8,128)(2,1)S(1)}, bf16[512,512]{1,0:T(8,128)(2,1)S(1)}, u32[]{:S(2)}, u32[]{:S(2)}) collective-permute-start(bf16[512,512]{1,0:T(8,128)(2,1)S(1)} %bitcast.64), channel_id=1, source_target_pairs={{0,128},{4,140},{8,136},{12,132},{16,144},{20,156},{24,152},{28,14... | collective-permute-start | bytes 1572872 | tf_op jit(solution)/shard_map/ppermute | solution.py:76
  34.5 12.8 %collective-permute-start.1 = (bf16[512,512]{1,0:T(8,128)(2,1)S(1)}, bf16[512,512]{1,0:T(8,128)(2,1)}, u32[]{:S(2)}, u32[]{:S(2)}) collective-permute-start(bf16[512,512]{1,0:T(8,128)(2,1)S(1)} %bitcast.65), channel_id=1, source_target_pairs={{0,16},{4,116},{8,24},{12,124},{16,0},{20,36},{24,8},{28,44},{32,4... | collective-permute-start | bytes 1572872 | tf_op jit(solution)/shard_map/ppermute | solution.py:76
  47.3 6.2 %collective-permute-start.4 = (bf16[512,512]{1,0:T(8,128)(2,1)}, bf16[512,512]{1,0:T(8,128)(2,1)S(1)}, u32[]{:S(2)}, u32[]{:S(2)}) collective-permute-start(bf16[512,512]{1,0:T(8,128)(2,1)} %collective-permute-done.1.refs_1_), channel_id=1, source_target_pairs={{0,4},{4,0},{8,12},{12,8},{16,20},{20,16},{24,28},{28,24},{32,36},... | collective-permute-start | bytes 1572872 | tf_op jit(solution)/shard_map/ppermute | solution.py:72
  47.4 12.6 %collective-permute-start.5 = (bf16[512,512]{1,0:T(8,128)(2,1)S(1)}, bf16[512,512]{1,0:T(8,128)(2,1)S(1)}, u32[]{:S(2)}, u32[]{:S(2)}) collective-permute-start(bf16[512,512]{1,0:T(8,128)(2,1)S(1)} %collective-permute-done.2.refs_1_), channel_id=1, source_target_pairs={{0,4},{4,0},{8,12},{12,8},{16,20},{20,16},{24,28},{28,24},{32,36},... | collective-permute-start | bytes 1572872 | tf_op jit(solution)/shard_map/ppermute | solution.py:72
  47.8 12.2 %collective-permute-start.6 = (bf16[512,512]{1,0:T(8,128)(2,1)S(1)}, bf16[512,512]{1,0:T(8,128)(2,1)S(1)}, u32[]{:S(2)}, u32[]{:S(2)}) collective-permute-start(bf16[512,512]{1,0:T(8,128)(2,1)S(1)} %collective-permute-done.3.refs_3_), channel_id=1, source_target_pairs={{0,4},{4,0},{8,12},{12,8},{16,20},{20,16},{24,28},{28,24},{32,36},... | collective-permute-start | bytes 1572872 | tf_op jit(solution)/shard_map/ppermute | solution.py:72
  50.5 24.5 %collective-permute-start.7 = (bf16[2,256,512]{2,1,0:T(8,128)(2,1)S(1)}, bf16[2,256,512]{2,1,0:T(8,128)(2,1)S(1)}, u32[]{:S(2)}, u32[]{:S(2)}) collective-permute-start(bf16[2,256,512]{2,1,0:T(8,128)(2,1)S(1)} %pad_maximum_fusion.1), channel_id=1, source_target_pairs={{0,1},{1,2},{2,3},{3,0},{4,7},{5,4},{6,5},{7,6},{8,9},{9,10},{10,1... | collective-permute-start | bytes 1572872 | tf_op jit(solution)/shard_map/ppermute | solution.py:68
  53.3 21.6 %collective-permute-start.8 = (bf16[2,256,512]{2,1,0:T(8,128)(2,1)S(1)}, bf16[2,256,512]{2,1,0:T(8,128)(2,1)S(1)}, u32[]{:S(2)}, u32[]{:S(2)}) collective-permute-start(bf16[2,256,512]{2,1,0:T(8,128)(2,1)S(1)} %pad_maximum_fusion.2), channel_id=1, source_target_pairs={{0,3},{1,0},{2,1},{3,2},{4,5},{5,6},{6,7},{7,4},{8,11},{9,8},{10,9... | collective-permute-start | bytes 1572872 | tf_op jit(solution)/shard_map/ppermute | solution.py:68
  53.6 26.0 %collective-permute-start.11 = (bf16[2,256,512]{2,1,0:T(8,128)(2,1)S(1)}, bf16[2,256,512]{2,1,0:T(8,128)(2,1)S(1)}, u32[]{:S(2)}, u32[]{:S(2)}) collective-permute-start(bf16[2,256,512]{2,1,0:T(8,128)(2,1)S(1)} %pad_maximum_fusion.3), channel_id=1, source_target_pairs={{0,2},{1,3},{2,0},{3,1},{4,6},{5,7},{6,4},{7,5},{8,10},{9,11},{10,... | collective-permute-start | bytes 1572872 | tf_op jit(solution)/shard_map/ppermute | solution.py:68
  56.1 18.8 %slice-start = ((s8[8388608]{0:T(1024)(128)(4,1)}), s8[4194304]{0:T(1024)(128)(4,1)S(1)}, s32[]{:S(2)}) async-start(s8[8388608]{0:T(1024)(128)(4,1)} %bitcast.59), calls=%async_computation.2 | async-start | bytes 8388608
  60.0 15.0 %slice-start.1 = ((s8[8388608]{0:T(1024)(128)(4,1)}), s8[4194304]{0:T(1024)(128)(4,1)S(1)}, s32[]{:S(2)}) async-start(s8[8388608]{0:T(1024)(128)(4,1)} %bitcast.59), calls=%async_computation.3 | async-start | bytes 8388608
  76.4 6.9 %collective-permute-start.9 = (bf16[2,512,512]{2,1,0:T(8,128)(2,1)S(1)}, bf16[2,512,512]{2,1,0:T(8,128)(2,1)S(1)}, u32[]{:S(2)}, u32[]{:S(2)}) collective-permute-start(bf16[2,512,512]{2,1,0:T(8,128)(2,1)S(1)} %memory_pieces.4), channel_id=1, source_target_pairs={{0,4},{4,0},{8,12},{12,8},{16,20},{20,16},{24,28},{28,24},{32,36},... | collective-permute-start | bytes 3145736 | tf_op jit(solution)/shard_map/ppermute | solution.py:72
  79.6 10.8 %copy-start.3 = (bf16[2,256,512]{2,1,0:T(8,128)(2,1)}, bf16[2,256,512]{2,1,0:T(8,128)(2,1)S(1)}, u32[]{:S(2)}) copy-start(bf16[2,256,512]{2,1,0:T(8,128)(2,1)S(1)} %collective-permute-done.11.across) | copy-start | bytes 1572868
  79.6 5.7 %collective-permute-start.12 = (bf16[2,512,512]{2,1,0:T(8,128)(2,1)S(1)}, bf16[2,512,512]{2,1,0:T(8,128)(2,1)S(1)}, u32[]{:S(2)}, u32[]{:S(2)}) collective-permute-start(bf16[2,512,512]{2,1,0:T(8,128)(2,1)S(1)} %memory_pieces.6), channel_id=1, source_target_pairs={{0,4},{4,0},{8,12},{12,8},{16,20},{20,16},{24,28},{28,24},{32,36},... | collective-permute-start | bytes 3145736 | tf_op jit(solution)/shard_map/ppermute | solution.py:72
  79.7 23.6 %collective-permute-start.17 = (bf16[2,512,512]{2,1,0:T(8,128)(2,1)S(1)}, bf16[2,512,512]{2,1,0:T(8,128)(2,1)S(1)}, u32[]{:S(2)}, u32[]{:S(2)}) collective-permute-start(bf16[2,512,512]{2,1,0:T(8,128)(2,1)S(1)} %get-tuple-element.45.g0), channel_id=1, source_target_pairs={{0,3},{1,0},{2,1},{3,2},{4,5},{5,6},{6,7},{7,4},{8,11},{9,8},{10,9... | collective-permute-start | bytes 3145736 | tf_op jit(solution)/shard_map/ppermute | solution.py:68
  80.2 25.4 %collective-permute-start.16 = (bf16[2,512,512]{2,1,0:T(8,128)(2,1)S(1)}, bf16[2,512,512]{2,1,0:T(8,128)(2,1)}, u32[]{:S(2)}, u32[]{:S(2)}) collective-permute-start(bf16[2,512,512]{2,1,0:T(8,128)(2,1)S(1)} %get-tuple-element.45.g0), channel_id=1, source_target_pairs={{0,1},{1,2},{2,3},{3,0},{4,7},{5,4},{6,5},{7,6},{8,9},{9,10},{10,1... | collective-permute-start | bytes 3145736 | tf_op jit(solution)/shard_map/ppermute | solution.py:68
  84.9 8.5 %collective-permute-start.10 = (bf16[512,512]{1,0:T(8,128)(2,1)S(1)}, bf16[512,512]{1,0:T(8,128)(2,1)S(1)}, u32[]{:S(2)}, u32[]{:S(2)}) collective-permute-start(bf16[512,512]{1,0:T(8,128)(2,1)S(1)} %get-tuple-element.38), channel_id=1, source_target_pairs={{0,16},{4,116},{8,24},{12,124},{16,0},{20,36},{24,8},{28,44},{32,4... | collective-permute-start | bytes 1572872 | tf_op jit(solution)/shard_map/ppermute | solution.py:76
  86.9 15.3 %collective-permute-start.13 = (bf16[512,512]{1,0:T(8,128)(2,1)S(1)}, bf16[512,512]{1,0:T(8,128)(2,1)S(1)}, u32[]{:S(2)}, u32[]{:S(2)}) collective-permute-start(bf16[512,512]{1,0:T(8,128)(2,1)S(1)} %get-tuple-element.40), channel_id=1, source_target_pairs={{0,128},{4,140},{8,136},{12,132},{16,144},{20,156},{24,152},{28,14... | collective-permute-start | bytes 1572872 | tf_op jit(solution)/shard_map/ppermute | solution.py:76
  87.8 14.4 %collective-permute-start.14 = (bf16[512,512]{1,0:T(8,128)(2,1)S(1)}, bf16[512,512]{1,0:T(8,128)(2,1)S(1)}, u32[]{:S(2)}, u32[]{:S(2)}) collective-permute-start(bf16[512,512]{1,0:T(8,128)(2,1)S(1)} %get-tuple-element.41), channel_id=1, source_target_pairs={{0,144},{4,252},{8,152},{12,244},{16,128},{20,172},{24,136},{28,16... | collective-permute-start | bytes 1572872 | tf_op jit(solution)/shard_map/ppermute | solution.py:76
  93.4 22.5 %collective-permute-start.15 = (bf16[3,2,256,512]{3,2,1,0:T(8,128)(2,1)}, bf16[3,2,256,512]{3,2,1,0:T(8,128)(2,1)S(1)}, u32[]{:S(2)}, u32[]{:S(2)}) collective-permute-start(bf16[3,2,256,512]{3,2,1,0:T(8,128)(2,1)} %pad_maximum_fusion), channel_id=1, source_target_pairs={{0,4},{4,0},{8,12},{12,8},{16,20},{20,16},{24,28},{28,24},{32,36},... | collective-permute-start | bytes 4718600 | tf_op jit(solution)/shard_map/ppermute | solution.py:72
  105.6 17.6 %collective-permute-start.18 = (bf16[2,512,512]{2,1,0:T(8,128)(2,1)}, bf16[2,512,512]{2,1,0:T(8,128)(2,1)}, u32[]{:S(2)}, u32[]{:S(2)}) collective-permute-start(bf16[2,512,512]{2,1,0:T(8,128)(2,1)} %collective-permute-done.16.g1), channel_id=1, source_target_pairs={{0,1},{1,2},{2,3},{3,0},{4,7},{5,4},{6,5},{7,6},{8,9},{9,10},{10,1... | collective-permute-start | bytes 3145736 | tf_op jit(solution)/shard_map/ppermute | solution.py:68
  109.9 22.9 %all-to-all-start.1 = ((bf16[8,64,512]{2,1,0:T(8,128)(2,1)}), bf16[8,64,512]{2,1,0:T(8,128)(2,1)}, u32[]{:S(2)}, u32[]{:S(2)}) async-start(bf16[8,64,512]{2,1,0:T(8,128)(2,1)} %bitcast.74), calls=%async_computation.1 | async-start | bytes 1048576 | tf_op jit(solution)/shard_map/all_to_all | solution.py:60
  (16 other events, 53.7 us)
